TPU v7x, 32 devices: a whole 2x2x4 slice. The times are simulated.
32 devices in a mesh: seq: 32 (over z, y, x, core).
Axes of the slice: x: 2, y: 2, z: 4, core: 2. Of those that a mesh axis runs over, the one named last changes fastest.
Arguments:
- queries: bfloat16 [8192, 8, 128], P('seq'), may hold values from -6 to 6
- key_rows: bfloat16 [8192, 4, 128], P('seq'), may hold values from -6 to 6
- value_rows: bfloat16 [8192, 4, 128], P('seq'), may hold values from -6 to 6
- attn_output: bfloat16 [8192, 8, 128], P('seq'), may hold values from -6 to 6
- grad_output: bfloat16 [8192, 8, 128], P('seq'), may hold values from -144 to 144
- log_norm: float32 [8, 8192], P(None, 'seq'), may hold values from 6.5 to 8
Outputs:
- grad_queries: bfloat16 [8192, 8, 128], P('seq')
- grad_keys: bfloat16 [8192, 4, 128], P('seq')
- grad_values: bfloat16 [8192, 4, 128], P('seq')
All inputs are finite; a program needn't handle non-finite values.
Results may differ from a plain program's by a relative error of at most 0.0057.
Values may be sent and summed in bfloat16 or wider, within the bound.
No kernel may reach another device: no remote copies, remote signals or barrier semaphores. Data moves between devices by JAX's collectives and lax.ppermute only.
A program may use at most 64 MiB of HBM per device.

v0:
```python
import jax
import jax.numpy as jnp
from jax import lax
from jax.sharding import PartitionSpec as P

W = 1024


query_scale = 168.0 ** (-0.5)


def from_behind(block, axis, distance):
    devices = range(lax.axis_size(axis))
    route = [(i - distance, i) for i in devices if i - distance in devices]
    return lax.ppermute(block, axis, route)


def band_mask(query_pos, key_pos, seq_rows):
    offset = query_pos[:, None] - key_pos[None, :]
    inside = (offset >= 0) & (offset < W)
    return inside & (key_pos >= 0)[None, :] & (query_pos < seq_rows)[:, None]


def band_grads(queries, grad_output, log_norm, delta_rows, key_rows, value_rows, allowed):
    row_count, head_count, head_size = queries.shape
    group_count = key_rows.shape[1]
    share = head_count // group_count
    query_group = queries.reshape(row_count, group_count, share, head_size)
    grad_group = grad_output.reshape(row_count, group_count, share, head_size)
    scores = (
        jnp.einsum("qkgd,lkd->kgql", query_group, key_rows, preferred_element_type=jnp.float32)
        * query_scale
    )
    norm_part = log_norm.reshape(group_count, share, row_count)[..., None]
    delta_part = delta_rows.reshape(group_count, share, row_count)[..., None]
    probs = jnp.where(allowed[None, None], jnp.exp(scores - norm_part), 0.0)
    grad_v = jnp.einsum(
        "kgql,qkgd->lkd", probs.astype(jnp.bfloat16), grad_group, preferred_element_type=jnp.float32
    )
    dprobs = jnp.einsum(
        "qkgd,lkd->kgql", grad_group, value_rows, preferred_element_type=jnp.float32
    )
    dscores = (probs * (dprobs - delta_part)).astype(jnp.bfloat16)
    grad_q = (
        jnp.einsum("kgql,lkd->qkgd", dscores, key_rows, preferred_element_type=jnp.float32)
        * query_scale
    )
    grad_k = (
        jnp.einsum("kgql,qkgd->lkd", dscores, query_group, preferred_element_type=jnp.float32)
        * query_scale
    )
    return (grad_q.reshape(row_count, head_count, head_size), grad_k, grad_v)


def shards(queries, key_rows, value_rows, attn_output, grad_output, log_norm):
    local_rows = queries.shape[0]
    hop_count = W // local_rows
    row_block = min(local_rows, 256)
    device = lax.axis_index("seq")
    seq_rows = lax.axis_size("seq") * local_rows
    own_first = device * local_rows
    ext_first = own_first - W
    delta_rows = jnp.sum(
        grad_output.astype(jnp.float32) * attn_output.astype(jnp.float32), axis=-1
    ).T
    halo_parts = []
    for distance in range(1, hop_count + 1):
        halo_parts.append(from_behind((key_rows, value_rows), "seq", distance))
    ordered = halo_parts[::-1]
    ext_keys = jnp.concatenate([pair_part[0] for pair_part in ordered] + [key_rows], 0)
    ext_values = jnp.concatenate([pair_part[1] for pair_part in ordered] + [value_rows], 0)

    def sweep(bounds):
        ext_grad_k = jnp.zeros(ext_keys.shape, jnp.float32)
        ext_grad_v = jnp.zeros(ext_keys.shape, jnp.float32)
        key_low, key_high = bounds[0]
        allowed = band_mask(
            own_first + 0 + jnp.arange(row_block, dtype=jnp.int32),
            ext_first + key_low + jnp.arange(key_high - key_low, dtype=jnp.int32),
            seq_rows,
        )
        grad_q, grad_k, grad_v = band_grads(
            queries,
            grad_output,
            log_norm,
            delta_rows,
            ext_keys[key_low:key_high],
            ext_values[key_low:key_high],
            allowed,
        )
        ext_grad_k = ext_grad_k.at[key_low:key_high].add(grad_k)
        ext_grad_v = ext_grad_v.at[key_low:key_high].add(grad_v)
        return (grad_q, ext_grad_k, ext_grad_v)

    halo_bounds = [(0, W)]
    local_bounds = [(W, W + row_block)]
    grad_halo, halo_k, halo_v = sweep(halo_bounds)
    deliver_halo_k = halo_k[:W]
    deliver_halo_v = halo_v[:W]
    taken_k = jnp.zeros(key_rows.shape, jnp.float32)
    taken_v = jnp.zeros(key_rows.shape, jnp.float32)
    for distance in range(1, hop_count + 1):
        lower = (hop_count - distance) * local_rows
        got_k, got_v = from_behind(
            (
                deliver_halo_k[lower : lower + local_rows].astype(jnp.bfloat16),
                deliver_halo_v[lower : lower + local_rows].astype(jnp.bfloat16),
            ),
            "seq",
            -distance,
        )
        taken_k = taken_k + got_k.astype(jnp.float32)
        taken_v = taken_v + got_v.astype(jnp.float32)
    taken_k, taken_v = (taken_k, taken_v)
    grad_local, local_k, local_v = sweep(local_bounds)
    grad_total = grad_halo + grad_local
    own_k = local_k[W:] + taken_k
    own_v = local_v[W:] + taken_v
    return (grad_total.astype(jnp.bfloat16), own_k.astype(jnp.bfloat16), own_v.astype(jnp.bfloat16))


def solution(mesh):
    in_specs = (
        P("seq", None, None),
        P("seq", None, None),
        P("seq", None, None),
        P("seq", None, None),
        P("seq", None, None),
        P(None, "seq"),
    )
    out_specs = (P("seq", None, None), P("seq", None, None), P("seq", None, None))
    return jax.shard_map(shards, mesh=mesh, in_specs=in_specs, out_specs=out_specs, check_vma=False)
```

profile of v0, /device:TPU:6, one launch (start us, length us, event | category | flops | bytes accessed | tf_op | source)
XLA Modules:
  0.0 92.6 jit_solution(2855192435886442888)
XLA Ops:
  0.7 1.8 %copy.63 = bf16[256,4,128]{2,0,1:T(8,128)(2,1)} copy(bf16[256,4,128]{2,1,0:T(4,128)(2,1)} %param.15) | data formatting | bytes 524288 | tf_op args[1]
  2.4 3.4 %collective-permute-start = (bf16[256,4,128]{2,0,1:T(8,128)(2,1)}, bf16[256,4,128]{2,0,1:T(8,128)(2,1)}, u32[]{:S(2)}, u32[]{:S(2)}) collective-permute-start(bf16[256,4,128]{2,0,1:T(8,128)(2,1)} %copy.63), channel_id=1, source_target_pairs={{0,4},{1,5},{2,6},{3,7},{4,8},{5,9},{6,10},{7,11},{8,12},{9,13},{1... | collective-permute-start | bytes 786440 | tf_op jit(solution)/shard_map/ppermute | solution.py:15
  5.8 2.6 %collective-permute-start.1 = (bf16[256,4,128]{2,0,1:T(8,128)(2,1)}, bf16[256,4,128]{2,0,1:T(8,128)(2,1)}, u32[]{:S(2)}, u32[]{:S(2)}) collective-permute-start(bf16[256,4,128]{2,0,1:T(8,128)(2,1)} %copy.63), channel_id=1, source_target_pairs={{0,3},{1,4},{2,5},{3,6},{4,7},{5,8},{6,9},{7,10},{8,11},{9,12},{10... | collective-permute-start | bytes 786440 | tf_op jit(solution)/shard_map/ppermute | solution.py:15
  8.4 3.4 %collective-permute-start.2 = (bf16[256,4,128]{2,0,1:T(8,128)(2,1)}, bf16[256,4,128]{2,0,1:T(8,128)(2,1)}, u32[]{:S(2)}, u32[]{:S(2)}) collective-permute-start(bf16[256,4,128]{2,0,1:T(8,128)(2,1)} %copy.63), channel_id=1, source_target_pairs={{0,2},{1,3},{2,4},{3,5},{4,6},{5,7},{6,8},{7,9},{8,10},{9,11},{10,... | collective-permute-start | bytes 786440 | tf_op jit(solution)/shard_map/ppermute | solution.py:15
  11.8 2.6 %collective-permute-start.3 = (bf16[256,4,128]{2,0,1:T(8,128)(2,1)}, bf16[256,4,128]{2,0,1:T(8,128)(2,1)}, u32[]{:S(2)}, u32[]{:S(2)}) collective-permute-start(bf16[256,4,128]{2,0,1:T(8,128)(2,1)} %copy.63), channel_id=1, source_target_pairs={{0,1},{1,2},{2,3},{3,4},{4,5},{5,6},{6,7},{7,8},{8,9},{9,10},{10,1... | collective-permute-start | bytes 786440 | tf_op jit(solution)/shard_map/ppermute | solution.py:15
  14.4 1.7 %copy.68 = bf16[256,4,128]{2,0,1:T(8,128)(2,1)} copy(bf16[256,4,128]{2,1,0:T(4,128)(2,1)} %param.16) | data formatting | bytes 524288 | tf_op args[2]
  16.1 3.4 %collective-permute-start.4 = (bf16[256,4,128]{2,0,1:T(8,128)(2,1)}, bf16[256,4,128]{2,0,1:T(8,128)(2,1)}, u32[]{:S(2)}, u32[]{:S(2)}) collective-permute-start(bf16[256,4,128]{2,0,1:T(8,128)(2,1)} %copy.68), channel_id=1, source_target_pairs={{0,4},{1,5},{2,6},{3,7},{4,8},{5,9},{6,10},{7,11},{8,12},{9,13},{1... | collective-permute-start | bytes 786440 | tf_op jit(solution)/shard_map/ppermute | solution.py:15
  20.3 1.5 %multiply_reduce_fusion = f32[256,8]{1,0:T(8,128)S(1)} fusion(bf16[256,8,128]{2,1,0:T(8,128)(2,1)} %param.17, bf16[256,8,128]{2,1,0:T(8,128)(2,1)} %param.18), kind=kLoop, calls=%fused_computation.44 | loop fusion | flops 1046528 | bytes 1056768 | tf_op jit(solution)/shard_map/reduce_sum | solution.py:63
  23.6 1.4 %fusion.13 = bf16[4,2,256,256]{2,3,1,0:T(8,128)(2,1)S(1)} fusion(f32[4,2,256,256]{2,3,1,0:T(8,128)S(1)} %fusion.15, f32[4,2,256]{2,1,0:T(2,128)S(1)} %sub.80, bf16[256,4,2,128]{3,2,1,0:T(2,128)(2,1)S(1)} %bitcast.106, bf16[256,4,128,1]{2,1,0,3:T(4,128)(2,1)} %bitcast.112), kind=kOutput, calls=%fused_computation.17 | convolution fusion | flops 135790592 | bytes 3940352 | tf_op jit(solution)/shard_map/qkgd,lkd->kgql/dot_general | solution.py:40
  25.4 3.6 %collective-permute-start.5 = (bf16[256,4,128]{2,0,1:T(8,128)(2,1)}, bf16[256,4,128]{2,0,1:T(8,128)(2,1)S(1)}, u32[]{:S(2)}, u32[]{:S(2)}) collective-permute-start(bf16[256,4,128]{2,0,1:T(8,128)(2,1)} %copy.68), channel_id=1, source_target_pairs={{0,3},{1,4},{2,5},{3,6},{4,7},{5,8},{6,9},{7,10},{8,11},{9,12},{10... | collective-permute-start | bytes 786440 | tf_op jit(solution)/shard_map/ppermute | solution.py:15
  29.1 3.4 %collective-permute-start.6 = (bf16[256,4,128]{2,0,1:T(8,128)(2,1)}, bf16[256,4,128]{2,0,1:T(8,128)(2,1)S(1)}, u32[]{:S(2)}, u32[]{:S(2)}) collective-permute-start(bf16[256,4,128]{2,0,1:T(8,128)(2,1)} %copy.68), channel_id=1, source_target_pairs={{0,2},{1,3},{2,4},{3,5},{4,6},{5,7},{6,8},{7,9},{8,10},{9,11},{10,... | collective-permute-start | bytes 786440 | tf_op jit(solution)/shard_map/ppermute | solution.py:15
  32.5 1.9 %collective-permute-start.7 = (bf16[256,4,128]{2,0,1:T(8,128)(2,1)}, bf16[256,4,128]{2,0,1:T(8,128)(2,1)S(1)}, u32[]{:S(2)}, u32[]{:S(2)}) collective-permute-start(bf16[256,4,128]{2,0,1:T(8,128)(2,1)} %copy.68), channel_id=1, source_target_pairs={{0,1},{1,2},{2,3},{3,4},{4,5},{5,6},{6,7},{7,8},{8,9},{9,10},{10,1... | collective-permute-start | bytes 786440 | tf_op jit(solution)/shard_map/ppermute | solution.py:15
  34.4 2.4 %fusion.38 = f32[4,1024,256,2]{2,1,3,0:T(8,128)S(1)} fusion(bf16[256,4,128]{2,0,1:T(8,128)(2,1)} %collective-permute-done.3, bf16[256,4,128]{2,0,1:T(8,128)(2,1)} %collective-permute-done.2, bf16[256,4,128]{2,0,1:T(8,128)(2,1)} %collective-permute-done.1, bf16[256,4,128]{2,0,1:T(8,128)(2,1)} %collective-permute-done, bf16[256,4,2,128]{3,2,1,0:T(2,128)(2,1)S(1)} %bitcast.102), kind=kOutput, calls=%fused_computation.50 | convolution fusion | flops 541065216 | bytes 9961472 | tf_op jit(solution)/shard_map/qkgd,lkd->kgql/dot_general | solution.py:31
  36.9 1.6 %fusion.19 = bf16[1024,4,128]{2,0,1:T(8,128)(2,1)S(1)} fusion(f32[4,1024,256,2]{2,1,3,0:T(8,128)S(1)} %fusion.38, f32[4,2,256]{2,1,0:T(2,128)S(1)} %sub.77, pred[256,1024]{0,1:T(8,128)(4,1)S(1)} %fusion.37, bf16[256,4,2,128]{3,2,1,0:T(2,128)(2,1)S(1)} %bitcast.107), kind=kOutput, calls=%fused_computation.24 | convolution fusion | flops 545783808 | bytes 10231808 | tf_op jit(solution)/shard_map/kgql,qkgd->lkd/dot_general | solution.py:37
  39.4 3.6 %collective-permute-start.12 = (bf16[256,4,128]{2,0,1:T(8,128)(2,1)}, bf16[256,4,128]{2,0,1:T(8,128)(2,1)}, u32[]{:S(2)}, u32[]{:S(2)}) collective-permute-start(bf16[256,4,128]{2,0,1:T(8,128)(2,1)} %get-tuple-element.60), channel_id=1, source_target_pairs={{1,0},{2,1},{3,2},{4,3},{5,4},{6,5},{7,6},{8,7},{9,8},{10,9},{11,1... | collective-permute-start | bytes 786440 | tf_op jit(solution)/shard_map/ppermute | solution.py:15
  43.1 3.3 %collective-permute-start.13 = (bf16[256,4,128]{2,0,1:T(8,128)(2,1)}, bf16[256,4,128]{2,0,1:T(8,128)(2,1)}, u32[]{:S(2)}, u32[]{:S(2)}) collective-permute-start(bf16[256,4,128]{2,0,1:T(8,128)(2,1)} %get-tuple-element.63), channel_id=1, source_target_pairs={{2,0},{3,1},{4,2},{5,3},{6,4},{7,5},{8,6},{9,7},{10,8},{11,9},{12,... | collective-permute-start | bytes 786440 | tf_op jit(solution)/shard_map/ppermute | solution.py:15
  46.4 1.9 %collective-permute-start.14 = (bf16[256,4,128]{2,0,1:T(8,128)(2,1)}, bf16[256,4,128]{2,0,1:T(8,128)(2,1)}, u32[]{:S(2)}, u32[]{:S(2)}) collective-permute-start(bf16[256,4,128]{2,0,1:T(8,128)(2,1)} %get-tuple-element.62), channel_id=1, source_target_pairs={{3,0},{4,1},{5,2},{6,3},{7,4},{8,5},{9,6},{10,7},{11,8},{12,9},{13... | collective-permute-start | bytes 786440 | tf_op jit(solution)/shard_map/ppermute | solution.py:15
  48.4 1.9 %collective-permute-start.15 = (bf16[256,4,128]{2,0,1:T(8,128)(2,1)S(1)}, bf16[256,4,128]{2,0,1:T(8,128)(2,1)}, u32[]{:S(2)}, u32[]{:S(2)}) collective-permute-start(bf16[256,4,128]{2,0,1:T(8,128)(2,1)S(1)} %get-tuple-element.61), channel_id=1, source_target_pairs={{4,0},{5,1},{6,2},{7,3},{8,4},{9,5},{10,6},{11,7},{12,8},{13,9},{1... | collective-permute-start | bytes 786440 | tf_op jit(solution)/shard_map/ppermute | solution.py:15
  50.3 3.7 %fusion.1 = bf16[4,2,256,1024]{2,3,1,0:T(8,128)(2,1)S(1)} fusion(f32[4,1024,256,2]{2,1,3,0:T(8,128)S(1)} %fusion.38, f32[4,2,256]{2,1,0:T(2,128)S(1)} %sub.80, f32[4,2,256]{2,1,0:T(2,128)S(1)} %sub.77, pred[256,1024]{0,1:T(8,128)(4,1)S(1)} %fusion.37, bf16[256,4,128]{2,0,1:T(8,128)(2,1)S(1)} %collective-permute-done.7, ...), kind=kOutput, calls=%fused_computation.2 | convolution fusion | flops 553648128 | bytes 14434304 | tf_op jit(solution)/shard_map/qkgd,lkd->kgql/dot_general | solution.py:40
  54.0 1.3 %fusion.18 = bf16[1024,4,128]{2,0,1:T(8,128)(2,1)S(1)} fusion(bf16[4,2,256,1024]{2,3,1,0:T(8,128)(2,1)S(1)} %fusion.1, bf16[256,4,2,128]{3,2,1,0:T(2,128)(2,1)S(1)} %bitcast.103), kind=kOutput, calls=%fused_computation.23 | convolution fusion | flops 537919488 | bytes 5767168 | tf_op jit(solution)/shard_map/kgql,qkgd->lkd/dot_general | solution.py:49
  56.2 1.9 %collective-permute-start.10 = (bf16[256,4,128]{2,0,1:T(8,128)(2,1)}, bf16[256,4,128]{2,0,1:T(8,128)(2,1)}, u32[]{:S(2)}, u32[]{:S(2)}) collective-permute-start(bf16[256,4,128]{2,0,1:T(8,128)(2,1)} %get-tuple-element.66), channel_id=1, source_target_pairs={{3,0},{4,1},{5,2},{6,3},{7,4},{8,5},{9,6},{10,7},{11,8},{12,9},{13... | collective-permute-start | bytes 786440 | tf_op jit(solution)/shard_map/ppermute | solution.py:15
  58.2 2.8 %fusion.25 = bf16[256,4,2,128]{0,3,2,1:T(8,128)(2,1)} fusion(f32[256,4,2,128]{0,3,2,1:T(8,128)S(1)} %fusion.24, bf16[4,2,256,1024]{2,3,1,0:T(8,128)(2,1)S(1)} %fusion.1, bf16[256,4,128]{2,0,1:T(8,128)(2,1)} %collective-permute-done.3, bf16[256,4,128]{2,0,1:T(8,128)(2,1)} %collective-permute-done.2, bf16[256,4,128]{2,0,1:T(8,128)(2,1)} %collective-permute-done.1, ...), kind=kOutput, calls=%fused_computation.30 | convolution fusion | flops 541851648 | bytes 6815744 | tf_op jit(solution)/shard_map/kgql,lkd->qkgd/dot_general | solution.py:45
  61.0 2.1 %copy.87 = bf16[256,8,128]{2,1,0:T(8,128)(2,1)} copy(bf16[256,8,128]{0,2,1:T(8,128)(2,1)} %bitcast.114) | data formatting | bytes 1048576
  63.1 1.9 %collective-permute-start.11 = (bf16[256,4,128]{2,0,1:T(8,128)(2,1)}, bf16[256,4,128]{2,0,1:T(8,128)(2,1)S(1)}, u32[]{:S(2)}, u32[]{:S(2)}) collective-permute-start(bf16[256,4,128]{2,0,1:T(8,128)(2,1)} %get-tuple-element.65), channel_id=1, source_target_pairs={{4,0},{5,1},{6,2},{7,3},{8,4},{9,5},{10,6},{11,7},{12,8},{13,9},{1... | collective-permute-start | bytes 786440 | tf_op jit(solution)/shard_map/ppermute | solution.py:15
  65.0 2.2 %collective-permute-start.8 = (bf16[256,4,128]{2,0,1:T(8,128)(2,1)}, bf16[256,4,128]{2,0,1:T(8,128)(2,1)S(1)}, u32[]{:S(2)}, u32[]{:S(2)}) collective-permute-start(bf16[256,4,128]{2,0,1:T(8,128)(2,1)} %get-tuple-element.64), channel_id=1, source_target_pairs={{1,0},{2,1},{3,2},{4,3},{5,4},{6,5},{7,6},{8,7},{9,8},{10,9},{11,1... | collective-permute-start | bytes 786440 | tf_op jit(solution)/shard_map/ppermute | solution.py:15
  67.2 2.3 %collective-permute-start.9 = (bf16[256,4,128]{2,0,1:T(8,128)(2,1)}, bf16[256,4,128]{2,0,1:T(8,128)(2,1)S(1)}, u32[]{:S(2)}, u32[]{:S(2)}) collective-permute-start(bf16[256,4,128]{2,0,1:T(8,128)(2,1)} %get-tuple-element.67), channel_id=1, source_target_pairs={{2,0},{3,1},{4,2},{5,3},{6,4},{7,5},{8,6},{9,7},{10,8},{11,9},{12,... | collective-permute-start | bytes 786440 | tf_op jit(solution)/shard_map/ppermute | solution.py:15
  69.6 7.7 %collective-permute-done.15 = bf16[256,4,128]{2,0,1:T(8,128)(2,1)} collective-permute-done((bf16[256,4,128]{2,0,1:T(8,128)(2,1)S(1)}, bf16[256,4,128]{2,0,1:T(8,128)(2,1)}, u32[]{:S(2)}, u32[]{:S(2)}) %collective-permute-start.15) | collective-permute-done | bytes 262176 | tf_op jit(solution)/shard_map/ppermute | solution.py:15
  77.3 1.6 %add_convert_fusion = bf16[256,4,128]{2,0,1:T(8,128)(2,1)S(1)} fusion(bf16[256,4,128]{2,0,1:T(8,128)(2,1)} %collective-permute-done.15, bf16[256,4,128]{2,0,1:T(8,128)(2,1)} %collective-permute-done.14, bf16[256,4,128]{2,0,1:T(8,128)(2,1)} %collective-permute-done.13, bf16[256,4,128]{2,0,1:T(8,128)(2,1)} %collective-permute-done.12, ...), kind=kOutput, calls=%fused_computation.48 | convolution fusion | flops 135921664 | bytes 3932160 | tf_op jit(solution)/shard_map/kgql,qkgd->lkd/dot_general | solution.py:37
  79.8 2.0 %collective-permute-done.10 = bf16[256,4,128]{2,0,1:T(8,128)(2,1)} collective-permute-done((bf16[256,4,128]{2,0,1:T(8,128)(2,1)}, bf16[256,4,128]{2,0,1:T(8,128)(2,1)}, u32[]{:S(2)}, u32[]{:S(2)}) %collective-permute-start.10) | collective-permute-done | bytes 262176 | tf_op jit(solution)/shard_map/ppermute | solution.py:15
  81.8 2.8 %collective-permute-done.11 = bf16[256,4,128]{2,0,1:T(8,128)(2,1)S(1)} collective-permute-done((bf16[256,4,128]{2,0,1:T(8,128)(2,1)}, bf16[256,4,128]{2,0,1:T(8,128)(2,1)S(1)}, u32[]{:S(2)}, u32[]{:S(2)}) %collective-permute-start.11) | collective-permute-done | bytes 262176 | tf_op jit(solution)/shard_map/ppermute | solution.py:15
  84.6 5.6 %collective-permute-done.9 = bf16[256,4,128]{2,0,1:T(8,128)(2,1)S(1)} collective-permute-done((bf16[256,4,128]{2,0,1:T(8,128)(2,1)}, bf16[256,4,128]{2,0,1:T(8,128)(2,1)S(1)}, u32[]{:S(2)}, u32[]{:S(2)}) %collective-permute-start.9) | collective-permute-done | bytes 262176 | tf_op jit(solution)/shard_map/ppermute | solution.py:15
  90.3 1.4 %add_convert_fusion.1 = bf16[256,4,128]{2,0,1:T(8,128)(2,1)S(1)} fusion(bf16[256,4,128]{2,0,1:T(8,128)(2,1)S(1)} %collective-permute-done.11, bf16[256,4,128]{2,0,1:T(8,128)(2,1)} %collective-permute-done.10, bf16[256,4,128]{2,0,1:T(8,128)(2,1)S(1)} %collective-permute-done.9, bf16[256,4,128]{2,0,1:T(8,128)(2,1)S(1)} %collective-permute-done.8, ...), kind=kOutput, calls=%fused_computation.49 | convolution fusion | flops 135528448 | bytes 2883584 | tf_op jit(solution)/shard_map/kgql,qkgd->lkd/dot_general | solution.py:49
  (38 shorter events, 6.5 us)
Async XLA Ops:
  0.6 22.3 %copy-start = (bf16[256,8,128]{2,1,0:T(8,128)(2,1)S(1)}, bf16[256,8,128]{2,1,0:T(8,128)(2,1)}, u32[]{:S(2)}) copy-start(bf16[256,8,128]{2,1,0:T(8,128)(2,1)} %param.14) | copy-start | bytes 1572868
  0.6 22.3 %copy-start.4 = (bf16[256,4,128]{2,1,0:T(4,128)(2,1)S(1)}, bf16[256,4,128]{2,1,0:T(4,128)(2,1)}, u32[]{:S(2)}) copy-start(bf16[256,4,128]{2,1,0:T(4,128)(2,1)} %param.15) | copy-start | bytes 786436
  2.4 23.0 %collective-permute-start = (bf16[256,4,128]{2,0,1:T(8,128)(2,1)}, bf16[256,4,128]{2,0,1:T(8,128)(2,1)}, u32[]{:S(2)}, u32[]{:S(2)}) collective-permute-start(bf16[256,4,128]{2,0,1:T(8,128)(2,1)} %copy.63), channel_id=1, source_target_pairs={{0,4},{1,5},{2,6},{3,7},{4,8},{5,9},{6,10},{7,11},{8,12},{9,13},{1... | collective-permute-start | bytes 786440 | tf_op jit(solution)/shard_map/ppermute | solution.py:15
  5.8 23.2 %collective-permute-start.1 = (bf16[256,4,128]{2,0,1:T(8,128)(2,1)}, bf16[256,4,128]{2,0,1:T(8,128)(2,1)}, u32[]{:S(2)}, u32[]{:S(2)}) collective-permute-start(bf16[256,4,128]{2,0,1:T(8,128)(2,1)} %copy.63), channel_id=1, source_target_pairs={{0,3},{1,4},{2,5},{3,6},{4,7},{5,8},{6,9},{7,10},{8,11},{9,12},{10... | collective-permute-start | bytes 786440 | tf_op jit(solution)/shard_map/ppermute | solution.py:15
  8.4 24.0 %collective-permute-start.2 = (bf16[256,4,128]{2,0,1:T(8,128)(2,1)}, bf16[256,4,128]{2,0,1:T(8,128)(2,1)}, u32[]{:S(2)}, u32[]{:S(2)}) collective-permute-start(bf16[256,4,128]{2,0,1:T(8,128)(2,1)} %copy.63), channel_id=1, source_target_pairs={{0,2},{1,3},{2,4},{3,5},{4,6},{5,7},{6,8},{7,9},{8,10},{9,11},{10,... | collective-permute-start | bytes 786440 | tf_op jit(solution)/shard_map/ppermute | solution.py:15
  11.8 22.6 %collective-permute-start.3 = (bf16[256,4,128]{2,0,1:T(8,128)(2,1)}, bf16[256,4,128]{2,0,1:T(8,128)(2,1)}, u32[]{:S(2)}, u32[]{:S(2)}) collective-permute-start(bf16[256,4,128]{2,0,1:T(8,128)(2,1)} %copy.63), channel_id=1, source_target_pairs={{0,1},{1,2},{2,3},{3,4},{4,5},{5,6},{6,7},{7,8},{8,9},{9,10},{10,1... | collective-permute-start | bytes 786440 | tf_op jit(solution)/shard_map/ppermute | solution.py:15
  16.1 26.9 %collective-permute-start.4 = (bf16[256,4,128]{2,0,1:T(8,128)(2,1)}, bf16[256,4,128]{2,0,1:T(8,128)(2,1)}, u32[]{:S(2)}, u32[]{:S(2)}) collective-permute-start(bf16[256,4,128]{2,0,1:T(8,128)(2,1)} %copy.68), channel_id=1, source_target_pairs={{0,4},{1,5},{2,6},{3,7},{4,8},{5,9},{6,10},{7,11},{8,12},{9,13},{1... | collective-permute-start | bytes 786440 | tf_op jit(solution)/shard_map/ppermute | solution.py:15
  21.9 1.7 %copy-start.1 = (bf16[256,8,128]{2,1,0:T(8,128)(2,1)S(1)}, bf16[256,8,128]{2,1,0:T(8,128)(2,1)}, u32[]{:S(2)}) copy-start(bf16[256,8,128]{2,1,0:T(8,128)(2,1)} %param.18) | copy-start | bytes 1572868
  25.0 9.4 %copy-start.2 = (bf16[4,2,256,256]{2,3,1,0:T(8,128)(2,1)}, bf16[4,2,256,256]{2,3,1,0:T(8,128)(2,1)S(1)}, u32[]{:S(2)}) copy-start(bf16[4,2,256,256]{2,3,1,0:T(8,128)(2,1)S(1)} %fusion.13) | copy-start | bytes 3145732
  25.4 21.0 %collective-permute-start.5 = (bf16[256,4,128]{2,0,1:T(8,128)(2,1)}, bf16[256,4,128]{2,0,1:T(8,128)(2,1)S(1)}, u32[]{:S(2)}, u32[]{:S(2)}) collective-permute-start(bf16[256,4,128]{2,0,1:T(8,128)(2,1)} %copy.68), channel_id=1, source_target_pairs={{0,3},{1,4},{2,5},{3,6},{4,7},{5,8},{6,9},{7,10},{8,11},{9,12},{10... | collective-permute-start | bytes 786440 | tf_op jit(solution)/shard_map/ppermute | solution.py:15
  29.1 19.3 %collective-permute-start.6 = (bf16[256,4,128]{2,0,1:T(8,128)(2,1)}, bf16[256,4,128]{2,0,1:T(8,128)(2,1)S(1)}, u32[]{:S(2)}, u32[]{:S(2)}) collective-permute-start(bf16[256,4,128]{2,0,1:T(8,128)(2,1)} %copy.68), channel_id=1, source_target_pairs={{0,2},{1,3},{2,4},{3,5},{4,6},{5,7},{6,8},{7,9},{8,10},{9,11},{10,... | collective-permute-start | bytes 786440 | tf_op jit(solution)/shard_map/ppermute | solution.py:15
  32.5 17.8 %collective-permute-start.7 = (bf16[256,4,128]{2,0,1:T(8,128)(2,1)}, bf16[256,4,128]{2,0,1:T(8,128)(2,1)S(1)}, u32[]{:S(2)}, u32[]{:S(2)}) collective-permute-start(bf16[256,4,128]{2,0,1:T(8,128)(2,1)} %copy.68), channel_id=1, source_target_pairs={{0,1},{1,2},{2,3},{3,4},{4,5},{5,6},{6,7},{7,8},{8,9},{9,10},{10,1... | collective-permute-start | bytes 786440 | tf_op jit(solution)/shard_map/ppermute | solution.py:15
  39.4 23.7 %collective-permute-start.12 = (bf16[256,4,128]{2,0,1:T(8,128)(2,1)}, bf16[256,4,128]{2,0,1:T(8,128)(2,1)}, u32[]{:S(2)}, u32[]{:S(2)}) collective-permute-start(bf16[256,4,128]{2,0,1:T(8,128)(2,1)} %get-tuple-element.60), channel_id=1, source_target_pairs={{1,0},{2,1},{3,2},{4,3},{5,4},{6,5},{7,6},{8,7},{9,8},{10,9},{11,1... | collective-permute-start | bytes 786440 | tf_op jit(solution)/shard_map/ppermute | solution.py:15
  43.1 22.0 %collective-permute-start.13 = (bf16[256,4,128]{2,0,1:T(8,128)(2,1)}, bf16[256,4,128]{2,0,1:T(8,128)(2,1)}, u32[]{:S(2)}, u32[]{:S(2)}) collective-permute-start(bf16[256,4,128]{2,0,1:T(8,128)(2,1)} %get-tuple-element.63), channel_id=1, source_target_pairs={{2,0},{3,1},{4,2},{5,3},{6,4},{7,5},{8,6},{9,7},{10,8},{11,9},{12,... | collective-permute-start | bytes 786440 | tf_op jit(solution)/shard_map/ppermute | solution.py:15
  46.4 20.8 %collective-permute-start.14 = (bf16[256,4,128]{2,0,1:T(8,128)(2,1)}, bf16[256,4,128]{2,0,1:T(8,128)(2,1)}, u32[]{:S(2)}, u32[]{:S(2)}) collective-permute-start(bf16[256,4,128]{2,0,1:T(8,128)(2,1)} %get-tuple-element.62), channel_id=1, source_target_pairs={{3,0},{4,1},{5,2},{6,3},{7,4},{8,5},{9,6},{10,7},{11,8},{12,9},{13... | collective-permute-start | bytes 786440 | tf_op jit(solution)/shard_map/ppermute | solution.py:15
  48.4 28.9 %collective-permute-start.15 = (bf16[256,4,128]{2,0,1:T(8,128)(2,1)S(1)}, bf16[256,4,128]{2,0,1:T(8,128)(2,1)}, u32[]{:S(2)}, u32[]{:S(2)}) collective-permute-start(bf16[256,4,128]{2,0,1:T(8,128)(2,1)S(1)} %get-tuple-element.61), channel_id=1, source_target_pairs={{4,0},{5,1},{6,2},{7,3},{8,4},{9,5},{10,6},{11,7},{12,8},{13,9},{1... | collective-permute-start | bytes 786440 | tf_op jit(solution)/shard_map/ppermute | solution.py:15
  56.2 25.6 %collective-permute-start.10 = (bf16[256,4,128]{2,0,1:T(8,128)(2,1)}, bf16[256,4,128]{2,0,1:T(8,128)(2,1)}, u32[]{:S(2)}, u32[]{:S(2)}) collective-permute-start(bf16[256,4,128]{2,0,1:T(8,128)(2,1)} %get-tuple-element.66), channel_id=1, source_target_pairs={{3,0},{4,1},{5,2},{6,3},{7,4},{8,5},{9,6},{10,7},{11,8},{12,9},{13... | collective-permute-start | bytes 786440 | tf_op jit(solution)/shard_map/ppermute | solution.py:15
  63.1 21.5 %collective-permute-start.11 = (bf16[256,4,128]{2,0,1:T(8,128)(2,1)}, bf16[256,4,128]{2,0,1:T(8,128)(2,1)S(1)}, u32[]{:S(2)}, u32[]{:S(2)}) collective-permute-start(bf16[256,4,128]{2,0,1:T(8,128)(2,1)} %get-tuple-element.65), channel_id=1, source_target_pairs={{4,0},{5,1},{6,2},{7,3},{8,4},{9,5},{10,6},{11,7},{12,8},{13,9},{1... | collective-permute-start | bytes 786440 | tf_op jit(solution)/shard_map/ppermute | solution.py:15
  65.0 19.6 %collective-permute-start.8 = (bf16[256,4,128]{2,0,1:T(8,128)(2,1)}, bf16[256,4,128]{2,0,1:T(8,128)(2,1)S(1)}, u32[]{:S(2)}, u32[]{:S(2)}) collective-permute-start(bf16[256,4,128]{2,0,1:T(8,128)(2,1)} %get-tuple-element.64), channel_id=1, source_target_pairs={{1,0},{2,1},{3,2},{4,3},{5,4},{6,5},{7,6},{8,7},{9,8},{10,9},{11,1... | collective-permute-start | bytes 786440 | tf_op jit(solution)/shard_map/ppermute | solution.py:15
  67.2 23.0 %copy-start.3 = (bf16[4,2,256,256]{2,3,1,0:T(8,128)(2,1)S(1)}, bf16[4,2,256,256]{2,3,1,0:T(8,128)(2,1)}, u32[]{:S(2)}) copy-start(bf16[4,2,256,256]{2,3,1,0:T(8,128)(2,1)} %copy-done.2) | copy-start | bytes 3145732
  67.2 23.0 %collective-permute-start.9 = (bf16[256,4,128]{2,0,1:T(8,128)(2,1)}, bf16[256,4,128]{2,0,1:T(8,128)(2,1)S(1)}, u32[]{:S(2)}, u32[]{:S(2)}) collective-permute-start(bf16[256,4,128]{2,0,1:T(8,128)(2,1)} %get-tuple-element.67), channel_id=1, source_target_pairs={{2,0},{3,1},{4,2},{5,3},{6,4},{7,5},{8,6},{9,7},{10,8},{11,9},{12,... | collective-permute-start | bytes 786440 | tf_op jit(solution)/shard_map/ppermute | solution.py:15
where the time goes:
time: 93.4 us; the launch traced here: 92.6 us
  starting transfers between devices  43.5 us (47%)
  waiting for transfers between devices  18.2 us (19%)
  matrix products  17.2 us (18%)
  local copies, waits for them, and re-layouts  10.1 us (11%)
  other arithmetic  2.56 us (3%)
  between operations  1.03 us (1%)
    ppermute x16, starting transfers between devices, from_behind(): return lax.ppermute(block, axis, route)  43.5 us
    ppermute x16, waiting for transfers between devices, from_behind(): return lax.ppermute(block, axis, route)  18.2 us
    unnamed x15, local copies, waits for them, and re-layouts  7.42 us
    dot_general x2, matrix products, band_grads(): jnp.einsum('qkgd,lkd->kgql', grad_group, value_rows, preferred_element_ty...  5.12 us
    dot_general x2, matrix products, band_grads(): jnp.einsum('kgql,qkgd->lkd', probs.astype(jnp.bfloat16), grad_group, pref...  3.26 us
    dot_general x2, matrix products, band_grads(): jnp.einsum('kgql,lkd->qkgd', dscores, key_rows, preferred_element_type=jn...  3.16 us
    dot_general x2, matrix products, band_grads(): jnp.einsum('qkgd,lkd->kgql', query_group, key_rows, preferred_element_typ...  3.07 us
    dot_general x2, matrix products, band_grads(): jnp.einsum('kgql,qkgd->lkd', dscores, query_group, preferred_element_type...  2.63 us
  transfers between devices with their start and end apart: 16, of which 4 were waited for; matrix products, arithmetic and copies ran while one was open for 28% of the time, Pallas kernels for 0%

commit v1 on v0

v1 whole, which is shorter than its diff:
```python
import functools
import math

import jax
import jax.numpy as jnp
from jax import lax
from jax.experimental import pallas as pl
from jax.experimental.pallas import tpu as pltpu
from jax.sharding import PartitionSpec as P

W = 1024

query_scale = 168.0 ** (-0.5)
LOG2E = math.log2(math.e)
AXIS = "seq"
VMEM_LIMIT = 48 * 1024 * 1024

NT = (((1,), (1,)), ((), ()))
NN = (((1,), (0,)), ((), ()))
TN = (((0,), (0,)), ((), ()))


def dot(a, b, dims):
    return lax.dot_general(a, b, dims, preferred_element_type=jnp.float32)


def call(kernel, name, out_shape, scratch=(), flops=0, aliases=None):
    return pl.pallas_call(
        kernel,
        out_shape=out_shape,
        scratch_shapes=list(scratch),
        name=name,
        input_output_aliases=aliases or {},
        cost_estimate=pl.CostEstimate(flops=flops, bytes_accessed=2 << 20, transcendentals=0),
        compiler_params=pltpu.CompilerParams(vmem_limit_bytes=VMEM_LIMIT),
    )


def pack_kv_kernel(k_ref, v_ref, keep_ref, give_ref, wide):
    rows, heads, _ = k_ref.shape
    half = heads // 2
    core = lax.axis_index(AXIS) % 2
    wide[:, :heads, :] = k_ref[...].astype(jnp.float32)
    wide[:, heads:, :] = v_ref[...].astype(jnp.float32)
    flat = wide.reshape(rows * 2 * heads, wide.shape[2])
    for out, side in ((keep_ref, core), (give_ref, 1 - core)):
        for part in range(2):
            for j in range(half):
                head = part * heads + side * half + j
                out[part * half + j] = flat[pl.ds(head, rows, stride=2 * heads), :].astype(out.dtype)


def pack_q_kernel(q_ref, g_ref, o_ref, norm_ref, keep_ref, give_ref, keep_rows, give_rows, wide):
    rows, heads, size = q_ref.shape
    half = heads // 2
    core = lax.axis_index(AXIS) % 2
    ones = jnp.ones((8, size), jnp.float32)
    flat = wide.reshape(rows * heads, size)
    sides = ((keep_ref, keep_rows, core), (give_ref, give_rows, 1 - core))
    wide[...] = q_ref[...].astype(jnp.float32)
    for out, _, side in sides:
        for j in range(half):
            out[j] = flat[pl.ds(side * half + j, rows, stride=heads), :].astype(out.dtype)
    wide[...] = g_ref[...].astype(jnp.float32)
    for out, _, side in sides:
        for j in range(half):
            out[half + j] = flat[pl.ds(side * half + j, rows, stride=heads), :].astype(out.dtype)
    wide[...] = g_ref[...].astype(jnp.float32) * o_ref[...].astype(jnp.float32)
    for _, out, side in sides:
        for j in range(half):
            product = flat[pl.ds(side * half + j, rows, stride=heads), :]
            total = lax.dot_general(
                ones, product, NT, precision=lax.Precision.HIGHEST, preferred_element_type=jnp.float32
            )
            out[j : j + 1] = norm_ref[pl.ds(side * half + j, 1), :] * LOG2E
            out[half + j : half + j + 1] = total[:1]


def tile(kv_ref, qg_ref, row_ref, grad_ref, gq_ref, offset, first):
    groups = kv_ref.shape[0] // 2
    share = qg_ref.shape[0] // (2 * groups)
    heads = groups * share
    rows, size = kv_ref.shape[1], kv_ref.shape[2]
    for g in range(groups):
        k = kv_ref[g]
        v = kv_ref[groups + g]
        q = qg_ref[g * share : (g + 1) * share].reshape(share * rows, size)
        d = qg_ref[heads + g * share : heads + (g + 1) * share].reshape(share * rows, size)
        norm = jnp.concatenate([row_ref[g * share + j : g * share + j + 1] for j in range(share)], 1)
        delta = jnp.concatenate([row_ref[heads + g * share + j : heads + g * share + j + 1] for j in range(share)], 1)
        x = dot(k, q, NT) * (query_scale * LOG2E) - norm
        if offset is not None:
            key = lax.broadcasted_iota(jnp.int32, (rows, rows), 0)
            query = lax.broadcasted_iota(jnp.int32, (rows, rows), 1)
            gap = query - key + offset
            seen = (gap >= 0) & (gap < W)
            x = jnp.concatenate(
                [jnp.where(seen, x[:, j * rows : (j + 1) * rows], -jnp.inf) for j in range(share)], 1
            )
        p = jnp.exp2(x)
        ds = (p * (dot(v, d, NT) - delta)).astype(jnp.bfloat16)
        gv = dot(p.astype(jnp.bfloat16), d, NN)
        gk = dot(ds, q, NN)
        gq = dot(ds, k, TN)
        if first:
            grad_ref[g] = gk
            grad_ref[groups + g] = gv
        else:
            grad_ref[g] += gk
            grad_ref[groups + g] += gv
        gq_ref[g] += gq


def scale_keys(grad_ref):
    groups = grad_ref.shape[0] // 2
    grad_ref[:groups] = grad_ref[:groups] * query_scale


def edge_kernel(back, kv_s, kv_r, qg_s, qg_r, rows_s, rows_r, gq_s_in, gq_r_in, grad_s, grad_r, gq_s, gq_r):
    device = lax.axis_index(AXIS)
    core = device % 2
    valid = device // 2 >= back
    rows = kv_s.shape[1]
    if back:
        gq_s[...] = gq_s_in[...]
        gq_r[...] = gq_r_in[...]
    else:
        gq_s[...] = jnp.zeros_like(gq_s)
        gq_r[...] = jnp.zeros_like(gq_r)

    @pl.when(valid)
    def _():
        tile(kv_s, qg_s, rows_s, grad_s, gq_s, 2 * back * rows, True)
        tile(kv_r, qg_r, rows_r, grad_r, gq_r, 2 * back * rows, True)
        full_from_s = (core == 0) if back == 0 else (core == 1)

        @pl.when(full_from_s)
        def _():
            tile(kv_s, qg_r, rows_r, grad_s, gq_r, None, False)

        @pl.when(jnp.logical_not(full_from_s))
        def _():
            tile(kv_r, qg_s, rows_s, grad_r, gq_s, None, False)

        scale_keys(grad_s)
        scale_keys(grad_r)

    if back:

        @pl.when(jnp.logical_not(valid))
        def _():
            grad_s[...] = jnp.zeros_like(grad_s)
            grad_r[...] = jnp.zeros_like(grad_r)


def full_kernel(kv, qg_s, qg_r, rows_s, rows_r, gq_s_in, gq_r_in, out, gq_s, gq_r, grad):
    valid = lax.axis_index(AXIS) // 2 >= 1
    gq_s[...] = gq_s_in[...]
    gq_r[...] = gq_r_in[...]

    @pl.when(valid)
    def _():
        tile(kv, qg_s, rows_s, grad, gq_s, None, True)
        tile(kv, qg_r, rows_r, grad, gq_r, None, False)
        scale_keys(grad)
        out[...] = grad[...].astype(out.dtype)

    @pl.when(jnp.logical_not(valid))
    def _():
        out[...] = jnp.zeros_like(out)


def final_q_kernel(own_ref, got_ref, out_ref, wide):
    rows, heads, size = out_ref.shape
    half = heads // 2
    core = lax.axis_index(AXIS) % 2
    flat = wide.reshape(rows * heads, size)
    groups = own_ref.shape[0]
    share = half // groups
    for j in range(half):
        g, r = j // share, j % share
        flat[pl.ds(core * half + j, rows, stride=heads), :] = own_ref[g, r * rows : (r + 1) * rows] * query_scale
        flat[pl.ds((1 - core) * half + j, rows, stride=heads), :] = got_ref[g, r * rows : (r + 1) * rows].astype(
            jnp.float32
        )
    out_ref[...] = wide[...].astype(out_ref.dtype)


def final_kv_kernel(own_ref, got_ref, back_s, back_r, side_s, side_r, out_k, out_v, wide):
    rows, heads, size = out_k.shape
    half = heads // 2
    device = lax.axis_index(AXIS)
    core = device % 2
    even = jnp.where((device // 2) % 2 == 0, 1.0, 0.0).astype(jnp.float32)
    flat = wide.reshape(rows * 2 * heads, size)
    for side, base_ref, back_ref, near_ref in (
        (core, own_ref, back_s, side_s),
        (1 - core, got_ref, back_r, side_r),
    ):
        for part in range(2):
            for j in range(half):
                n = part * half + j
                total = (
                    base_ref[n].astype(jnp.float32)
                    + back_ref[n].astype(jnp.float32)
                    + near_ref[n].astype(jnp.float32) * even
                )
                flat[pl.ds(part * heads + side * half + j, rows, stride=2 * heads), :] = total
    out_k[...] = wide[:, :heads, :].astype(out_k.dtype)
    out_v[...] = wide[:, heads:, :].astype(out_v.dtype)


def shards(queries, key_rows, value_rows, attn_output, grad_output, log_norm):
    rows, heads, size = queries.shape
    groups = key_rows.shape[1]
    devices = lax.axis_size(AXIS)
    hops = W // rows
    assert hops == 4 and devices % 4 == 0
    low, f32 = jnp.bfloat16, jnp.float32
    device = lax.axis_index(AXIS)
    even = (device // 2) % 2 == 0

    def move(x, target):
        return lax.ppermute(x, AXIS, [(i, target(i)) for i in range(devices)])

    ahead = lambda i: (i + hops) % devices
    behind = lambda i: (i - hops) % devices
    sibling = lambda i: i ^ 1
    beside = lambda i: i ^ 2

    shape = jax.ShapeDtypeStruct
    kv_block = (groups, rows, size)
    qg_block = (heads, rows, size)
    row_block = (heads, rows)
    gq_block = (groups // 2, heads // groups * rows, size)
    tile_flops = 10 * rows * rows * size * heads // 2

    kv_s, kv_give = call(
        pack_kv_kernel,
        "pack_kv",
        [shape(kv_block, low)] * 2,
        [pltpu.VMEM((rows, 2 * groups, size), f32)],
    )(key_rows, value_rows)
    two_s = move(kv_s, ahead)
    kv_r = move(kv_give, sibling)
    two_r = move(kv_r, ahead)
    qg_s, qg_give, rows_s, rows_give = call(
        pack_q_kernel,
        "pack_q",
        [shape(qg_block, low)] * 2 + [shape(row_block, f32)] * 2,
        [pltpu.VMEM((rows, heads, size), f32)],
    )(queries, grad_output, attn_output, log_norm)
    qg_r = move(qg_give, sibling)
    rows_r = move(rows_give, sibling)
    one_s = move(jnp.where(even, kv_s, two_s), beside)
    one_r = move(jnp.where(even, kv_r, two_r), beside)

    def edge(back, block_s, block_r, gq_s, gq_r):
        return call(
            functools.partial(edge_kernel, back),
            "edge%d" % back,
            [shape(kv_block, f32)] * 2 + [shape(gq_block, f32)] * 2,
            flops=3 * tile_flops,
            aliases={6: 2, 7: 3},
        )(block_s, block_r, qg_s, qg_r, rows_s, rows_r, gq_s, gq_r)

    def full(block, gq_s, gq_r):
        return call(
            full_kernel,
            "full",
            [shape(kv_block, low)] + [shape(gq_block, f32)] * 2,
            [pltpu.VMEM(kv_block, f32)],
            flops=2 * tile_flops,
            aliases={5: 1, 6: 2},
        )(block, qg_s, qg_r, rows_s, rows_r, gq_s, gq_r)

    zero = jnp.zeros(gq_block, f32)
    own_s, own_r, gq_s, gq_r = edge(0, kv_s, kv_r, zero, zero)
    local_r = move(own_r.astype(low), sibling)
    far_s, far_r, gq_s, gq_r = edge(2, two_s, two_r, gq_s, gq_r)
    near_s, gq_s, gq_r = full(one_s, gq_s, gq_r)
    side_s = move(near_s, beside)
    near_r, gq_s, gq_r = full(one_r, gq_s, gq_r)
    side_r = move(near_r, lambda i: i ^ 3 if i & 2 else i ^ 2)

    def join(far, side):
        return (far + jnp.where(even, 0.0, side.astype(f32))).astype(low)

    back_s = move(join(far_s, side_s), behind)
    back_r = move(join(far_r, side_r), lambda i: sibling(behind(i)))
    gq_got = move((gq_r * query_scale).astype(low), sibling)
    grad_q = call(
        final_q_kernel,
        "final_q",
        shape(queries.shape, low),
        [pltpu.VMEM((rows, heads, size), f32)],
    )(gq_s, gq_got)
    grad_k, grad_v = call(
        final_kv_kernel,
        "final_kv",
        [shape(key_rows.shape, low), shape(value_rows.shape, low)],
        [pltpu.VMEM((rows, 2 * groups, size), f32)],
    )(own_s, local_r, back_s, back_r, side_s, side_r)
    return grad_q, grad_k, grad_v


def solution(mesh):
    in_specs = (
        P("seq", None, None),
        P("seq", None, None),
        P("seq", None, None),
        P("seq", None, None),
        P("seq", None, None),
        P(None, "seq"),
    )
    out_specs = (P("seq", None, None), P("seq", None, None), P("seq", None, None))
    return jax.shard_map(shards, mesh=mesh, in_specs=in_specs, out_specs=out_specs, check_vma=False)
```

time: 93.4 us -> 55.3 us (0.59)
  the two profiles are of different devices: /device:TPU:6 before, /device:TPU:0 now
where the time goes in v1:
time: 55.3 us; the launch traced here: 55 us
  starting transfers between devices  22.8 us (41%)
  waiting for transfers between devices  18.5 us (33%)
  Pallas kernels  7.93 us (14%)
  local copies, waits for them, and re-layouts  4.75 us (9%)
  between operations  0.75 us (1%)
    ppermute x13, starting transfers between devices, move(): return lax.ppermute(x, AXIS, [(i, target(i)) for i in range(devices)])  22.8 us
    ppermute x13, waiting for transfers between devices, move(): return lax.ppermute(x, AXIS, [(i, target(i)) for i in range(devices)])  18.5 us
    unnamed x12, local copies, waits for them, and re-layouts  4.68 us
    pallas_call x2, Pallas kernels, edge(): call(functools.partial(edge_kernel, back), 'edge%d' % back, [shape(kv_blo...  2.95 us
    pallas_call x1, Pallas kernels, shards(): call(pack_q_kernel, 'pack_q', [shape(qg_block, low)] * 2 + [shape(row_blo...  1.77 us
    pallas_call x1, Pallas kernels, shards(): call(final_kv_kernel, 'final_kv', [shape(key_rows.shape, low), shape(valu...  1.32 us
    pallas_call x1, Pallas kernels, shards(): call(final_q_kernel, 'final_q', shape(queries.shape, low), [pltpu.VMEM((r...  1.12 us
  transfers between devices with their start and end apart: 13, of which 5 were waited for; matrix products, arithmetic and copies ran while one was open for 1% of the time, Pallas kernels for 12%

profile of v1, /device:TPU:0, one launch (start us, length us, event | category | flops | bytes accessed | tf_op | source)
XLA Modules:
  0.0 55.0 jit_solution(2933718352425285564)
XLA Ops:
  0.6 0.9 %copy-done.3 = bf16[256,4,128]{2,1,0:T(4,128)(2,1)S(1)} copy-done((bf16[256,4,128]{2,1,0:T(4,128)(2,1)S(1)}, bf16[256,4,128]{2,1,0:T(4,128)(2,1)}, u32[]{:S(2)}) %copy-start.3) | copy-done | bytes 262168
  1.6 0.9 %copy-done.4 = bf16[256,4,128]{2,1,0:T(4,128)(2,1)S(1)} copy-done((bf16[256,4,128]{2,1,0:T(4,128)(2,1)S(1)}, bf16[256,4,128]{2,1,0:T(4,128)(2,1)}, u32[]{:S(2)}) %copy-start.4) | copy-done | bytes 262168
  2.5 0.3 pack_kv.1
  2.8 0.5 collective-permute-start
  3.3 2.6 %collective-permute-start.5 = (bf16[4,256,128]{2,1,0:T(8,128)(2,1)S(1)}, bf16[4,256,128]{2,1,0:T(8,128)(2,1)S(1)}, u32[]{:S(2)}, u32[]{:S(2)}) collective-permute-start(bf16[4,256,128]{2,1,0:T(8,128)(2,1)S(1)} %get-tuple-element.30.kv_s), channel_id=1, source_target_pairs={{0,4},{1,5},{2,6},{3,7},{4,8},{5,9},{6,10},{7,11},{8,12},{9,13},{1... | collective-permute-start | bytes 786440 | tf_op jit(solution)/shard_map/ppermute | solution.py:224
  5.9 1.0 %copy-done.1 = bf16[256,8,128]{2,1,0:T(8,128)(2,1)S(1)} copy-done((bf16[256,8,128]{2,1,0:T(8,128)(2,1)S(1)}, bf16[256,8,128]{2,1,0:T(8,128)(2,1)}, u32[]{:S(2)}) %copy-start.1) | copy-done | bytes 524312
  6.9 1.0 %copy-done.2 = bf16[256,8,128]{2,1,0:T(8,128)(2,1)S(1)} copy-done((bf16[256,8,128]{2,1,0:T(8,128)(2,1)S(1)}, bf16[256,8,128]{2,1,0:T(8,128)(2,1)}, u32[]{:S(2)}) %copy-start.2) | copy-done | bytes 524312
  8.0 0.7 %copy-done.5 = f32[8,256]{1,0:T(8,128)S(1)} copy-done((f32[8,256]{1,0:T(8,128)S(1)}, f32[8,256]{1,0:T(8,128)}, u32[]{:S(2)}) %copy-start.5) | copy-done | bytes 8216
  8.7 1.8 %pack_q.1 = (bf16[8,256,128]{2,1,0:T(8,128)(2,1)S(1)}, bf16[8,256,128]{2,1,0:T(8,128)(2,1)S(1)}, f32[8,256]{1,0:T(8,128)S(1)}, f32[8,256]{1,0:T(8,128)S(1)}) custom-call(bf16[256,8,128]{2,1,0:T(8,128)(2,1)S(1)} %copy-done, bf16[256,8,128]{2,1,0:T(8,128)(2,1)S(1)} %copy-done.1, bf16[256,8,128]{2,1,0:T(8,128)(2,1)S(1)} %copy-done.2, f32[8,256]{1,0:T(8,128)S(1)} %copy-done.5), custom_call_target="tpu_custom_call" | custom-call | bytes 2097152 | tf_op jit(solution)/shard_map/pack_q/pallas_call | solution.py:247
  10.5 0.2 collective-permute-start.3
  10.6 1.5 %collective-permute-start.1 = (bf16[4,256,128]{2,1,0:T(8,128)(2,1)S(1)}, bf16[4,256,128]{2,1,0:T(8,128)(2,1)S(1)}, u32[]{:S(2)}, u32[]{:S(2)}) collective-permute-start(bf16[4,256,128]{2,1,0:T(8,128)(2,1)S(1)} %collective-permute-done.kv_r), channel_id=1, source_target_pairs={{0,4},{1,5},{2,6},{3,7},{4,8},{5,9},{6,10},{7,11},{8,12},{9,13},{1... | collective-permute-start | bytes 786440 | tf_op jit(solution)/shard_map/ppermute | solution.py:224
  12.2 3.7 %collective-permute-done.5.kv_s = bf16[4,256,128]{2,1,0:T(8,128)(2,1)S(1)} collective-permute-done((bf16[4,256,128]{2,1,0:T(8,128)(2,1)S(1)}, bf16[4,256,128]{2,1,0:T(8,128)(2,1)S(1)}, u32[]{:S(2)}, u32[]{:S(2)}) %collective-permute-start.5) | collective-permute-done | bytes 262176 | tf_op jit(solution)/shard_map/ppermute | solution.py:224
  15.9 1.6 %collective-permute-start.6 = (bf16[4,256,128]{2,1,0:T(8,128)(2,1)S(1)}, bf16[4,256,128]{2,1,0:T(8,128)(2,1)S(1)}, u32[]{:S(2)}, u32[]{:S(2)}) collective-permute-start(bf16[4,256,128]{2,1,0:T(8,128)(2,1)S(1)} %broadcast_select_fusion), channel_id=1, source_target_pairs={{0,2},{1,3},{2,0},{3,1},{4,6},{5,7},{6,4},{7,5},{8,10},{9,11},{10,... | collective-permute-start | bytes 786440 | tf_op jit(solution)/shard_map/ppermute | solution.py:224
  17.4 4.5 %collective-permute-done.1.kv_r = bf16[4,256,128]{2,1,0:T(8,128)(2,1)S(1)} collective-permute-done((bf16[4,256,128]{2,1,0:T(8,128)(2,1)S(1)}, bf16[4,256,128]{2,1,0:T(8,128)(2,1)S(1)}, u32[]{:S(2)}, u32[]{:S(2)}) %collective-permute-start.1) | collective-permute-done | bytes 262176 | tf_op jit(solution)/shard_map/ppermute | solution.py:224
  21.9 1.6 %collective-permute-start.2 = (bf16[4,256,128]{2,1,0:T(8,128)(2,1)S(1)}, bf16[4,256,128]{2,1,0:T(8,128)(2,1)S(1)}, u32[]{:S(2)}, u32[]{:S(2)}) collective-permute-start(bf16[4,256,128]{2,1,0:T(8,128)(2,1)S(1)} %broadcast_select_fusion.1), channel_id=1, source_target_pairs={{0,2},{1,3},{2,0},{3,1},{4,6},{5,7},{6,4},{7,5},{8,10},{9,11},{10,... | collective-permute-start | bytes 786440 | tf_op jit(solution)/shard_map/ppermute | solution.py:224
  23.5 1.2 %collective-permute-done.4.rows_r = f32[8,256]{1,0:T(8,128)S(1)} collective-permute-done((f32[8,256]{1,0:T(8,128)S(1)}, f32[8,256]{1,0:T(8,128)S(1)}, u32[]{:S(2)}, u32[]{:S(2)}) %collective-permute-start.4) | collective-permute-done | bytes 8224 | tf_op jit(solution)/shard_map/ppermute | solution.py:224
  24.7 2.8 %edge0.1 = (f32[4,256,128]{2,1,0:T(8,128)S(1)}, f32[4,256,128]{2,1,0:T(8,128)S(1)}, f32[2,512,128]{2,1,0:T(8,128)S(1)}, f32[2,512,128]{2,1,0:T(8,128)S(1)}) custom-call(bf16[4,256,128]{2,1,0:T(8,128)(2,1)S(1)} %get-tuple-element.30.kv_s, bf16[4,256,128]{2,1,0:T(8,128)(2,1)S(1)} %collective-permute-done.kv_r, ...), custom_call_target="tpu_custom_call", output_to_operand_aliasing={{2}: (6, {}), {3}: (7, {})} | custom-call | flops 1006632960 | bytes 2097152 | tf_op jit(solution)/shard_map/edge0/pallas_call | solution.py:259
  27.5 0.2 collective-permute-start.8
  27.8 0.2 edge2.1
  28.0 0.2 full.2
  28.2 2.2 %collective-permute-start.9 = (bf16[4,256,128]{2,1,0:T(8,128)(2,1)S(1)}, bf16[4,256,128]{2,1,0:T(8,128)(2,1)S(1)}, u32[]{:S(2)}, u32[]{:S(2)}) collective-permute-start(bf16[4,256,128]{2,1,0:T(8,128)(2,1)S(1)} %get-tuple-element.42), channel_id=1, source_target_pairs={{0,2},{1,3},{2,0},{3,1},{4,6},{5,7},{6,4},{7,5},{8,10},{9,11},{10,... | collective-permute-start | bytes 786440 | tf_op jit(solution)/shard_map/ppermute | solution.py:224
  30.4 0.3 full.3
  30.8 2.5 %collective-permute-start.11 = (bf16[4,256,128]{2,1,0:T(8,128)(2,1)S(1)}, bf16[4,256,128]{2,1,0:T(8,128)(2,1)S(1)}, u32[]{:S(2)}, u32[]{:S(2)}) collective-permute-start(bf16[4,256,128]{2,1,0:T(8,128)(2,1)S(1)} %get-tuple-element.44), channel_id=1, source_target_pairs={{0,2},{1,3},{2,1},{3,0},{4,6},{5,7},{6,5},{7,4},{8,10},{9,11},{10,... | collective-permute-start | bytes 786440 | tf_op jit(solution)/shard_map/ppermute | solution.py:224
  33.3 0.1 collective-permute-start.7
  33.4 4.1 %collective-permute-done.9.side_s = bf16[4,256,128]{2,1,0:T(8,128)(2,1)S(1)} collective-permute-done((bf16[4,256,128]{2,1,0:T(8,128)(2,1)S(1)}, bf16[4,256,128]{2,1,0:T(8,128)(2,1)S(1)}, u32[]{:S(2)}, u32[]{:S(2)}) %collective-permute-start.9) | collective-permute-done | bytes 262176 | tf_op jit(solution)/shard_map/ppermute | solution.py:224
  37.6 0.1 add_convert_fusion.1
  37.6 5.4 %collective-permute-start.10 = (bf16[4,256,128]{2,1,0:T(8,128)(2,1)S(1)}, bf16[4,256,128]{2,1,0:T(8,128)(2,1)S(1)}, u32[]{:S(2)}, u32[]{:S(2)}) collective-permute-start(bf16[4,256,128]{2,1,0:T(8,128)(2,1)S(1)} %add_convert_fusion.1), channel_id=1, source_target_pairs={{0,28},{1,29},{2,30},{3,31},{4,0},{5,1},{6,2},{7,3},{8,4},{9,5},{1... | collective-permute-start | bytes 786440 | tf_op jit(solution)/shard_map/ppermute | solution.py:224
  43.1 0.1 add_convert_fusion
  43.1 4.4 %collective-permute-start.12 = (bf16[4,256,128]{2,1,0:T(8,128)(2,1)S(1)}, bf16[4,256,128]{2,1,0:T(8,128)(2,1)S(1)}, u32[]{:S(2)}, u32[]{:S(2)}) collective-permute-start(bf16[4,256,128]{2,1,0:T(8,128)(2,1)S(1)} %add_convert_fusion), channel_id=1, source_target_pairs={{0,29},{1,28},{2,31},{3,30},{4,1},{5,0},{6,3},{7,2},{8,5},{9,4},{1... | collective-permute-start | bytes 786440 | tf_op jit(solution)/shard_map/ppermute | solution.py:224
  47.5 1.1 %final_q.1 = bf16[256,8,128]{2,1,0:T(8,128)(2,1)} custom-call(f32[2,512,128]{2,1,0:T(8,128)S(1)} %get-tuple-element.37.own_ref, bf16[2,512,128]{2,1,0:T(8,128)(2,1)S(1)} %collective-permute-done.7.got_ref), custom_call_target="tpu_custom_call" | custom-call | bytes 2097152 | tf_op jit(solution)/shard_map/final_q/pallas_call | solution.py:292
  48.7 5.0 %collective-permute-done.12.back_r = bf16[4,256,128]{2,1,0:T(8,128)(2,1)S(1)} collective-permute-done((bf16[4,256,128]{2,1,0:T(8,128)(2,1)S(1)}, bf16[4,256,128]{2,1,0:T(8,128)(2,1)S(1)}, u32[]{:S(2)}, u32[]{:S(2)}) %collective-permute-start.12) | collective-permute-done | bytes 262176 | tf_op jit(solution)/shard_map/ppermute | solution.py:224
  53.7 1.3 %final_kv.1 = (bf16[256,4,128]{2,1,0:T(4,128)(2,1)}, bf16[256,4,128]{2,1,0:T(4,128)(2,1)}) custom-call(f32[4,256,128]{2,1,0:T(8,128)S(1)} %get-tuple-element.39.own_ref, bf16[4,256,128]{2,1,0:T(8,128)(2,1)S(1)} %collective-permute-done.8.got_ref, bf16[4,256,128]{2,1,0:T(8,128)(2,1)S(1)} %collective-permute-done.10.back_s, ...), custom_call_target="tpu_custom_call" | custom-call | bytes 2097152 | tf_op jit(solution)/shard_map/final_kv/pallas_call | solution.py:298
  (22 shorter events, 0.3 us)
Async XLA Ops:
  0.6 1.0 %copy-start.3 = (bf16[256,4,128]{2,1,0:T(4,128)(2,1)S(1)}, bf16[256,4,128]{2,1,0:T(4,128)(2,1)}, u32[]{:S(2)}) copy-start(bf16[256,4,128]{2,1,0:T(4,128)(2,1)} %k_ref.1) | copy-start | bytes 786436
  1.6 0.9 %copy-start.4 = (bf16[256,4,128]{2,1,0:T(4,128)(2,1)S(1)}, bf16[256,4,128]{2,1,0:T(4,128)(2,1)}, u32[]{:S(2)}) copy-start(bf16[256,4,128]{2,1,0:T(4,128)(2,1)} %v_ref.1) | copy-start | bytes 786436
  2.5 3.4 %copy-start = (bf16[256,8,128]{2,1,0:T(8,128)(2,1)S(1)}, bf16[256,8,128]{2,1,0:T(8,128)(2,1)}, u32[]{:S(2)}) copy-start(bf16[256,8,128]{2,1,0:T(8,128)(2,1)} %q_ref.1) | copy-start | bytes 1572868
  2.8 7.8 %collective-permute-start = (bf16[4,256,128]{2,1,0:T(8,128)(2,1)S(1)}, bf16[4,256,128]{2,1,0:T(8,128)(2,1)S(1)}, u32[]{:S(2)}, u32[]{:S(2)}) collective-permute-start(bf16[4,256,128]{2,1,0:T(8,128)(2,1)S(1)} %get-tuple-element.25), channel_id=1, source_target_pairs={{0,1},{1,0},{2,3},{3,2},{4,5},{5,4},{6,7},{7,6},{8,9},{9,8},{10,11... | collective-permute-start | bytes 786440 | tf_op jit(solution)/shard_map/ppermute | solution.py:224
  3.3 12.5 %collective-permute-start.5 = (bf16[4,256,128]{2,1,0:T(8,128)(2,1)S(1)}, bf16[4,256,128]{2,1,0:T(8,128)(2,1)S(1)}, u32[]{:S(2)}, u32[]{:S(2)}) collective-permute-start(bf16[4,256,128]{2,1,0:T(8,128)(2,1)S(1)} %get-tuple-element.30.kv_s), channel_id=1, source_target_pairs={{0,4},{1,5},{2,6},{3,7},{4,8},{5,9},{6,10},{7,11},{8,12},{9,13},{1... | collective-permute-start | bytes 786440 | tf_op jit(solution)/shard_map/ppermute | solution.py:224
  5.9 1.0 %copy-start.1 = (bf16[256,8,128]{2,1,0:T(8,128)(2,1)S(1)}, bf16[256,8,128]{2,1,0:T(8,128)(2,1)}, u32[]{:S(2)}) copy-start(bf16[256,8,128]{2,1,0:T(8,128)(2,1)} %g_ref.1) | copy-start | bytes 1572868
  6.9 1.0 %copy-start.2 = (bf16[256,8,128]{2,1,0:T(8,128)(2,1)S(1)}, bf16[256,8,128]{2,1,0:T(8,128)(2,1)}, u32[]{:S(2)}) copy-start(bf16[256,8,128]{2,1,0:T(8,128)(2,1)} %o_ref.1) | copy-start | bytes 1572868
  8.0 0.7 %copy-start.5 = (f32[8,256]{1,0:T(8,128)S(1)}, f32[8,256]{1,0:T(8,128)}, u32[]{:S(2)}) copy-start(f32[8,256]{1,0:T(8,128)} %norm_ref.1) | copy-start | bytes 24580
  10.5 14.2 %collective-permute-start.3 = (bf16[8,256,128]{2,1,0:T(8,128)(2,1)S(1)}, bf16[8,256,128]{2,1,0:T(8,128)(2,1)S(1)}, u32[]{:S(2)}, u32[]{:S(2)}) collective-permute-start(bf16[8,256,128]{2,1,0:T(8,128)(2,1)S(1)} %get-tuple-element.27), channel_id=1, source_target_pairs={{0,1},{1,0},{2,3},{3,2},{4,5},{5,4},{6,7},{7,6},{8,9},{9,8},{10,11... | collective-permute-start | bytes 1572872 | tf_op jit(solution)/shard_map/ppermute | solution.py:224
  10.6 11.3 %collective-permute-start.1 = (bf16[4,256,128]{2,1,0:T(8,128)(2,1)S(1)}, bf16[4,256,128]{2,1,0:T(8,128)(2,1)S(1)}, u32[]{:S(2)}, u32[]{:S(2)}) collective-permute-start(bf16[4,256,128]{2,1,0:T(8,128)(2,1)S(1)} %collective-permute-done.kv_r), channel_id=1, source_target_pairs={{0,4},{1,5},{2,6},{3,7},{4,8},{5,9},{6,10},{7,11},{8,12},{9,13},{1... | collective-permute-start | bytes 786440 | tf_op jit(solution)/shard_map/ppermute | solution.py:224
  15.9 12.1 %collective-permute-start.6 = (bf16[4,256,128]{2,1,0:T(8,128)(2,1)S(1)}, bf16[4,256,128]{2,1,0:T(8,128)(2,1)S(1)}, u32[]{:S(2)}, u32[]{:S(2)}) collective-permute-start(bf16[4,256,128]{2,1,0:T(8,128)(2,1)S(1)} %broadcast_select_fusion), channel_id=1, source_target_pairs={{0,2},{1,3},{2,0},{3,1},{4,6},{5,7},{6,4},{7,5},{8,10},{9,11},{10,... | collective-permute-start | bytes 786440 | tf_op jit(solution)/shard_map/ppermute | solution.py:224
  21.9 8.5 %collective-permute-start.2 = (bf16[4,256,128]{2,1,0:T(8,128)(2,1)S(1)}, bf16[4,256,128]{2,1,0:T(8,128)(2,1)S(1)}, u32[]{:S(2)}, u32[]{:S(2)}) collective-permute-start(bf16[4,256,128]{2,1,0:T(8,128)(2,1)S(1)} %broadcast_select_fusion.1), channel_id=1, source_target_pairs={{0,2},{1,3},{2,0},{3,1},{4,6},{5,7},{6,4},{7,5},{8,10},{9,11},{10,... | collective-permute-start | bytes 786440 | tf_op jit(solution)/shard_map/ppermute | solution.py:224
  23.5 1.2 %collective-permute-start.4 = (f32[8,256]{1,0:T(8,128)S(1)}, f32[8,256]{1,0:T(8,128)S(1)}, u32[]{:S(2)}, u32[]{:S(2)}) collective-permute-start(f32[8,256]{1,0:T(8,128)S(1)} %get-tuple-element.29), channel_id=1, source_target_pairs={{0,1},{1,0},{2,3},{3,2},{4,5},{5,4},{6,7},{7,6},{8,9},{9,8},{10,11... | collective-permute-start | bytes 24584 | tf_op jit(solution)/shard_map/ppermute | solution.py:224
  27.5 21.1 %collective-permute-start.8 = (bf16[4,256,128]{2,1,0:T(8,128)(2,1)S(1)}, bf16[4,256,128]{2,1,0:T(8,128)(2,1)S(1)}, u32[]{:S(2)}, u32[]{:S(2)}) collective-permute-start(bf16[4,256,128]{2,1,0:T(8,128)(2,1)S(1)} %convert_element_type.19), channel_id=1, source_target_pairs={{0,1},{1,0},{2,3},{3,2},{4,5},{5,4},{6,7},{7,6},{8,9},{9,8},{10,11... | collective-permute-start | bytes 786440 | tf_op jit(solution)/shard_map/ppermute | solution.py:224
  28.2 9.4 %collective-permute-start.9 = (bf16[4,256,128]{2,1,0:T(8,128)(2,1)S(1)}, bf16[4,256,128]{2,1,0:T(8,128)(2,1)S(1)}, u32[]{:S(2)}, u32[]{:S(2)}) collective-permute-start(bf16[4,256,128]{2,1,0:T(8,128)(2,1)S(1)} %get-tuple-element.42), channel_id=1, source_target_pairs={{0,2},{1,3},{2,0},{3,1},{4,6},{5,7},{6,4},{7,5},{8,10},{9,11},{10,... | collective-permute-start | bytes 786440 | tf_op jit(solution)/shard_map/ppermute | solution.py:224
  30.8 12.3 %collective-permute-start.11 = (bf16[4,256,128]{2,1,0:T(8,128)(2,1)S(1)}, bf16[4,256,128]{2,1,0:T(8,128)(2,1)S(1)}, u32[]{:S(2)}, u32[]{:S(2)}) collective-permute-start(bf16[4,256,128]{2,1,0:T(8,128)(2,1)S(1)} %get-tuple-element.44), channel_id=1, source_target_pairs={{0,2},{1,3},{2,1},{3,0},{4,6},{5,7},{6,5},{7,4},{8,10},{9,11},{10,... | collective-permute-start | bytes 786440 | tf_op jit(solution)/shard_map/ppermute | solution.py:224
  33.3 14.2 %collective-permute-start.7 = (bf16[2,512,128]{2,1,0:T(8,128)(2,1)S(1)}, bf16[2,512,128]{2,1,0:T(8,128)(2,1)S(1)}, u32[]{:S(2)}, u32[]{:S(2)}) collective-permute-start(bf16[2,512,128]{2,1,0:T(8,128)(2,1)S(1)} %multiply_convert_fusion), channel_id=1, source_target_pairs={{0,1},{1,0},{2,3},{3,2},{4,5},{5,4},{6,7},{7,6},{8,9},{9,8},{10,11... | collective-permute-start | bytes 786440 | tf_op jit(solution)/shard_map/ppermute | solution.py:224
  37.6 11.0 %collective-permute-start.10 = (bf16[4,256,128]{2,1,0:T(8,128)(2,1)S(1)}, bf16[4,256,128]{2,1,0:T(8,128)(2,1)S(1)}, u32[]{:S(2)}, u32[]{:S(2)}) collective-permute-start(bf16[4,256,128]{2,1,0:T(8,128)(2,1)S(1)} %add_convert_fusion.1), channel_id=1, source_target_pairs={{0,28},{1,29},{2,30},{3,31},{4,0},{5,1},{6,2},{7,3},{8,4},{9,5},{1... | collective-permute-start | bytes 786440 | tf_op jit(solution)/shard_map/ppermute | solution.py:224
  43.1 10.6 %collective-permute-start.12 = (bf16[4,256,128]{2,1,0:T(8,128)(2,1)S(1)}, bf16[4,256,128]{2,1,0:T(8,128)(2,1)S(1)}, u32[]{:S(2)}, u32[]{:S(2)}) collective-permute-start(bf16[4,256,128]{2,1,0:T(8,128)(2,1)S(1)} %add_convert_fusion), channel_id=1, source_target_pairs={{0,29},{1,28},{2,31},{3,30},{4,1},{5,0},{6,3},{7,2},{8,5},{9,4},{1... | collective-permute-start | bytes 786440 | tf_op jit(solution)/shard_map/ppermute | solution.py:224

commit v2 on v1

v2 whole, which is shorter than its diff:
```python
import functools
import math

import jax
import jax.numpy as jnp
from jax import lax
from jax.experimental import pallas as pl
from jax.experimental.pallas import tpu as pltpu
from jax.sharding import PartitionSpec as P

W = 1024

query_scale = 168.0 ** (-0.5)
LOG2E = math.log2(math.e)
AXIS = "seq"
VMEM_LIMIT = 48 * 1024 * 1024

NT = (((1,), (1,)), ((), ()))
NN = (((1,), (0,)), ((), ()))
TN = (((0,), (0,)), ((), ()))


def dot(a, b, dims):
    return lax.dot_general(a, b, dims, preferred_element_type=jnp.float32)


def call(kernel, name, out_shape, scratch=(), flops=0, in_specs=None):
    specs = {} if in_specs is None else {"in_specs": in_specs}
    return pl.pallas_call(
        kernel,
        out_shape=out_shape,
        scratch_shapes=list(scratch),
        name=name,
        cost_estimate=pl.CostEstimate(flops=flops, bytes_accessed=2 << 20, transcendentals=0),
        compiler_params=pltpu.CompilerParams(vmem_limit_bytes=VMEM_LIMIT),
        **specs,
    )


def fetch(pairs, sems):
    copies = [pltpu.make_async_copy(src, dst, sems.at[n]) for n, (src, dst) in enumerate(pairs)]
    for copy in copies:
        copy.start()
    return copies


def pack_kv_kernel(k_hbm, v_hbm, keep_ref, give_ref, k_ref, v_ref, wide, sems):
    copy_k, copy_v = fetch(((k_hbm, k_ref), (v_hbm, v_ref)), sems)
    rows, heads, _ = k_ref.shape
    half = heads // 2
    core = lax.axis_index(AXIS) % 2
    copy_k.wait()
    wide[:, :heads, :] = k_ref[...].astype(jnp.float32)
    copy_v.wait()
    wide[:, heads:, :] = v_ref[...].astype(jnp.float32)
    flat = wide.reshape(rows * 2 * heads, wide.shape[2])
    for out, side in ((keep_ref, core), (give_ref, 1 - core)):
        for part in range(2):
            for j in range(half):
                head = part * heads + side * half + j
                out[part * half + j] = flat[pl.ds(head, rows, stride=2 * heads), :].astype(out.dtype)


def split_three(x):
    parts = []
    for _ in range(3):
        part = x.astype(jnp.bfloat16)
        parts.append(part)
        x = x - part.astype(jnp.float32)
    return parts


def join_three(ref, start, count):
    high, mid, low = (ref[start + n * count : start + (n + 1) * count].astype(jnp.float32) for n in range(3))
    return high + mid + low


def pack_q_kernel(
    q_hbm, g_hbm, o_hbm, norm_ref, after, keep_ref, keep_rows, give_ref, q_ref, g_ref, o_ref, wide, give_rows, sems
):
    copy_q, copy_g, copy_o = fetch(((q_hbm, q_ref), (g_hbm, g_ref), (o_hbm, o_ref)), sems)
    rows, heads, size = q_ref.shape
    half = heads // 2
    pieces = rows // size
    core = lax.axis_index(AXIS) % 2
    ones = jnp.ones((8, size), jnp.float32)
    flat = wide.reshape(rows * heads, size)
    sides = ((keep_ref, keep_rows, core), (give_ref, give_rows, 1 - core))

    def spread(base):
        for out, _, side in sides:
            for j in range(half):
                block = flat[pl.ds(side * half + j, rows, stride=heads), :]
                out[(base + j) * rows : (base + j + 1) * rows] = block.astype(out.dtype)

    copy_q.wait()
    wide[...] = q_ref[...].astype(jnp.float32)
    spread(0)
    copy_g.wait()
    wide[...] = g_ref[...].astype(jnp.float32)
    spread(half)
    copy_o.wait()
    wide[...] = g_ref[...].astype(jnp.float32) * o_ref[...].astype(jnp.float32)
    for _, out, side in sides:
        for j in range(half):
            product = flat[pl.ds(side * half + j, rows, stride=heads), :]
            delta = lax.dot_general(
                ones, product, NT, precision=lax.Precision.HIGHEST, preferred_element_type=jnp.float32
            )
            norm = norm_ref[pl.ds(side * half + j, 1), :] * LOG2E
            for n in range(pieces):
                out[j * pieces + n : j * pieces + n + 1] = norm[:, n * size : (n + 1) * size]
                at = (half + j) * pieces + n
                out[at : at + 1] = delta[:1, n * size : (n + 1) * size]
    count = heads * pieces
    for n, part in enumerate(split_three(give_rows[...])):
        give_ref[heads * rows + n * count : heads * rows + (n + 1) * count] = part


def rows_of(row_ref, qg_ref, rows, size):
    if row_ref is not None:
        return row_ref[...]
    total = qg_ref.shape[0] - qg_ref.shape[0] % rows
    return join_three(qg_ref, total, (qg_ref.shape[0] - total) // 3)


def tile(kv_ref, side, grad_ref, gq_in, gq_ref, offset, first):
    qg_ref, row_ref = side
    groups = kv_ref.shape[0] // 2
    rows, size = kv_ref.shape[1], kv_ref.shape[2]
    span = gq_ref.shape[1]
    share = span // rows
    heads = groups * share
    pieces = span // size
    vectors = rows_of(row_ref, qg_ref, rows, size)

    def vector(at):
        return jnp.concatenate([vectors[at + n : at + n + 1] for n in range(pieces)], 1)

    for g in range(groups):
        k = kv_ref[g]
        v = kv_ref[groups + g]
        q = qg_ref[g * span : (g + 1) * span]
        d = qg_ref[heads * rows + g * span : heads * rows + (g + 1) * span]
        norm = vector(g * pieces)
        delta = vector((groups + g) * pieces)
        x = dot(k, q, NT) * (query_scale * LOG2E) - norm
        if offset is not None:
            key = lax.broadcasted_iota(jnp.int32, (rows, rows), 0)
            query = lax.broadcasted_iota(jnp.int32, (rows, rows), 1)
            gap = query - key + offset
            seen = (gap >= 0) & (gap < W)
            x = jnp.concatenate(
                [jnp.where(seen, x[:, j * rows : (j + 1) * rows], -jnp.inf) for j in range(share)], 1
            )
        p = jnp.exp2(x)
        ds = (p * (dot(v, d, NT) - delta)).astype(jnp.bfloat16)
        gv = dot(p.astype(jnp.bfloat16), d, NN)
        gk = dot(ds, q, NN)
        gq = dot(ds, k, TN)
        if first:
            grad_ref[g] = gk
            grad_ref[groups + g] = gv
        else:
            grad_ref[g] += gk
            grad_ref[groups + g] += gv
        gq_ref[g] = gq if gq_in is None else gq_in[g] + gq


def scale_keys(grad_ref):
    groups = grad_ref.shape[0] // 2
    grad_ref[:groups] = grad_ref[:groups] * query_scale


def own_kernel(kv_s, kv_r, qg_s, rows_s, qg_r, gq_s_in, gq_r_in, grad_s, grad_r, gq_s, gq_r):
    side_s, side_r = (qg_s, rows_s), (qg_r, None)
    core = lax.axis_index(AXIS) % 2
    tile(kv_s, side_s, grad_s, gq_s_in, gq_s, 0, True)
    tile(kv_r, side_r, grad_r, gq_r_in, gq_r, 0, True)

    @pl.when(core == 0)
    def _():
        tile(kv_s, side_r, grad_s, gq_r, gq_r, None, False)

    @pl.when(core == 1)
    def _():
        tile(kv_r, side_s, grad_r, gq_s, gq_s, None, False)

    scale_keys(grad_s)
    scale_keys(grad_r)


def far_kernel(first, kv, qg_s, rows_s, qg_r, *refs):
    if first:
        out, gq_s, gq_r, grad = refs
        side_s, side_r, seen_by = (qg_s, rows_s), (qg_r, None), 1
    else:
        gq_r_in, gq_s_in, out, gq_r, gq_s, grad = refs
        side_s, side_r, seen_by = (qg_r, None), (qg_s, rows_s), 0
    device = lax.axis_index(AXIS)
    core = device % 2
    valid = device // 2 >= 2
    rows = kv.shape[1]

    @pl.when(valid)
    def _():
        tile(kv, side_s, grad, None if first else gq_s_in, gq_s, W, True)

    @pl.when(valid & (core == seen_by))
    def _():
        tile(kv, side_r, grad, None if first else gq_r_in, gq_r, None, False)

    @pl.when(valid)
    def _():
        scale_keys(grad)
        out[...] = grad[...].astype(out.dtype)

    @pl.when(jnp.logical_not(valid))
    def _():
        out[...] = jnp.zeros_like(out)
        gq_s[...] = jnp.zeros_like(gq_s) if first else gq_s_in[...]

    @pl.when(jnp.logical_not(valid & (core == seen_by)))
    def _():
        gq_r[...] = jnp.zeros_like(gq_r) if first else gq_r_in[...]


def near_kernel(kv, qg_s, rows_s, qg_r, gq_s_in, gq_r_in, out, gq_s, gq_r, grad):
    side_s, side_r = (qg_s, rows_s), (qg_r, None)
    valid = lax.axis_index(AXIS) // 2 >= 1

    @pl.when(valid)
    def _():
        tile(kv, side_s, grad, gq_s_in, gq_s, None, True)
        tile(kv, side_r, grad, gq_r_in, gq_r, None, False)
        scale_keys(grad)
        out[...] = grad[...].astype(out.dtype)

    @pl.when(jnp.logical_not(valid))
    def _():
        out[...] = jnp.zeros_like(out)
        gq_s[...] = gq_s_in[...]
        gq_r[...] = gq_r_in[...]


def final_q_kernel(own_ref, got_ref, out_ref, wide):
    rows, heads, size = out_ref.shape
    half = heads // 2
    core = lax.axis_index(AXIS) % 2
    flat = wide.reshape(rows * heads, size)
    share = half // own_ref.shape[0]
    skip = got_ref.shape[0] - half
    for j in range(half):
        g, r = j // share, j % share
        flat[pl.ds(core * half + j, rows, stride=heads), :] = own_ref[g, r * rows : (r + 1) * rows] * query_scale
        flat[pl.ds((1 - core) * half + j, rows, stride=heads), :] = got_ref[skip + j].astype(jnp.float32)
    out_ref[...] = wide[...].astype(out_ref.dtype)


def final_kv_kernel(own_ref, got_ref, back_s, back_r, side_s, side_r, out_k, out_v, wide):
    rows, heads, size = out_k.shape
    half = heads // 2
    device = lax.axis_index(AXIS)
    core = device % 2
    even = jnp.where((device // 2) % 2 == 0, 1.0, 0.0).astype(jnp.float32)
    flat = wide.reshape(rows * 2 * heads, size)
    for side, base_ref, back_ref, near_ref, share in (
        (core, own_ref, back_s, side_s, None),
        (1 - core, got_ref, back_r, side_r, even),
    ):
        for part in range(2):
            for j in range(half):
                n = part * half + j
                near = near_ref[n].astype(jnp.float32)
                near = near if share is None else near * share
                total = base_ref[n].astype(jnp.float32) + back_ref[n].astype(jnp.float32) + near
                flat[pl.ds(part * heads + side * half + j, rows, stride=2 * heads), :] = total
    out_k[...] = wide[:, :heads, :].astype(out_k.dtype)
    out_v[...] = wide[:, heads:, :].astype(out_v.dtype)


def shards(queries, key_rows, value_rows, attn_output, grad_output, log_norm):
    rows, heads, size = queries.shape
    groups = key_rows.shape[1]
    devices = lax.axis_size(AXIS)
    hops = W // rows
    assert hops == 4 and devices % 4 == 0
    low, f32 = jnp.bfloat16, jnp.float32
    device = lax.axis_index(AXIS)
    even = (device // 2) % 2 == 0

    def move(x, target):
        return lax.ppermute(x, AXIS, [(i, target(i)) for i in range(devices)])

    ahead = lambda i: (i + hops) % devices
    behind = lambda i: (i - hops) % devices
    sibling = lambda i: i ^ 1
    beside = lambda i: i ^ 2

    shape = jax.ShapeDtypeStruct
    kv_block = (groups, rows, size)
    qg_rows = heads * rows
    row_block = (heads * rows // size, size)
    gq_block = (groups // 2, heads // groups * rows, size)
    tile_flops = 10 * rows * rows * size * heads // 2

    hbm = pl.BlockSpec(memory_space=pltpu.HBM)
    vmem = pl.BlockSpec(memory_space=pltpu.VMEM)
    anywhere = pl.BlockSpec(memory_space=pl.ANY)
    hbm = pl.BlockSpec(memory_space=pltpu.HBM)
    vmem = pl.BlockSpec(memory_space=pltpu.VMEM)
    anywhere = pl.BlockSpec(memory_space=pl.ANY)

    def pin(x):
        return pltpu.with_memory_space_constraint(x, pltpu.HBM)

    kv_s, kv_give = call(
        pack_kv_kernel,
        "pack_kv",
        [shape(kv_block, low)] * 2,
        [pltpu.VMEM(key_rows.shape, low)] * 2
        + [pltpu.VMEM((rows, 2 * groups, size), f32), pltpu.SemaphoreType.DMA((2,))],
        in_specs=[hbm, hbm],
    )(pin(key_rows), pin(value_rows))
    kv_r = move(kv_give, sibling)
    two_s = move(kv_s, ahead)
    one_r = move(kv_r, lambda i: (i + 2) % devices)
    two_r = move(kv_r, ahead)
    qg_s, rows_s, qg_give = call(
        pack_q_kernel,
        "pack_q",
        [shape((qg_rows, size), low), shape(row_block, f32), shape((qg_rows + 3 * row_block[0], size), low)],
        [pltpu.VMEM(queries.shape, low)] * 3
        + [pltpu.VMEM((rows, heads, size), f32), pltpu.VMEM(row_block, f32), pltpu.SemaphoreType.DMA((3,))],
        in_specs=[hbm, hbm, hbm, vmem, anywhere],
    )(pin(queries), pin(grad_output), pin(attn_output), log_norm, kv_r)
    qg_r = move(qg_give, sibling)
    one_s = move(jnp.where(even, kv_s, two_s), beside)

    acc = [shape(gq_block, f32)] * 2
    grad_scratch = [pltpu.VMEM(kv_block, f32)]
    sides = (qg_s, rows_s, qg_r)
    far_s, gq_s, gq_r = call(
        functools.partial(far_kernel, True),
        "far_s",
        [shape(kv_block, low)] + acc,
        grad_scratch,
        flops=2 * tile_flops,
    )(two_s, *sides)
    back_s = move(far_s, behind)
    own_s, own_r, gq_s, gq_r = call(
        own_kernel, "own", [shape(kv_block, f32)] * 2 + acc, flops=3 * tile_flops
    )(kv_s, kv_r, *sides, gq_s, gq_r)
    near = functools.partial(
        call, near_kernel, out_shape=[shape(kv_block, low)] + acc, scratch=grad_scratch, flops=2 * tile_flops
    )
    near_r, gq_s, gq_r = near(name="near_r")(one_r, *sides, gq_s, gq_r)
    side_r = move(near_r, lambda i: i ^ 3 if i & 2 else i ^ 2)
    near_s, gq_s, gq_r = near(name="near_s")(one_s, *sides, gq_s, gq_r)
    side_s = move(near_s, lambda i: (i - 2) % devices)
    far_r, gq_s, gq_r = call(
        functools.partial(far_kernel, False),
        "far_r",
        [shape(kv_block, f32)] + acc,
        grad_scratch,
        flops=2 * tile_flops,
    )(two_r, *sides, gq_s, gq_r)
    side_r, back_s = lax.optimization_barrier((side_r, back_s))
    joined = (far_r + jnp.where(even, 0.0, side_r.astype(f32))).astype(low)
    back_r = move(joined, lambda i: sibling(behind(i)))
    give = jnp.concatenate([own_r.astype(low), (gq_r * query_scale).astype(low).reshape(-1, rows, size)])
    got = move(give, sibling)
    grad_q = call(
        final_q_kernel,
        "final_q",
        shape(queries.shape, low),
        [pltpu.VMEM((rows, heads, size), f32)],
    )(gq_s, got)
    grad_k, grad_v = call(
        final_kv_kernel,
        "final_kv",
        [shape(key_rows.shape, low), shape(value_rows.shape, low)],
        [pltpu.VMEM((rows, 2 * groups, size), f32)],
    )(own_s, got, back_s, back_r, side_s, side_r)
    return grad_q, grad_k, grad_v


def solution(mesh):
    in_specs = (
        P("seq", None, None),
        P("seq", None, None),
        P("seq", None, None),
        P("seq", None, None),
        P("seq", None, None),
        P(None, "seq"),
    )
    out_specs = (P("seq", None, None), P("seq", None, None), P("seq", None, None))
    return jax.shard_map(shards, mesh=mesh, in_specs=in_specs, out_specs=out_specs, check_vma=False)
```

time: 55.3 us -> 54.6 us (0.987)
  local copies, waits for them, and re-layouts: 4.75 us -> 0.01 us
  waiting for transfers between devices: 18.5 us -> 21 us
  Pallas kernels: 7.93 us -> 9.71 us
    unnamed x12 -> x2, local copies, waits for them, and re-layouts: 4.68 us -> 0.01 us
    ppermute x13 -> x11, waiting for transfers between devices: 18.5 us -> 21 us  [move(): return lax.ppermute(x, AXIS, [(i, target(i)) for i in range(devices)])]
    pallas_call x6 -> x7, Pallas kernels: 5.49 us -> 7.28 us  [the longest x1 2.69 us: shards(): call(own_kernel, 'own', [shape(kv_block, f32)] * 2 + acc, flops=3 * tile_...]
    ppermute x13 -> x11, starting transfers between devices: 22.8 us -> 22.8 us  [move(): return lax.ppermute(x, AXIS, [(i, target(i)) for i in range(devices)])]
  transfers between devices with their start and end apart: 13 -> 11, of which waited for: 5 -> 3; matrix products, arithmetic and copies ran while one was open for 1% -> 0% of each run, Pallas kernels for 12% -> 13%
where the time goes in v2:
time: 54.6 us; the launch traced here: 54.5 us
  starting transfers between devices  22.8 us (42%)
  waiting for transfers between devices  21 us (38%)
  Pallas kernels  9.71 us (18%)
  between operations  0.76 us (1%)
    ppermute x11, starting transfers between devices, move(): return lax.ppermute(x, AXIS, [(i, target(i)) for i in range(devices)])  22.8 us
    ppermute x11, waiting for transfers between devices, move(): return lax.ppermute(x, AXIS, [(i, target(i)) for i in range(devices)])  21 us
    pallas_call x1, Pallas kernels, shards(): call(own_kernel, 'own', [shape(kv_block, f32)] * 2 + acc, flops=3 * tile_...  2.69 us
    pallas_call x1, Pallas kernels, shards(): call(pack_q_kernel, 'pack_q', [shape((qg_rows, size), low), shape(row_blo...  2.67 us
    pallas_call x1, Pallas kernels, shards(): call(final_kv_kernel, 'final_kv', [shape(key_rows.shape, low), shape(valu...  1.3 us
    pallas_call x1, Pallas kernels, shards(): call(pack_kv_kernel, 'pack_kv', [shape(kv_block, low)] * 2, [pltpu.VMEM(k...  1.27 us
    pallas_call x1, Pallas kernels, shards(): call(final_q_kernel, 'final_q', shape(queries.shape, low), [pltpu.VMEM((r...  1.13 us
  transfers between devices with their start and end apart: 11, of which 3 were waited for; matrix products, arithmetic and copies ran while one was open for 0% of the time, Pallas kernels for 13%

profile of v2, /device:TPU:0, one launch (start us, length us, event | category | flops | bytes accessed | tf_op | source)
XLA Modules:
  0.0 54.5 jit_solution(4636809937092645581)
XLA Ops:
  0.6 1.3 %pack_kv.1 = (bf16[4,256,128]{2,1,0:T(8,128)(2,1)S(1)}, bf16[4,256,128]{2,1,0:T(8,128)(2,1)S(1)}) custom-call(bf16[256,4,128]{2,1,0:T(4,128)(2,1)} %k_hbm.1, bf16[256,4,128]{2,1,0:T(4,128)(2,1)} %v_hbm.1), custom_call_target="tpu_custom_call" | custom-call | bytes 2097152 | tf_op jit(solution)/shard_map/pack_kv/pallas_call | solution.py:317
  1.9 0.5 collective-permute-start
  2.4 2.6 %collective-permute-start.3 = (bf16[4,256,128]{2,1,0:T(8,128)(2,1)S(1)}, bf16[4,256,128]{2,1,0:T(8,128)(2,1)S(1)}, u32[]{:S(2)}, u32[]{:S(2)}) collective-permute-start(bf16[4,256,128]{2,1,0:T(8,128)(2,1)S(1)} %get-tuple-element.32.kv_s), channel_id=1, source_target_pairs={{0,4},{1,5},{2,6},{3,7},{4,8},{5,9},{6,10},{7,11},{8,12},{9,13},{1... | collective-permute-start | bytes 786440 | tf_op jit(solution)/shard_map/ppermute | solution.py:293
  5.0 0.0 collective-permute-done.after.kv_r
  5.0 2.7 %pack_q.1 = (bf16[2048,128]{1,0:T(8,128)(2,1)S(1)}, f32[16,128]{1,0:T(8,128)S(1)}, bf16[2096,128]{1,0:T(8,128)(2,1)S(1)}) custom-call(bf16[256,8,128]{2,1,0:T(8,128)(2,1)} %q_hbm.1, bf16[256,8,128]{2,1,0:T(8,128)(2,1)} %g_hbm.1, bf16[256,8,128]{2,1,0:T(8,128)(2,1)} %o_hbm.1, f32[8,256]{1,0:T(8,128)S(1)} %copy-done, ...), custom_call_target="tpu_custom_call" | custom-call | bytes 2097152 | tf_op jit(solution)/shard_map/pack_q/pallas_call | solution.py:329
  7.7 0.2 collective-permute-start.2
  7.9 1.5 %collective-permute-start.5 = (bf16[4,256,128]{2,1,0:T(8,128)(2,1)S(1)}, bf16[4,256,128]{2,1,0:T(8,128)(2,1)S(1)}, u32[]{:S(2)}, u32[]{:S(2)}) collective-permute-start(bf16[4,256,128]{2,1,0:T(8,128)(2,1)S(1)} %collective-permute-done.after.kv_r), channel_id=1, source_target_pairs={{0,2},{1,3},{2,4},{3,5},{4,6},{5,7},{6,8},{7,9},{8,10},{9,11},{10,... | collective-permute-start | bytes 786440 | tf_op jit(solution)/shard_map/ppermute | solution.py:293
  9.4 7.5 %collective-permute-done.3.kv = bf16[4,256,128]{2,1,0:T(8,128)(2,1)S(1)} collective-permute-done((bf16[4,256,128]{2,1,0:T(8,128)(2,1)S(1)}, bf16[4,256,128]{2,1,0:T(8,128)(2,1)S(1)}, u32[]{:S(2)}, u32[]{:S(2)}) %collective-permute-start.3) | collective-permute-done | bytes 262176 | tf_op jit(solution)/shard_map/ppermute | solution.py:293
  16.9 0.1 collective-permute-start.4
  17.0 2.7 %collective-permute-start.1 = (bf16[4,256,128]{2,1,0:T(8,128)(2,1)S(1)}, bf16[4,256,128]{2,1,0:T(8,128)(2,1)S(1)}, u32[]{:S(2)}, u32[]{:S(2)}) collective-permute-start(bf16[4,256,128]{2,1,0:T(8,128)(2,1)S(1)} %collective-permute-done.after.kv_r), channel_id=1, source_target_pairs={{0,4},{1,5},{2,6},{3,7},{4,8},{5,9},{6,10},{7,11},{8,12},{9,13},{1... | collective-permute-start | bytes 786440 | tf_op jit(solution)/shard_map/ppermute | solution.py:293
  19.7 0.0 collective-permute-done.2.qg_r
  19.7 0.1 far_s.1
  19.8 4.1 %collective-permute-start.8 = (bf16[4,256,128]{2,1,0:T(8,128)(2,1)S(1)}, bf16[4,256,128]{2,1,0:T(8,128)(2,1)S(1)}, u32[]{:S(2)}, u32[]{:S(2)}) collective-permute-start(bf16[4,256,128]{2,1,0:T(8,128)(2,1)S(1)} %get-tuple-element.46), channel_id=1, source_target_pairs={{0,28},{1,29},{2,30},{3,31},{4,0},{5,1},{6,2},{7,3},{8,4},{9,5},{1... | collective-permute-start | bytes 786440 | tf_op jit(solution)/shard_map/ppermute | solution.py:293
  23.9 2.7 %own.1 = (f32[4,256,128]{2,1,0:T(8,128)S(1)}, f32[4,256,128]{2,1,0:T(8,128)S(1)}, f32[2,512,128]{2,1,0:T(8,128)S(1)}, f32[2,512,128]{2,1,0:T(8,128)S(1)}) custom-call(bf16[4,256,128]{2,1,0:T(8,128)(2,1)S(1)} %get-tuple-element.32.kv_s, bf16[4,256,128]{2,1,0:T(8,128)(2,1)S(1)} %collective-permute-done.after.kv_r, ...), custom_call_target="tpu_custom_call" | custom-call | flops 1006632960 | bytes 2097152 | tf_op jit(solution)/shard_map/own/pallas_call | solution.py:351
  26.7 0.0 collective-permute-done.5.kv
  26.7 0.1 near_r.1
  26.8 3.5 %collective-permute-start.7 = (bf16[4,256,128]{2,1,0:T(8,128)(2,1)S(1)}, bf16[4,256,128]{2,1,0:T(8,128)(2,1)S(1)}, u32[]{:S(2)}, u32[]{:S(2)}) collective-permute-start(bf16[4,256,128]{2,1,0:T(8,128)(2,1)S(1)} %get-tuple-element.45), channel_id=1, source_target_pairs={{0,2},{1,3},{2,1},{3,0},{4,6},{5,7},{6,5},{7,4},{8,10},{9,11},{10,... | collective-permute-start | bytes 786440 | tf_op jit(solution)/shard_map/ppermute | solution.py:293
  30.3 0.0 collective-permute-done.4.kv
  30.3 0.1 near_s.1
  30.5 0.0 collective-permute-done.1.kv
  30.5 0.3 far_r.1
  30.8 0.1 multiply_convert_fusion
  30.9 0.1 collective-permute-start.6
  31.0 7.4 %collective-permute-start.10 = (bf16[4,256,128]{2,1,0:T(8,128)(2,1)S(1)}, bf16[4,256,128]{2,1,0:T(8,128)(2,1)S(1)}, u32[]{:S(2)}, u32[]{:S(2)}) collective-permute-start(bf16[4,256,128]{2,1,0:T(8,128)(2,1)S(1)} %get-tuple-element.50), channel_id=1, source_target_pairs={{0,30},{1,31},{2,0},{3,1},{4,2},{5,3},{6,4},{7,5},{8,6},{9,7},{10,... | collective-permute-start | bytes 786440 | tf_op jit(solution)/shard_map/ppermute | solution.py:293
  38.4 0.0 collective-permute-done.8.back_s
  38.4 0.1 add_convert_fusion
  38.5 0.1 collective-permute-start.9
  38.6 0.0 collective-permute-done.6.got_ref
  38.6 1.1 %final_q.1 = bf16[256,8,128]{2,1,0:T(8,128)(2,1)} custom-call(f32[2,512,128]{2,1,0:T(8,128)S(1)} %get-tuple-element.41.own_ref, bf16[8,256,128]{2,1,0:T(8,128)(2,1)S(1)} %collective-permute-done.6.got_ref), custom_call_target="tpu_custom_call" | custom-call | bytes 2097152 | tf_op jit(solution)/shard_map/final_q/pallas_call | solution.py:373
  39.7 7.4 %collective-permute-done.10.side_s = bf16[4,256,128]{2,1,0:T(8,128)(2,1)S(1)} collective-permute-done((bf16[4,256,128]{2,1,0:T(8,128)(2,1)S(1)}, bf16[4,256,128]{2,1,0:T(8,128)(2,1)S(1)}, u32[]{:S(2)}, u32[]{:S(2)}) %collective-permute-start.10) | collective-permute-done | bytes 262176 | tf_op jit(solution)/shard_map/ppermute | solution.py:293
  47.0 6.1 %collective-permute-done.9.back_r = bf16[4,256,128]{2,1,0:T(8,128)(2,1)S(1)} collective-permute-done((bf16[4,256,128]{2,1,0:T(8,128)(2,1)S(1)}, bf16[4,256,128]{2,1,0:T(8,128)(2,1)S(1)}, u32[]{:S(2)}, u32[]{:S(2)}) %collective-permute-start.9) | collective-permute-done | bytes 262176 | tf_op jit(solution)/shard_map/ppermute | solution.py:293
  53.2 1.3 %final_kv.1 = (bf16[256,4,128]{2,1,0:T(4,128)(2,1)}, bf16[256,4,128]{2,1,0:T(4,128)(2,1)}) custom-call(f32[4,256,128]{2,1,0:T(8,128)S(1)} %get-tuple-element.44.own_ref, bf16[8,256,128]{2,1,0:T(8,128)(2,1)S(1)} %collective-permute-done.6.got_ref, bf16[4,256,128]{2,1,0:T(8,128)(2,1)S(1)} %collective-permute-done.8.back_s, ...), custom_call_target="tpu_custom_call" | custom-call | bytes 2097152 | tf_op jit(solution)/shard_map/final_kv/pallas_call | solution.py:379
  (6 shorter events, 0.1 us)
Async XLA Ops:
  0.6 4.4 %copy-start = (f32[8,256]{1,0:T(8,128)S(1)}, f32[8,256]{1,0:T(8,128)}, u32[]{:S(2)}) copy-start(f32[8,256]{1,0:T(8,128)} %norm_ref.1) | copy-start | bytes 24580
  1.9 3.1 %collective-permute-start = (bf16[4,256,128]{2,1,0:T(8,128)(2,1)S(1)}, bf16[4,256,128]{2,1,0:T(8,128)(2,1)S(1)}, u32[]{:S(2)}, u32[]{:S(2)}) collective-permute-start(bf16[4,256,128]{2,1,0:T(8,128)(2,1)S(1)} %get-tuple-element.28), channel_id=1, source_target_pairs={{0,1},{1,0},{2,3},{3,2},{4,5},{5,4},{6,7},{7,6},{8,9},{9,8},{10,11... | collective-permute-start | bytes 786440 | tf_op jit(solution)/shard_map/ppermute | solution.py:293
  2.4 14.4 %collective-permute-start.3 = (bf16[4,256,128]{2,1,0:T(8,128)(2,1)S(1)}, bf16[4,256,128]{2,1,0:T(8,128)(2,1)S(1)}, u32[]{:S(2)}, u32[]{:S(2)}) collective-permute-start(bf16[4,256,128]{2,1,0:T(8,128)(2,1)S(1)} %get-tuple-element.32.kv_s), channel_id=1, source_target_pairs={{0,4},{1,5},{2,6},{3,7},{4,8},{5,9},{6,10},{7,11},{8,12},{9,13},{1... | collective-permute-start | bytes 786440 | tf_op jit(solution)/shard_map/ppermute | solution.py:293
  7.7 12.0 %collective-permute-start.2 = (bf16[2096,128]{1,0:T(8,128)(2,1)S(1)}, bf16[2096,128]{1,0:T(8,128)(2,1)S(1)}, u32[]{:S(2)}, u32[]{:S(2)}) collective-permute-start(bf16[2096,128]{1,0:T(8,128)(2,1)S(1)} %get-tuple-element.31), channel_id=1, source_target_pairs={{0,1},{1,0},{2,3},{3,2},{4,5},{5,4},{6,7},{7,6},{8,9},{9,8},{10,11... | collective-permute-start | bytes 1609736 | tf_op jit(solution)/shard_map/ppermute | solution.py:293
  7.9 18.7 %collective-permute-start.5 = (bf16[4,256,128]{2,1,0:T(8,128)(2,1)S(1)}, bf16[4,256,128]{2,1,0:T(8,128)(2,1)S(1)}, u32[]{:S(2)}, u32[]{:S(2)}) collective-permute-start(bf16[4,256,128]{2,1,0:T(8,128)(2,1)S(1)} %collective-permute-done.after.kv_r), channel_id=1, source_target_pairs={{0,2},{1,3},{2,4},{3,5},{4,6},{5,7},{6,8},{7,9},{8,10},{9,11},{10,... | collective-permute-start | bytes 786440 | tf_op jit(solution)/shard_map/ppermute | solution.py:293
  16.9 13.4 %collective-permute-start.4 = (bf16[4,256,128]{2,1,0:T(8,128)(2,1)S(1)}, bf16[4,256,128]{2,1,0:T(8,128)(2,1)S(1)}, u32[]{:S(2)}, u32[]{:S(2)}) collective-permute-start(bf16[4,256,128]{2,1,0:T(8,128)(2,1)S(1)} %broadcast_select_fusion), channel_id=1, source_target_pairs={{0,2},{1,3},{2,0},{3,1},{4,6},{5,7},{6,4},{7,5},{8,10},{9,11},{10,... | collective-permute-start | bytes 786440 | tf_op jit(solution)/shard_map/ppermute | solution.py:293
  17.0 13.5 %collective-permute-start.1 = (bf16[4,256,128]{2,1,0:T(8,128)(2,1)S(1)}, bf16[4,256,128]{2,1,0:T(8,128)(2,1)S(1)}, u32[]{:S(2)}, u32[]{:S(2)}) collective-permute-start(bf16[4,256,128]{2,1,0:T(8,128)(2,1)S(1)} %collective-permute-done.after.kv_r), channel_id=1, source_target_pairs={{0,4},{1,5},{2,6},{3,7},{4,8},{5,9},{6,10},{7,11},{8,12},{9,13},{1... | collective-permute-start | bytes 786440 | tf_op jit(solution)/shard_map/ppermute | solution.py:293
  19.8 18.6 %collective-permute-start.8 = (bf16[4,256,128]{2,1,0:T(8,128)(2,1)S(1)}, bf16[4,256,128]{2,1,0:T(8,128)(2,1)S(1)}, u32[]{:S(2)}, u32[]{:S(2)}) collective-permute-start(bf16[4,256,128]{2,1,0:T(8,128)(2,1)S(1)} %get-tuple-element.46), channel_id=1, source_target_pairs={{0,28},{1,29},{2,30},{3,31},{4,0},{5,1},{6,2},{7,3},{8,4},{9,5},{1... | collective-permute-start | bytes 786440 | tf_op jit(solution)/shard_map/ppermute | solution.py:293
  26.8 11.6 %collective-permute-start.7 = (bf16[4,256,128]{2,1,0:T(8,128)(2,1)S(1)}, bf16[4,256,128]{2,1,0:T(8,128)(2,1)S(1)}, u32[]{:S(2)}, u32[]{:S(2)}) collective-permute-start(bf16[4,256,128]{2,1,0:T(8,128)(2,1)S(1)} %get-tuple-element.45), channel_id=1, source_target_pairs={{0,2},{1,3},{2,1},{3,0},{4,6},{5,7},{6,5},{7,4},{8,10},{9,11},{10,... | collective-permute-start | bytes 786440 | tf_op jit(solution)/shard_map/ppermute | solution.py:293
  30.9 7.7 %collective-permute-start.6 = (bf16[8,256,128]{2,1,0:T(8,128)(2,1)S(1)}, bf16[8,256,128]{2,1,0:T(8,128)(2,1)S(1)}, u32[]{:S(2)}, u32[]{:S(2)}) collective-permute-start(bf16[8,256,128]{2,1,0:T(8,128)(2,1)S(1)} %pad_maximum_fusion), channel_id=1, source_target_pairs={{0,1},{1,0},{2,3},{3,2},{4,5},{5,4},{6,7},{7,6},{8,9},{9,8},{10,11... | collective-permute-start | bytes 1572872 | tf_op jit(solution)/shard_map/ppermute | solution.py:293
  31.0 16.1 %collective-permute-start.10 = (bf16[4,256,128]{2,1,0:T(8,128)(2,1)S(1)}, bf16[4,256,128]{2,1,0:T(8,128)(2,1)S(1)}, u32[]{:S(2)}, u32[]{:S(2)}) collective-permute-start(bf16[4,256,128]{2,1,0:T(8,128)(2,1)S(1)} %get-tuple-element.50), channel_id=1, source_target_pairs={{0,30},{1,31},{2,0},{3,1},{4,2},{5,3},{6,4},{7,5},{8,6},{9,7},{10,... | collective-permute-start | bytes 786440 | tf_op jit(solution)/shard_map/ppermute | solution.py:293
  38.5 14.7 %collective-permute-start.9 = (bf16[4,256,128]{2,1,0:T(8,128)(2,1)S(1)}, bf16[4,256,128]{2,1,0:T(8,128)(2,1)S(1)}, u32[]{:S(2)}, u32[]{:S(2)}) collective-permute-start(bf16[4,256,128]{2,1,0:T(8,128)(2,1)S(1)} %add_convert_fusion), channel_id=1, source_target_pairs={{0,29},{1,28},{2,31},{3,30},{4,1},{5,0},{6,3},{7,2},{8,5},{9,4},{1... | collective-permute-start | bytes 786440 | tf_op jit(solution)/shard_map/ppermute | solution.py:293

commit v3 on v2

--- a/solution.py
+++ b/solution.py
@@ -13,7 +13,8 @@
 query_scale = 168.0 ** (-0.5)
 LOG2E = math.log2(math.e)
 AXIS = "seq"
-VMEM_LIMIT = 48 * 1024 * 1024
+VMEM_LIMIT = 16 * 1024 * 1024
+LONG = 10**9
 
 NT = (((1,), (1,)), ((), ()))
 NN = (((1,), (0,)), ((), ()))
@@ -76,7 +77,22 @@
 
 
 def pack_q_kernel(
-    q_hbm, g_hbm, o_hbm, norm_ref, after, keep_ref, keep_rows, give_ref, q_ref, g_ref, o_ref, wide, give_rows, sems
+    q_hbm,
+    g_hbm,
+    o_hbm,
+    norm_ref,
+    after,
+    keep_q,
+    keep_g,
+    keep_rows,
+    give_q,
+    give_g,
+    q_ref,
+    g_ref,
+    o_ref,
+    wide,
+    give_rows,
+    sems,
 ):
     copy_q, copy_g, copy_o = fetch(((q_hbm, q_ref), (g_hbm, g_ref), (o_hbm, o_ref)), sems)
     rows, heads, size = q_ref.shape
@@ -85,23 +101,22 @@
     core = lax.axis_index(AXIS) % 2
     ones = jnp.ones((8, size), jnp.float32)
     flat = wide.reshape(rows * heads, size)
-    sides = ((keep_ref, keep_rows, core), (give_ref, give_rows, 1 - core))
-
-    def spread(base):
-        for out, _, side in sides:
+
+    def spread(outs):
+        for out, side in zip(outs, (core, 1 - core), strict=True):
             for j in range(half):
                 block = flat[pl.ds(side * half + j, rows, stride=heads), :]
-                out[(base + j) * rows : (base + j + 1) * rows] = block.astype(out.dtype)
+                out[j * rows : (j + 1) * rows] = block.astype(out.dtype)
 
     copy_q.wait()
     wide[...] = q_ref[...].astype(jnp.float32)
-    spread(0)
+    spread((keep_q, give_q))
     copy_g.wait()
     wide[...] = g_ref[...].astype(jnp.float32)
-    spread(half)
+    spread((keep_g, give_g))
     copy_o.wait()
     wide[...] = g_ref[...].astype(jnp.float32) * o_ref[...].astype(jnp.float32)
-    for _, out, side in sides:
+    for out, side in ((keep_rows, core), (give_rows, 1 - core)):
         for j in range(half):
             product = flat[pl.ds(side * half + j, rows, stride=heads), :]
             delta = lax.dot_general(
@@ -114,25 +129,20 @@
                 out[at : at + 1] = delta[:1, n * size : (n + 1) * size]
     count = heads * pieces
     for n, part in enumerate(split_three(give_rows[...])):
-        give_ref[heads * rows + n * count : heads * rows + (n + 1) * count] = part
-
-
-def rows_of(row_ref, qg_ref, rows, size):
-    if row_ref is not None:
-        return row_ref[...]
-    total = qg_ref.shape[0] - qg_ref.shape[0] % rows
-    return join_three(qg_ref, total, (qg_ref.shape[0] - total) // 3)
+        give_q[half * rows + n * count : half * rows + (n + 1) * count] = part
 
 
 def tile(kv_ref, side, grad_ref, gq_in, gq_ref, offset, first):
-    qg_ref, row_ref = side
+    q_ref, g_ref, row_ref = side
     groups = kv_ref.shape[0] // 2
     rows, size = kv_ref.shape[1], kv_ref.shape[2]
     span = gq_ref.shape[1]
     share = span // rows
-    heads = groups * share
     pieces = span // size
-    vectors = rows_of(row_ref, qg_ref, rows, size)
+    if row_ref is None:
+        vectors = join_three(q_ref, g_ref.shape[0], 2 * groups * pieces)
+    else:
+        vectors = row_ref[...]
 
     def vector(at):
         return jnp.concatenate([vectors[at + n : at + n + 1] for n in range(pieces)], 1)
@@ -140,8 +150,8 @@
     for g in range(groups):
         k = kv_ref[g]
         v = kv_ref[groups + g]
-        q = qg_ref[g * span : (g + 1) * span]
-        d = qg_ref[heads * rows + g * span : heads * rows + (g + 1) * span]
+        q = q_ref[g * span : (g + 1) * span]
+        d = g_ref[g * span : (g + 1) * span]
         norm = vector(g * pieces)
         delta = vector((groups + g) * pieces)
         x = dot(k, q, NT) * (query_scale * LOG2E) - norm
@@ -172,43 +182,47 @@
     grad_ref[:groups] = grad_ref[:groups] * query_scale
 
 
-def own_kernel(kv_s, kv_r, qg_s, rows_s, qg_r, gq_s_in, gq_r_in, grad_s, grad_r, gq_s, gq_r):
-    side_s, side_r = (qg_s, rows_s), (qg_r, None)
+def own_side_kernel(kv_s, q_s, g_s, rows_s, grad_s, gq_s):
+    tile(kv_s, (q_s, g_s, rows_s), grad_s, None, gq_s, 0, True)
+
+
+def own_rest_kernel(kv_s, kv_r, q_s, g_s, rows_s, q_r, g_r, grad_s_in, gq_s_in, gq_r_in, grad_s, grad_r, gq_s, gq_r):
+    side_s, side_r = (q_s, g_s, rows_s), (q_r, g_r, None)
     core = lax.axis_index(AXIS) % 2
-    tile(kv_s, side_s, grad_s, gq_s_in, gq_s, 0, True)
+    grad_s[...] = grad_s_in[...]
     tile(kv_r, side_r, grad_r, gq_r_in, gq_r, 0, True)
 
     @pl.when(core == 0)
     def _():
         tile(kv_s, side_r, grad_s, gq_r, gq_r, None, False)
+        gq_s[...] = gq_s_in[...]
 
     @pl.when(core == 1)
     def _():
-        tile(kv_r, side_s, grad_r, gq_s, gq_s, None, False)
+        tile(kv_r, side_s, grad_r, gq_s_in, gq_s, None, False)
 
     scale_keys(grad_s)
     scale_keys(grad_r)
 
 
-def far_kernel(first, kv, qg_s, rows_s, qg_r, *refs):
+def far_kernel(first, kv, q_s, g_s, rows_s, q_r, g_r, *refs):
     if first:
-        out, gq_s, gq_r, grad = refs
-        side_s, side_r, seen_by = (qg_s, rows_s), (qg_r, None), 1
+        gq_s_in, out, gq_s, gq_r, grad = refs
+        gq_r_in, side_s, side_r, seen_by = None, (q_s, g_s, rows_s), (q_r, g_r, None), 1
     else:
         gq_r_in, gq_s_in, out, gq_r, gq_s, grad = refs
-        side_s, side_r, seen_by = (qg_r, None), (qg_s, rows_s), 0
+        side_s, side_r, seen_by = (q_r, g_r, None), (q_s, g_s, rows_s), 0
     device = lax.axis_index(AXIS)
     core = device % 2
     valid = device // 2 >= 2
-    rows = kv.shape[1]
 
     @pl.when(valid)
     def _():
-        tile(kv, side_s, grad, None if first else gq_s_in, gq_s, W, True)
+        tile(kv, side_s, grad, gq_s_in, gq_s, W, True)
 
     @pl.when(valid & (core == seen_by))
     def _():
-        tile(kv, side_r, grad, None if first else gq_r_in, gq_r, None, False)
+        tile(kv, side_r, grad, gq_r_in, gq_r, None, False)
 
     @pl.when(valid)
     def _():
@@ -218,15 +232,15 @@
     @pl.when(jnp.logical_not(valid))
     def _():
         out[...] = jnp.zeros_like(out)
-        gq_s[...] = jnp.zeros_like(gq_s) if first else gq_s_in[...]
+        gq_s[...] = gq_s_in[...]
 
     @pl.when(jnp.logical_not(valid & (core == seen_by)))
     def _():
         gq_r[...] = jnp.zeros_like(gq_r) if first else gq_r_in[...]
 
 
-def near_kernel(kv, qg_s, rows_s, qg_r, gq_s_in, gq_r_in, out, gq_s, gq_r, grad):
-    side_s, side_r = (qg_s, rows_s), (qg_r, None)
+def near_kernel(kv, q_s, g_s, rows_s, q_r, g_r, gq_s_in, gq_r_in, out, gq_s, gq_r, grad):
+    side_s, side_r = (q_s, g_s, rows_s), (q_r, g_r, None)
     valid = lax.axis_index(AXIS) // 2 >= 1
 
     @pl.when(valid)
@@ -243,7 +257,8 @@
         gq_r[...] = gq_r_in[...]
 
 
-def final_q_kernel(own_ref, got_ref, out_ref, wide):
+def final_q_kernel(own_ref, got_ref, out_ref, token_ref, wide):
+    token_ref[...] = jnp.zeros_like(token_ref)
     rows, heads, size = out_ref.shape
     half = heads // 2
     core = lax.axis_index(AXIS) % 2
@@ -257,24 +272,32 @@
     out_ref[...] = wide[...].astype(out_ref.dtype)
 
 
-def final_kv_kernel(own_ref, got_ref, back_s, back_r, side_s, side_r, out_k, out_v, wide):
+def partial_kernel(own_ref, back_ref, side_ref, out_ref):
+    out_ref[...] = own_ref[...] + back_ref[...].astype(jnp.float32) + side_ref[...].astype(jnp.float32)
+
+
+def join_kernel(own_ref, side_ref, after, out_ref):
+    odd = (lax.axis_index(AXIS) // 2) % 2 == 1
+    side = side_ref[...].astype(jnp.float32)
+    out_ref[...] = (own_ref[...] + jnp.where(odd, side, 0.0)).astype(out_ref.dtype)
+
+
+def final_kv_kernel(part_ref, got_ref, back_r, side_r, after, out_k, out_v, wide):
     rows, heads, size = out_k.shape
     half = heads // 2
     device = lax.axis_index(AXIS)
     core = device % 2
     even = jnp.where((device // 2) % 2 == 0, 1.0, 0.0).astype(jnp.float32)
     flat = wide.reshape(rows * 2 * heads, size)
-    for side, base_ref, back_ref, near_ref, share in (
-        (core, own_ref, back_s, side_s, None),
-        (1 - core, got_ref, back_r, side_r, even),
-    ):
-        for part in range(2):
-            for j in range(half):
-                n = part * half + j
-                near = near_ref[n].astype(jnp.float32)
-                near = near if share is None else near * share
-                total = base_ref[n].astype(jnp.float32) + back_ref[n].astype(jnp.float32) + near
-                flat[pl.ds(part * heads + side * half + j, rows, stride=2 * heads), :] = total
+    for part in range(2):
+        for j in range(half):
+            n = part * half + j
+            flat[pl.ds(part * heads + core * half + j, rows, stride=2 * heads), :] = part_ref[n]
+            flat[pl.ds(part * heads + (1 - core) * half + j, rows, stride=2 * heads), :] = (
+                got_ref[n].astype(jnp.float32)
+                + back_r[n].astype(jnp.float32)
+                + side_r[n].astype(jnp.float32) * even
+            )
     out_k[...] = wide[:, :heads, :].astype(out_k.dtype)
     out_v[...] = wide[:, heads:, :].astype(out_v.dtype)
 
@@ -290,7 +313,8 @@
     even = (device // 2) % 2 == 0
 
     def move(x, target):
-        return lax.ppermute(x, AXIS, [(i, target(i)) for i in range(devices)])
+        pairs = [(i, target(i)) for i in range(devices)]
+        return lax.ppermute(x, AXIS, [(i, j) for i, j in pairs if j >= 0])
 
     ahead = lambda i: (i + hops) % devices
     behind = lambda i: (i - hops) % devices
@@ -299,10 +323,9 @@
 
     shape = jax.ShapeDtypeStruct
     kv_block = (groups, rows, size)
-    qg_rows = heads * rows
+    half_rows = heads * rows // 2
     row_block = (heads * rows // size, size)
     gq_block = (groups // 2, heads // groups * rows, size)
-    tile_flops = 10 * rows * rows * size * heads // 2
 
     hbm = pl.BlockSpec(memory_space=pltpu.HBM)
     vmem = pl.BlockSpec(memory_space=pltpu.VMEM)
@@ -324,56 +347,71 @@
     )(pin(key_rows), pin(value_rows))
     kv_r = move(kv_give, sibling)
     two_s = move(kv_s, ahead)
-    one_r = move(kv_r, lambda i: (i + 2) % devices)
     two_r = move(kv_r, ahead)
-    qg_s, rows_s, qg_give = call(
+    q_s, g_s, rows_s, q_give, g_give = call(
         pack_q_kernel,
         "pack_q",
-        [shape((qg_rows, size), low), shape(row_block, f32), shape((qg_rows + 3 * row_block[0], size), low)],
+        [
+            shape((half_rows, size), low),
+            shape((half_rows, size), low),
+            shape(row_block, f32),
+            shape((half_rows + 3 * row_block[0], size), low),
+            shape((half_rows, size), low),
+        ],
         [pltpu.VMEM(queries.shape, low)] * 3
         + [pltpu.VMEM((rows, heads, size), f32), pltpu.VMEM(row_block, f32), pltpu.SemaphoreType.DMA((3,))],
         in_specs=[hbm, hbm, hbm, vmem, anywhere],
     )(pin(queries), pin(grad_output), pin(attn_output), log_norm, kv_r)
-    qg_r = move(qg_give, sibling)
+    q_r, g_r = move(q_give, sibling), move(g_give, sibling)
+    two_s, rows_s = lax.optimization_barrier((two_s, rows_s))
     one_s = move(jnp.where(even, kv_s, two_s), beside)
 
     acc = [shape(gq_block, f32)] * 2
     grad_scratch = [pltpu.VMEM(kv_block, f32)]
-    sides = (qg_s, rows_s, qg_r)
+    sides = (q_s, g_s, rows_s, q_r, g_r)
+    grad_s, gq_s = call(
+        own_side_kernel,
+        "own_side",
+        [shape(kv_block, f32), acc[0]],
+        flops=0,
+    )(kv_s, q_s, g_s, rows_s)
     far_s, gq_s, gq_r = call(
         functools.partial(far_kernel, True),
         "far_s",
         [shape(kv_block, low)] + acc,
         grad_scratch,
-        flops=2 * tile_flops,
-    )(two_s, *sides)
+        flops=0,
+    )(two_s, *sides, gq_s)
     back_s = move(far_s, behind)
-    own_s, own_r, gq_s, gq_r = call(
-        own_kernel, "own", [shape(kv_block, f32)] * 2 + acc, flops=3 * tile_flops
-    )(kv_s, kv_r, *sides, gq_s, gq_r)
-    near = functools.partial(
-        call, near_kernel, out_shape=[shape(kv_block, low)] + acc, scratch=grad_scratch, flops=2 * tile_flops
-    )
-    near_r, gq_s, gq_r = near(name="near_r")(one_r, *sides, gq_s, gq_r)
-    side_r = move(near_r, lambda i: i ^ 3 if i & 2 else i ^ 2)
-    near_s, gq_s, gq_r = near(name="near_s")(one_s, *sides, gq_s, gq_r)
-    side_s = move(near_s, lambda i: (i - 2) % devices)
+    two_r, gq_s, gq_r = lax.optimization_barrier((two_r, gq_s, gq_r))
+    one_r = move(jnp.where(even, kv_r, two_r), beside)
     far_r, gq_s, gq_r = call(
         functools.partial(far_kernel, False),
         "far_r",
         [shape(kv_block, f32)] + acc,
         grad_scratch,
-        flops=2 * tile_flops,
+        flops=0,
     )(two_r, *sides, gq_s, gq_r)
-    side_r, back_s = lax.optimization_barrier((side_r, back_s))
-    joined = (far_r + jnp.where(even, 0.0, side_r.astype(f32))).astype(low)
+    near = functools.partial(
+        call, near_kernel, out_shape=[shape(kv_block, low)] + acc, scratch=grad_scratch, flops=0
+    )
+    near_s, gq_s, gq_r = near(name="near_s")(one_s, *sides, gq_s, gq_r)
+    side_s = move(near_s, lambda i: i - 2)
+    near_r, gq_s, gq_r = near(name="near_r")(one_r, *sides, gq_s, gq_r)
+    side_r = move(near_r, lambda i: i ^ 3 if i & 2 else i ^ 2)
+    gq_s, back_s = lax.optimization_barrier((gq_s, back_s))
+    own_s, own_r, gq_s, gq_r = call(
+        own_rest_kernel, "own_rest", [shape(kv_block, f32)] * 2 + acc, flops=0
+    )(kv_s, kv_r, *sides, grad_s, gq_s, gq_r)
+    part = call(partial_kernel, "partial", shape(kv_block, f32), flops=LONG)(own_s, back_s, side_s)
+    joined = call(join_kernel, "join", shape(kv_block, low), in_specs=[vmem, vmem, anywhere])(far_r, side_r, part)
     back_r = move(joined, lambda i: sibling(behind(i)))
     give = jnp.concatenate([own_r.astype(low), (gq_r * query_scale).astype(low).reshape(-1, rows, size)])
     got = move(give, sibling)
-    grad_q = call(
+    grad_q, token = call(
         final_q_kernel,
         "final_q",
-        shape(queries.shape, low),
+        [shape(queries.shape, low), shape((8, 128), f32)],
         [pltpu.VMEM((rows, heads, size), f32)],
     )(gq_s, got)
     grad_k, grad_v = call(
@@ -381,7 +419,8 @@
         "final_kv",
         [shape(key_rows.shape, low), shape(value_rows.shape, low)],
         [pltpu.VMEM((rows, 2 * groups, size), f32)],
-    )(own_s, got, back_s, back_r, side_s, side_r)
+        in_specs=[vmem] * 4 + [anywhere],
+    )(part, got, back_r, side_r, token)
     return grad_q, grad_k, grad_v
 
 

time: 54.6 us -> 50.4 us (0.923)
  the two profiles are of different devices: /device:TPU:0 before, /device:TPU:3 now
where the time goes in v3:
time: 50.4 us; the launch traced here: 50 us
  waiting for transfers between devices  25.6 us (51%)
  Pallas kernels  13.2 us (26%)
  starting transfers between devices  10.2 us (20%)
  between operations  0.78 us (2%)
    ppermute x12, waiting for transfers between devices, move(): return lax.ppermute(x, AXIS, [(i, j) for i, j in pairs if j >= 0])  25.6 us
    ppermute x12, starting transfers between devices, move(): return lax.ppermute(x, AXIS, [(i, j) for i, j in pairs if j >= 0])  10.2 us
    pallas_call x1, Pallas kernels, shards(): call(pack_q_kernel, 'pack_q', [shape((half_rows, size), low), shape((half...  2.67 us
    pallas_call x1, Pallas kernels, shards(): call(own_rest_kernel, 'own_rest', [shape(kv_block, f32)] * 2 + acc, flops=0)  2.18 us
    pallas_call x1, Pallas kernels, shards(): near_s, gq_s, gq_r = near(name='near_s')(one_s, *sides, gq_s, gq_r)  1.7 us
    pallas_call x1, Pallas kernels, shards(): near_r, gq_s, gq_r = near(name='near_r')(one_r, *sides, gq_s, gq_r)  1.69 us
    pallas_call x1, Pallas kernels, shards(): call(pack_kv_kernel, 'pack_kv', [shape(kv_block, low)] * 2, [pltpu.VMEM(k...  1.27 us
    pallas_call x1, Pallas kernels, shards(): call(final_kv_kernel, 'final_kv', [shape(key_rows.shape, low), shape(valu...  1.26 us
  transfers between devices with their start and end apart: 12, of which 5 were waited for; matrix products, arithmetic and copies ran while one was open for 0% of the time, Pallas kernels for 21%

profile of v3, /device:TPU:3, one launch (start us, length us, event | category | flops | bytes accessed | tf_op | source)
XLA Modules:
  0.0 50.0 jit_solution(1619875213648036637)
XLA Ops:
  0.6 1.3 %pack_kv.1 = (bf16[4,256,128]{2,1,0:T(8,128)(2,1)S(1)}, bf16[4,256,128]{2,1,0:T(8,128)(2,1)S(1)}) custom-call(bf16[256,4,128]{2,1,0:T(4,128)(2,1)} %k_hbm.1, bf16[256,4,128]{2,1,0:T(4,128)(2,1)} %v_hbm.1), custom_call_target="tpu_custom_call" | custom-call | bytes 2097152 | tf_op jit(solution)/shard_map/pack_kv/pallas_call | solution.py:340
  1.9 0.7 %collective-permute-start = (bf16[4,256,128]{2,1,0:T(8,128)(2,1)S(1)}, bf16[4,256,128]{2,1,0:T(8,128)(2,1)S(1)}, u32[]{:S(2)}, u32[]{:S(2)}) collective-permute-start(bf16[4,256,128]{2,1,0:T(8,128)(2,1)S(1)} %get-tuple-element.40), channel_id=1, source_target_pairs={{0,1},{1,0},{2,3},{3,2},{4,5},{5,4},{6,7},{7,6},{8,9},{9,8},{10,11... | collective-permute-start | bytes 786440 | tf_op jit(solution)/shard_map/ppermute | solution.py:317
  2.7 1.2 %collective-permute-start.1 = (bf16[4,256,128]{2,1,0:T(8,128)(2,1)S(1)}, bf16[4,256,128]{2,1,0:T(8,128)(2,1)S(1)}, u32[]{:S(2)}, u32[]{:S(2)}) collective-permute-start(bf16[4,256,128]{2,1,0:T(8,128)(2,1)S(1)} %get-tuple-element.39.kv_s), channel_id=1, source_target_pairs={{0,4},{1,5},{2,6},{3,7},{4,8},{5,9},{6,10},{7,11},{8,12},{9,13},{1... | collective-permute-start | bytes 786440 | tf_op jit(solution)/shard_map/ppermute | solution.py:317
  3.9 0.0 collective-permute-done.after.kv_r
  3.9 2.7 %pack_q.1 = (bf16[1024,128]{1,0:T(8,128)(2,1)S(1)}, bf16[1024,128]{1,0:T(8,128)(2,1)S(1)}, f32[16,128]{1,0:T(8,128)S(1)}, bf16[1072,128]{1,0:T(8,128)(2,1)S(1)}, bf16[1024,128]{1,0:T(8,128)(2,1)S(1)}) custom-call(bf16[256,8,128]{2,1,0:T(8,128)(2,1)} %q_hbm.1, bf16[256,8,128]{2,1,0:T(8,128)(2,1)} %g_hbm.1, bf16[256,8,128]{2,1,0:T(8,128)(2,1)} %o_hbm.1, ...), custom_call_target="tpu_custom_call" | custom-call | bytes 2097152 | tf_op jit(solution)/shard_map/pack_q/pallas_call | solution.py:351
  6.6 0.4 collective-permute-start.2
  7.0 0.2 collective-permute-start.3
  7.2 1.2 %collective-permute-start.4 = (bf16[4,256,128]{2,1,0:T(8,128)(2,1)S(1)}, bf16[4,256,128]{2,1,0:T(8,128)(2,1)S(1)}, u32[]{:S(2)}, u32[]{:S(2)}) collective-permute-start(bf16[4,256,128]{2,1,0:T(8,128)(2,1)S(1)} %collective-permute-done.after.kv_r), channel_id=1, source_target_pairs={{0,4},{1,5},{2,6},{3,7},{4,8},{5,9},{6,10},{7,11},{8,12},{9,13},{1... | collective-permute-start | bytes 786440 | tf_op jit(solution)/shard_map/ppermute | solution.py:317
  8.4 5.1 %collective-permute-done.1.kv = bf16[4,256,128]{2,1,0:T(8,128)(2,1)S(1)} collective-permute-done((bf16[4,256,128]{2,1,0:T(8,128)(2,1)S(1)}, bf16[4,256,128]{2,1,0:T(8,128)(2,1)S(1)}, u32[]{:S(2)}, u32[]{:S(2)}) %collective-permute-start.1) | collective-permute-done | bytes 262176 | tf_op jit(solution)/shard_map/ppermute | solution.py:317
  13.5 0.4 collective-permute-start.6
  13.9 0.9 %own_side.1 = (f32[4,256,128]{2,1,0:T(8,128)S(1)}, f32[2,512,128]{2,1,0:T(8,128)S(1)}) custom-call(bf16[4,256,128]{2,1,0:T(8,128)(2,1)S(1)} %get-tuple-element.39.kv_s, bf16[1024,128]{1,0:T(8,128)(2,1)S(1)} %get-tuple-element.41.q_s, bf16[1024,128]{1,0:T(8,128)(2,1)S(1)} %get-tuple-element.42.g_s, f32[16,128]{1,0:T(8,128)S(1)} %get-tuple-element.44.rows_s), custom_call_target="tpu_custom_call" | custom-call | bytes 2097152 | tf_op jit(solution)/shard_map/own_side/pallas_call | solution.py:372
  14.9 0.0 collective-permute-done.3.g_r
  14.9 0.1 far_s.1
  15.0 4.1 %collective-permute-done.4.kv = bf16[4,256,128]{2,1,0:T(8,128)(2,1)S(1)} collective-permute-done((bf16[4,256,128]{2,1,0:T(8,128)(2,1)S(1)}, bf16[4,256,128]{2,1,0:T(8,128)(2,1)S(1)}, u32[]{:S(2)}, u32[]{:S(2)}) %collective-permute-start.4) | collective-permute-done | bytes 262176 | tf_op jit(solution)/shard_map/ppermute | solution.py:317
  19.1 0.4 collective-permute-start.5
  19.5 1.3 %collective-permute-start.7 = (bf16[4,256,128]{2,1,0:T(8,128)(2,1)S(1)}, bf16[4,256,128]{2,1,0:T(8,128)(2,1)S(1)}, u32[]{:S(2)}, u32[]{:S(2)}) collective-permute-start(bf16[4,256,128]{2,1,0:T(8,128)(2,1)S(1)} %get-tuple-element.60), channel_id=1, source_target_pairs={{0,28},{1,29},{2,30},{3,31},{4,0},{5,1},{6,2},{7,3},{8,4},{9,5},{1... | collective-permute-start | bytes 786440 | tf_op jit(solution)/shard_map/ppermute | solution.py:317
  20.8 0.1 far_r.1
  20.9 1.7 %near_s.1 = (bf16[4,256,128]{2,1,0:T(8,128)(2,1)S(1)}, f32[2,512,128]{2,1,0:T(8,128)S(1)}, f32[2,512,128]{2,1,0:T(8,128)S(1)}) custom-call(bf16[4,256,128]{2,1,0:T(8,128)(2,1)S(1)} %collective-permute-done.6.kv, bf16[1024,128]{1,0:T(8,128)(2,1)S(1)} %get-tuple-element.41.q_s, bf16[1024,128]{1,0:T(8,128)(2,1)S(1)} %get-tuple-element.42.g_s, ...), custom_call_target="tpu_custom_call" | custom-call | bytes 2097152 | tf_op jit(solution)/shard_map/near_s/pallas_call | solution.py:398
  22.6 1.9 %collective-permute-start.9 = (bf16[4,256,128]{2,1,0:T(8,128)(2,1)S(1)}, bf16[4,256,128]{2,1,0:T(8,128)(2,1)S(1)}, u32[]{:S(2)}, u32[]{:S(2)}) collective-permute-start(bf16[4,256,128]{2,1,0:T(8,128)(2,1)S(1)} %get-tuple-element.69), channel_id=1, source_target_pairs={{2,0},{3,1},{4,2},{5,3},{6,4},{7,5},{8,6},{9,7},{10,8},{11,9},{12,... | collective-permute-start | bytes 786440 | tf_op jit(solution)/shard_map/ppermute | solution.py:317
  24.5 1.8 %collective-permute-done.5.kv = bf16[4,256,128]{2,1,0:T(8,128)(2,1)S(1)} collective-permute-done((bf16[4,256,128]{2,1,0:T(8,128)(2,1)S(1)}, bf16[4,256,128]{2,1,0:T(8,128)(2,1)S(1)}, u32[]{:S(2)}, u32[]{:S(2)}) %collective-permute-start.5) | collective-permute-done | bytes 262176 | tf_op jit(solution)/shard_map/ppermute | solution.py:317
  26.3 1.7 %near_r.1 = (bf16[4,256,128]{2,1,0:T(8,128)(2,1)S(1)}, f32[2,512,128]{2,1,0:T(8,128)S(1)}, f32[2,512,128]{2,1,0:T(8,128)S(1)}) custom-call(bf16[4,256,128]{2,1,0:T(8,128)(2,1)S(1)} %collective-permute-done.5.kv, bf16[1024,128]{1,0:T(8,128)(2,1)S(1)} %get-tuple-element.41.q_s, bf16[1024,128]{1,0:T(8,128)(2,1)S(1)} %get-tuple-element.42.g_s, ...), custom_call_target="tpu_custom_call" | custom-call | bytes 2097152 | tf_op jit(solution)/shard_map/near_r/pallas_call | solution.py:400
  28.0 0.8 %collective-permute-start.10 = (bf16[4,256,128]{2,1,0:T(8,128)(2,1)S(1)}, bf16[4,256,128]{2,1,0:T(8,128)(2,1)S(1)}, u32[]{:S(2)}, u32[]{:S(2)}) collective-permute-start(bf16[4,256,128]{2,1,0:T(8,128)(2,1)S(1)} %get-tuple-element.71), channel_id=1, source_target_pairs={{0,2},{1,3},{2,1},{3,0},{4,6},{5,7},{6,5},{7,4},{8,10},{9,11},{10,... | collective-permute-start | bytes 786440 | tf_op jit(solution)/shard_map/ppermute | solution.py:317
  28.9 2.2 %own_rest.1 = (f32[4,256,128]{2,1,0:T(8,128)S(1)}, f32[4,256,128]{2,1,0:T(8,128)S(1)}, f32[2,512,128]{2,1,0:T(8,128)S(1)}, f32[2,512,128]{2,1,0:T(8,128)S(1)}) custom-call(bf16[4,256,128]{2,1,0:T(8,128)(2,1)S(1)} %get-tuple-element.39.kv_s, bf16[4,256,128]{2,1,0:T(8,128)(2,1)S(1)} %collective-permute-done.after.kv_r, ...), custom_call_target="tpu_custom_call" | custom-call | bytes 2097152 | tf_op jit(solution)/shard_map/own_rest/pallas_call | solution.py:403
  31.1 0.1 multiply_convert_fusion
  31.2 0.9 %collective-permute-start.8 = (bf16[8,256,128]{2,1,0:T(8,128)(2,1)S(1)}, bf16[8,256,128]{2,1,0:T(8,128)(2,1)S(1)}, u32[]{:S(2)}, u32[]{:S(2)}) collective-permute-start(bf16[8,256,128]{2,1,0:T(8,128)(2,1)S(1)} %pad_maximum_fusion), channel_id=1, source_target_pairs={{0,1},{1,0},{2,3},{3,2},{4,5},{5,4},{6,7},{7,6},{8,9},{9,8},{10,11... | collective-permute-start | bytes 1572872 | tf_op jit(solution)/shard_map/ppermute | solution.py:317
  32.1 0.1 partial.1.after.part_ref
  32.2 7.9 %collective-permute-done.10.side_ref.side_r = bf16[4,256,128]{2,1,0:T(8,128)(2,1)S(1)} collective-permute-done((bf16[4,256,128]{2,1,0:T(8,128)(2,1)S(1)}, bf16[4,256,128]{2,1,0:T(8,128)(2,1)S(1)}, u32[]{:S(2)}, u32[]{:S(2)}) %collective-permute-start.10) | collective-permute-done | bytes 262176 | tf_op jit(solution)/shard_map/ppermute | solution.py:317
  40.1 0.1 join.1
  40.2 0.7 %collective-permute-start.11 = (bf16[4,256,128]{2,1,0:T(8,128)(2,1)S(1)}, bf16[4,256,128]{2,1,0:T(8,128)(2,1)S(1)}, u32[]{:S(2)}, u32[]{:S(2)}) collective-permute-start(bf16[4,256,128]{2,1,0:T(8,128)(2,1)S(1)} %join.1), channel_id=1, source_target_pairs={{0,29},{1,28},{2,31},{3,30},{4,1},{5,0},{6,3},{7,2},{8,5},{9,4},{1... | collective-permute-start | bytes 786440 | tf_op jit(solution)/shard_map/ppermute | solution.py:317
  40.9 1.1 %final_q.1 = (bf16[256,8,128]{2,1,0:T(8,128)(2,1)}, f32[8,128]{1,0:T(8,128)S(1)}) custom-call(f32[2,512,128]{2,1,0:T(8,128)S(1)} %get-tuple-element.63.own_ref, bf16[8,256,128]{2,1,0:T(8,128)(2,1)S(1)} %collective-permute-done.8.got_ref), custom_call_target="tpu_custom_call" | custom-call | bytes 2097152 | tf_op jit(solution)/shard_map/final_q/pallas_call | solution.py:411
  42.0 6.8 %collective-permute-done.11.back_r = bf16[4,256,128]{2,1,0:T(8,128)(2,1)S(1)} collective-permute-done((bf16[4,256,128]{2,1,0:T(8,128)(2,1)S(1)}, bf16[4,256,128]{2,1,0:T(8,128)(2,1)S(1)}, u32[]{:S(2)}, u32[]{:S(2)}) %collective-permute-start.11) | collective-permute-done | bytes 262176 | tf_op jit(solution)/shard_map/ppermute | solution.py:317
  48.8 1.3 %final_kv.1 = (bf16[256,4,128]{2,1,0:T(4,128)(2,1)}, bf16[256,4,128]{2,1,0:T(4,128)(2,1)}) custom-call(f32[4,256,128]{2,1,0:T(8,128)S(1)} %partial.1.after.part_ref, bf16[8,256,128]{2,1,0:T(8,128)(2,1)S(1)} %collective-permute-done.8.got_ref, bf16[4,256,128]{2,1,0:T(8,128)(2,1)S(1)} %collective-permute-done.11.back_r, ...), custom_call_target="tpu_custom_call" | custom-call | bytes 2097152 | tf_op jit(solution)/shard_map/final_kv/pallas_call | solution.py:417
  (11 shorter events, 0.2 us)
Async XLA Ops:
  0.6 3.3 %copy-start = (f32[8,256]{1,0:T(8,128)S(1)}, f32[8,256]{1,0:T(8,128)}, u32[]{:S(2)}) copy-start(f32[8,256]{1,0:T(8,128)} %norm_ref.1) | copy-start | bytes 24580
  1.9 2.0 %collective-permute-start = (bf16[4,256,128]{2,1,0:T(8,128)(2,1)S(1)}, bf16[4,256,128]{2,1,0:T(8,128)(2,1)S(1)}, u32[]{:S(2)}, u32[]{:S(2)}) collective-permute-start(bf16[4,256,128]{2,1,0:T(8,128)(2,1)S(1)} %get-tuple-element.40), channel_id=1, source_target_pairs={{0,1},{1,0},{2,3},{3,2},{4,5},{5,4},{6,7},{7,6},{8,9},{9,8},{10,11... | collective-permute-start | bytes 786440 | tf_op jit(solution)/shard_map/ppermute | solution.py:317
  2.7 10.8 %collective-permute-start.1 = (bf16[4,256,128]{2,1,0:T(8,128)(2,1)S(1)}, bf16[4,256,128]{2,1,0:T(8,128)(2,1)S(1)}, u32[]{:S(2)}, u32[]{:S(2)}) collective-permute-start(bf16[4,256,128]{2,1,0:T(8,128)(2,1)S(1)} %get-tuple-element.39.kv_s), channel_id=1, source_target_pairs={{0,4},{1,5},{2,6},{3,7},{4,8},{5,9},{6,10},{7,11},{8,12},{9,13},{1... | collective-permute-start | bytes 786440 | tf_op jit(solution)/shard_map/ppermute | solution.py:317
  6.6 8.3 %collective-permute-start.2 = (bf16[1072,128]{1,0:T(8,128)(2,1)S(1)}, bf16[1072,128]{1,0:T(8,128)(2,1)S(1)}, u32[]{:S(2)}, u32[]{:S(2)}) collective-permute-start(bf16[1072,128]{1,0:T(8,128)(2,1)S(1)} %get-tuple-element.45), channel_id=1, source_target_pairs={{0,1},{1,0},{2,3},{3,2},{4,5},{5,4},{6,7},{7,6},{8,9},{9,8},{10,11... | collective-permute-start | bytes 823304 | tf_op jit(solution)/shard_map/ppermute | solution.py:317
  7.0 7.9 %collective-permute-start.3 = (bf16[1024,128]{1,0:T(8,128)(2,1)S(1)}, bf16[1024,128]{1,0:T(8,128)(2,1)S(1)}, u32[]{:S(2)}, u32[]{:S(2)}) collective-permute-start(bf16[1024,128]{1,0:T(8,128)(2,1)S(1)} %get-tuple-element.46), channel_id=1, source_target_pairs={{0,1},{1,0},{2,3},{3,2},{4,5},{5,4},{6,7},{7,6},{8,9},{9,8},{10,11... | collective-permute-start | bytes 786440 | tf_op jit(solution)/shard_map/ppermute | solution.py:317
  7.2 11.9 %collective-permute-start.4 = (bf16[4,256,128]{2,1,0:T(8,128)(2,1)S(1)}, bf16[4,256,128]{2,1,0:T(8,128)(2,1)S(1)}, u32[]{:S(2)}, u32[]{:S(2)}) collective-permute-start(bf16[4,256,128]{2,1,0:T(8,128)(2,1)S(1)} %collective-permute-done.after.kv_r), channel_id=1, source_target_pairs={{0,4},{1,5},{2,6},{3,7},{4,8},{5,9},{6,10},{7,11},{8,12},{9,13},{1... | collective-permute-start | bytes 786440 | tf_op jit(solution)/shard_map/ppermute | solution.py:317
  13.5 7.4 %collective-permute-start.6 = (bf16[4,256,128]{2,1,0:T(8,128)(2,1)S(1)}, bf16[4,256,128]{2,1,0:T(8,128)(2,1)S(1)}, u32[]{:S(2)}, u32[]{:S(2)}) collective-permute-start(bf16[4,256,128]{2,1,0:T(8,128)(2,1)S(1)} %broadcast_select_fusion), channel_id=1, source_target_pairs={{0,2},{1,3},{2,0},{3,1},{4,6},{5,7},{6,4},{7,5},{8,10},{9,11},{10,... | collective-permute-start | bytes 786440 | tf_op jit(solution)/shard_map/ppermute | solution.py:317
  19.1 7.2 %collective-permute-start.5 = (bf16[4,256,128]{2,1,0:T(8,128)(2,1)S(1)}, bf16[4,256,128]{2,1,0:T(8,128)(2,1)S(1)}, u32[]{:S(2)}, u32[]{:S(2)}) collective-permute-start(bf16[4,256,128]{2,1,0:T(8,128)(2,1)S(1)} %broadcast_select_fusion.1), channel_id=1, source_target_pairs={{0,2},{1,3},{2,0},{3,1},{4,6},{5,7},{6,4},{7,5},{8,10},{9,11},{10,... | collective-permute-start | bytes 786440 | tf_op jit(solution)/shard_map/ppermute | solution.py:317
  19.5 9.3 %collective-permute-start.7 = (bf16[4,256,128]{2,1,0:T(8,128)(2,1)S(1)}, bf16[4,256,128]{2,1,0:T(8,128)(2,1)S(1)}, u32[]{:S(2)}, u32[]{:S(2)}) collective-permute-start(bf16[4,256,128]{2,1,0:T(8,128)(2,1)S(1)} %get-tuple-element.60), channel_id=1, source_target_pairs={{0,28},{1,29},{2,30},{3,31},{4,0},{5,1},{6,2},{7,3},{8,4},{9,5},{1... | collective-permute-start | bytes 786440 | tf_op jit(solution)/shard_map/ppermute | solution.py:317
  22.6 9.5 %collective-permute-start.9 = (bf16[4,256,128]{2,1,0:T(8,128)(2,1)S(1)}, bf16[4,256,128]{2,1,0:T(8,128)(2,1)S(1)}, u32[]{:S(2)}, u32[]{:S(2)}) collective-permute-start(bf16[4,256,128]{2,1,0:T(8,128)(2,1)S(1)} %get-tuple-element.69), channel_id=1, source_target_pairs={{2,0},{3,1},{4,2},{5,3},{6,4},{7,5},{8,6},{9,7},{10,8},{11,9},{12,... | collective-permute-start | bytes 786440 | tf_op jit(solution)/shard_map/ppermute | solution.py:317
  28.0 12.1 %collective-permute-start.10 = (bf16[4,256,128]{2,1,0:T(8,128)(2,1)S(1)}, bf16[4,256,128]{2,1,0:T(8,128)(2,1)S(1)}, u32[]{:S(2)}, u32[]{:S(2)}) collective-permute-start(bf16[4,256,128]{2,1,0:T(8,128)(2,1)S(1)} %get-tuple-element.71), channel_id=1, source_target_pairs={{0,2},{1,3},{2,1},{3,0},{4,6},{5,7},{6,5},{7,4},{8,10},{9,11},{10,... | collective-permute-start | bytes 786440 | tf_op jit(solution)/shard_map/ppermute | solution.py:317
  31.2 9.7 %collective-permute-start.8 = (bf16[8,256,128]{2,1,0:T(8,128)(2,1)S(1)}, bf16[8,256,128]{2,1,0:T(8,128)(2,1)S(1)}, u32[]{:S(2)}, u32[]{:S(2)}) collective-permute-start(bf16[8,256,128]{2,1,0:T(8,128)(2,1)S(1)} %pad_maximum_fusion), channel_id=1, source_target_pairs={{0,1},{1,0},{2,3},{3,2},{4,5},{5,4},{6,7},{7,6},{8,9},{9,8},{10,11... | collective-permute-start | bytes 1572872 | tf_op jit(solution)/shard_map/ppermute | solution.py:317
  40.2 8.6 %collective-permute-start.11 = (bf16[4,256,128]{2,1,0:T(8,128)(2,1)S(1)}, bf16[4,256,128]{2,1,0:T(8,128)(2,1)S(1)}, u32[]{:S(2)}, u32[]{:S(2)}) collective-permute-start(bf16[4,256,128]{2,1,0:T(8,128)(2,1)S(1)} %join.1), channel_id=1, source_target_pairs={{0,29},{1,28},{2,31},{3,30},{4,1},{5,0},{6,3},{7,2},{8,5},{9,4},{1... | collective-permute-start | bytes 786440 | tf_op jit(solution)/shard_map/ppermute | solution.py:317

commit v4 on v3

--- a/solution.py
+++ b/solution.py
@@ -14,7 +14,7 @@
 LOG2E = math.log2(math.e)
 AXIS = "seq"
 VMEM_LIMIT = 16 * 1024 * 1024
-LONG = 10**9
+LONG = 10**10
 
 NT = (((1,), (1,)), ((), ()))
 NN = (((1,), (0,)), ((), ()))
@@ -186,11 +186,11 @@
     tile(kv_s, (q_s, g_s, rows_s), grad_s, None, gq_s, 0, True)
 
 
-def own_rest_kernel(kv_s, kv_r, q_s, g_s, rows_s, q_r, g_r, grad_s_in, gq_s_in, gq_r_in, grad_s, grad_r, gq_s, gq_r):
+def own_rest_kernel(kv_s, kv_r, q_s, g_s, rows_s, q_r, g_r, grad_s_in, gq_s_in, grad_s, grad_r, gq_s, gq_r):
     side_s, side_r = (q_s, g_s, rows_s), (q_r, g_r, None)
     core = lax.axis_index(AXIS) % 2
     grad_s[...] = grad_s_in[...]
-    tile(kv_r, side_r, grad_r, gq_r_in, gq_r, 0, True)
+    tile(kv_r, side_r, grad_r, None, gq_r, 0, True)
 
     @pl.when(core == 0)
     def _():
@@ -207,8 +207,8 @@
 
 def far_kernel(first, kv, q_s, g_s, rows_s, q_r, g_r, *refs):
     if first:
-        gq_s_in, out, gq_s, gq_r, grad = refs
-        gq_r_in, side_s, side_r, seen_by = None, (q_s, g_s, rows_s), (q_r, g_r, None), 1
+        gq_s_in, gq_r_in, out, gq_s, gq_r, grad = refs
+        side_s, side_r, seen_by = (q_s, g_s, rows_s), (q_r, g_r, None), 1
     else:
         gq_r_in, gq_s_in, out, gq_r, gq_s, grad = refs
         side_s, side_r, seen_by = (q_r, g_r, None), (q_s, g_s, rows_s), 0
@@ -236,7 +236,7 @@
 
     @pl.when(jnp.logical_not(valid & (core == seen_by)))
     def _():
-        gq_r[...] = jnp.zeros_like(gq_r) if first else gq_r_in[...]
+        gq_r[...] = gq_r_in[...]
 
 
 def near_kernel(kv, q_s, g_s, rows_s, q_r, g_r, gq_s_in, gq_r_in, out, gq_s, gq_r, grad):
@@ -257,7 +257,7 @@
         gq_r[...] = gq_r_in[...]
 
 
-def final_q_kernel(own_ref, got_ref, out_ref, token_ref, wide):
+def final_q_kernel(own_ref, got_ref, after, out_ref, token_ref, wide):
     token_ref[...] = jnp.zeros_like(token_ref)
     rows, heads, size = out_ref.shape
     half = heads // 2
@@ -276,18 +276,10 @@
     out_ref[...] = own_ref[...] + back_ref[...].astype(jnp.float32) + side_ref[...].astype(jnp.float32)
 
 
-def join_kernel(own_ref, side_ref, after, out_ref):
-    odd = (lax.axis_index(AXIS) // 2) % 2 == 1
-    side = side_ref[...].astype(jnp.float32)
-    out_ref[...] = (own_ref[...] + jnp.where(odd, side, 0.0)).astype(out_ref.dtype)
-
-
 def final_kv_kernel(part_ref, got_ref, back_r, side_r, after, out_k, out_v, wide):
     rows, heads, size = out_k.shape
     half = heads // 2
-    device = lax.axis_index(AXIS)
-    core = device % 2
-    even = jnp.where((device // 2) % 2 == 0, 1.0, 0.0).astype(jnp.float32)
+    core = lax.axis_index(AXIS) % 2
     flat = wide.reshape(rows * 2 * heads, size)
     for part in range(2):
         for j in range(half):
@@ -296,7 +288,7 @@
             flat[pl.ds(part * heads + (1 - core) * half + j, rows, stride=2 * heads), :] = (
                 got_ref[n].astype(jnp.float32)
                 + back_r[n].astype(jnp.float32)
-                + side_r[n].astype(jnp.float32) * even
+                + side_r[n].astype(jnp.float32)
             )
     out_k[...] = wide[:, :heads, :].astype(out_k.dtype)
     out_v[...] = wide[:, heads:, :].astype(out_v.dtype)
@@ -363,49 +355,38 @@
         in_specs=[hbm, hbm, hbm, vmem, anywhere],
     )(pin(queries), pin(grad_output), pin(attn_output), log_norm, kv_r)
     q_r, g_r = move(q_give, sibling), move(g_give, sibling)
+    acc = [shape(gq_block, f32)] * 2
+    grad_scratch = [pltpu.VMEM(kv_block, f32)]
     two_s, rows_s = lax.optimization_barrier((two_s, rows_s))
     one_s = move(jnp.where(even, kv_s, two_s), beside)
-
-    acc = [shape(gq_block, f32)] * 2
-    grad_scratch = [pltpu.VMEM(kv_block, f32)]
     sides = (q_s, g_s, rows_s, q_r, g_r)
-    grad_s, gq_s = call(
-        own_side_kernel,
-        "own_side",
-        [shape(kv_block, f32), acc[0]],
-        flops=0,
-    )(kv_s, q_s, g_s, rows_s)
+    grad_s, gq_s = call(own_side_kernel, "own_side", [shape(kv_block, f32), acc[0]], flops=0)(
+        kv_s, q_s, g_s, rows_s
+    )
+    own_s, own_r, gq_s, gq_r = call(own_rest_kernel, "own_rest", [shape(kv_block, f32)] * 2 + acc, flops=0)(
+        kv_s, kv_r, *sides, grad_s, gq_s
+    )
     far_s, gq_s, gq_r = call(
-        functools.partial(far_kernel, True),
-        "far_s",
-        [shape(kv_block, low)] + acc,
-        grad_scratch,
-        flops=0,
-    )(two_s, *sides, gq_s)
+        functools.partial(far_kernel, True), "far_s", [shape(kv_block, low)] + acc, grad_scratch
+    )(two_s, *sides, gq_s, gq_r)
     back_s = move(far_s, behind)
     two_r, gq_s, gq_r = lax.optimization_barrier((two_r, gq_s, gq_r))
     one_r = move(jnp.where(even, kv_r, two_r), beside)
     far_r, gq_s, gq_r = call(
         functools.partial(far_kernel, False),
         "far_r",
-        [shape(kv_block, f32)] + acc,
+        [shape(kv_block, low)] + acc,
         grad_scratch,
-        flops=0,
     )(two_r, *sides, gq_s, gq_r)
-    near = functools.partial(
-        call, near_kernel, out_shape=[shape(kv_block, low)] + acc, scratch=grad_scratch, flops=0
-    )
+    back_r = move(far_r, lambda i: sibling(behind(i)))
+    near = functools.partial(call, near_kernel, out_shape=[shape(kv_block, low)] + acc, scratch=grad_scratch)
     near_s, gq_s, gq_r = near(name="near_s")(one_s, *sides, gq_s, gq_r)
     side_s = move(near_s, lambda i: i - 2)
+    one_r, back_s = lax.optimization_barrier((one_r, back_s))
     near_r, gq_s, gq_r = near(name="near_r")(one_r, *sides, gq_s, gq_r)
-    side_r = move(near_r, lambda i: i ^ 3 if i & 2 else i ^ 2)
-    gq_s, back_s = lax.optimization_barrier((gq_s, back_s))
-    own_s, own_r, gq_s, gq_r = call(
-        own_rest_kernel, "own_rest", [shape(kv_block, f32)] * 2 + acc, flops=0
-    )(kv_s, kv_r, *sides, grad_s, gq_s, gq_r)
+    side_r = move(near_r, lambda i: sibling(i - 2) if i >= 2 else -1)
+
     part = call(partial_kernel, "partial", shape(kv_block, f32), flops=LONG)(own_s, back_s, side_s)
-    joined = call(join_kernel, "join", shape(kv_block, low), in_specs=[vmem, vmem, anywhere])(far_r, side_r, part)
-    back_r = move(joined, lambda i: sibling(behind(i)))
     give = jnp.concatenate([own_r.astype(low), (gq_r * query_scale).astype(low).reshape(-1, rows, size)])
     got = move(give, sibling)
     grad_q, token = call(
@@ -413,7 +394,8 @@
         "final_q",
         [shape(queries.shape, low), shape((8, 128), f32)],
         [pltpu.VMEM((rows, heads, size), f32)],
-    )(gq_s, got)
+        in_specs=[vmem, vmem, anywhere],
+    )(gq_s, got, part)
     grad_k, grad_v = call(
         final_kv_kernel,
         "final_kv",

time: 50.4 us -> 47.1 us (0.935)
  waiting for transfers between devices: 25.6 us -> 17.3 us
  starting transfers between devices: 10.2 us -> 15.6 us
    ppermute x12, waiting for transfers between devices: 25.6 us -> 17.3 us  [move(): return lax.ppermute(x, AXIS, [(i, j) for i, j in pairs if j >= 0])]
    ppermute x12, starting transfers between devices: 10.2 us -> 15.6 us  [move(): return lax.ppermute(x, AXIS, [(i, j) for i, j in pairs if j >= 0])]
  transfers between devices with their start and end apart: 12 -> 12, of which waited for: 5 -> 3; matrix products, arithmetic and copies ran while one was open for 0% -> 0% of each run, Pallas kernels for 21% -> 22%
where the time goes in v4:
time: 47.1 us; the launch traced here: 46.9 us
  waiting for transfers between devices  17.3 us (37%)
  starting transfers between devices  15.6 us (33%)
  Pallas kernels  13 us (28%)
  between operations  0.81 us (2%)
    ppermute x12, waiting for transfers between devices, move(): return lax.ppermute(x, AXIS, [(i, j) for i, j in pairs if j >= 0])  17.3 us
    ppermute x12, starting transfers between devices, move(): return lax.ppermute(x, AXIS, [(i, j) for i, j in pairs if j >= 0])  15.6 us
    pallas_call x1, Pallas kernels, shards(): call(pack_q_kernel, 'pack_q', [shape((half_rows, size), low), shape((half...  2.67 us
    pallas_call x1, Pallas kernels, shards(): call(own_rest_kernel, 'own_rest', [shape(kv_block, f32)] * 2 + acc, flops=0)  2.02 us
    pallas_call x1, Pallas kernels, shards(): near_s, gq_s, gq_r = near(name='near_s')(one_s, *sides, gq_s, gq_r)  1.7 us
    pallas_call x1, Pallas kernels, shards(): near_r, gq_s, gq_r = near(name='near_r')(one_r, *sides, gq_s, gq_r)  1.69 us
    pallas_call x1, Pallas kernels, shards(): call(pack_kv_kernel, 'pack_kv', [shape(kv_block, low)] * 2, [pltpu.VMEM(k...  1.27 us
    pallas_call x1, Pallas kernels, shards(): call(final_kv_kernel, 'final_kv', [shape(key_rows.shape, low), shape(valu...  1.24 us
  transfers between devices with their start and end apart: 12, of which 3 were waited for; matrix products, arithmetic and copies ran while one was open for 0% of the time, Pallas kernels for 22%

profile of v4, /device:TPU:3, one launch (start us, length us, event | category | flops | bytes accessed | tf_op | source)
XLA Modules:
  0.0 46.9 jit_solution(8781618576919745920)
XLA Ops:
  0.6 1.3 %pack_kv.1 = (bf16[4,256,128]{2,1,0:T(8,128)(2,1)S(1)}, bf16[4,256,128]{2,1,0:T(8,128)(2,1)S(1)}) custom-call(bf16[256,4,128]{2,1,0:T(4,128)(2,1)} %k_hbm.1, bf16[256,4,128]{2,1,0:T(4,128)(2,1)} %v_hbm.1), custom_call_target="tpu_custom_call" | custom-call | bytes 2097152 | tf_op jit(solution)/shard_map/pack_kv/pallas_call | solution.py:332
  1.9 0.7 %collective-permute-start = (bf16[4,256,128]{2,1,0:T(8,128)(2,1)S(1)}, bf16[4,256,128]{2,1,0:T(8,128)(2,1)S(1)}, u32[]{:S(2)}, u32[]{:S(2)}) collective-permute-start(bf16[4,256,128]{2,1,0:T(8,128)(2,1)S(1)} %get-tuple-element.39), channel_id=1, source_target_pairs={{0,1},{1,0},{2,3},{3,2},{4,5},{5,4},{6,7},{7,6},{8,9},{9,8},{10,11... | collective-permute-start | bytes 786440 | tf_op jit(solution)/shard_map/ppermute | solution.py:309
  2.7 1.2 %collective-permute-start.2 = (bf16[4,256,128]{2,1,0:T(8,128)(2,1)S(1)}, bf16[4,256,128]{2,1,0:T(8,128)(2,1)S(1)}, u32[]{:S(2)}, u32[]{:S(2)}) collective-permute-start(bf16[4,256,128]{2,1,0:T(8,128)(2,1)S(1)} %get-tuple-element.40.kv_s), channel_id=1, source_target_pairs={{0,4},{1,5},{2,6},{3,7},{4,8},{5,9},{6,10},{7,11},{8,12},{9,13},{1... | collective-permute-start | bytes 786440 | tf_op jit(solution)/shard_map/ppermute | solution.py:309
  3.9 0.0 collective-permute-done.after.kv_r
  3.9 2.7 %pack_q.1 = (bf16[1024,128]{1,0:T(8,128)(2,1)S(1)}, bf16[1024,128]{1,0:T(8,128)(2,1)S(1)}, f32[16,128]{1,0:T(8,128)S(1)}, bf16[1072,128]{1,0:T(8,128)(2,1)S(1)}, bf16[1024,128]{1,0:T(8,128)(2,1)S(1)}) custom-call(bf16[256,8,128]{2,1,0:T(8,128)(2,1)} %q_hbm.1, bf16[256,8,128]{2,1,0:T(8,128)(2,1)} %g_hbm.1, bf16[256,8,128]{2,1,0:T(8,128)(2,1)} %o_hbm.1, ...), custom_call_target="tpu_custom_call" | custom-call | bytes 2097152 | tf_op jit(solution)/shard_map/pack_q/pallas_call | solution.py:343
  6.6 0.4 collective-permute-start.3
  7.0 0.2 collective-permute-start.4
  7.2 1.2 %collective-permute-start.1 = (bf16[4,256,128]{2,1,0:T(8,128)(2,1)S(1)}, bf16[4,256,128]{2,1,0:T(8,128)(2,1)S(1)}, u32[]{:S(2)}, u32[]{:S(2)}) collective-permute-start(bf16[4,256,128]{2,1,0:T(8,128)(2,1)S(1)} %collective-permute-done.after.kv_r), channel_id=1, source_target_pairs={{0,4},{1,5},{2,6},{3,7},{4,8},{5,9},{6,10},{7,11},{8,12},{9,13},{1... | collective-permute-start | bytes 786440 | tf_op jit(solution)/shard_map/ppermute | solution.py:309
  8.4 5.1 %collective-permute-done.2.kv = bf16[4,256,128]{2,1,0:T(8,128)(2,1)S(1)} collective-permute-done((bf16[4,256,128]{2,1,0:T(8,128)(2,1)S(1)}, bf16[4,256,128]{2,1,0:T(8,128)(2,1)S(1)}, u32[]{:S(2)}, u32[]{:S(2)}) %collective-permute-start.2) | collective-permute-done | bytes 262176 | tf_op jit(solution)/shard_map/ppermute | solution.py:309
  13.5 0.4 collective-permute-start.7
  13.9 0.9 %own_side.1 = (f32[4,256,128]{2,1,0:T(8,128)S(1)}, f32[2,512,128]{2,1,0:T(8,128)S(1)}) custom-call(bf16[4,256,128]{2,1,0:T(8,128)(2,1)S(1)} %get-tuple-element.40.kv_s, bf16[1024,128]{1,0:T(8,128)(2,1)S(1)} %get-tuple-element.43.q_s, bf16[1024,128]{1,0:T(8,128)(2,1)S(1)} %get-tuple-element.44.g_s, f32[16,128]{1,0:T(8,128)S(1)} %get-tuple-element.45.rows_s), custom_call_target="tpu_custom_call" | custom-call | bytes 2097152 | tf_op jit(solution)/shard_map/own_side/pallas_call | solution.py:363
  14.9 0.0 collective-permute-done.4.g_r
  14.9 0.0 collective-permute-done.3.q_r
  14.9 2.0 %own_rest.1 = (f32[4,256,128]{2,1,0:T(8,128)S(1)}, f32[4,256,128]{2,1,0:T(8,128)S(1)}, f32[2,512,128]{2,1,0:T(8,128)S(1)}, f32[2,512,128]{2,1,0:T(8,128)S(1)}) custom-call(bf16[4,256,128]{2,1,0:T(8,128)(2,1)S(1)} %get-tuple-element.40.kv_s, bf16[4,256,128]{2,1,0:T(8,128)(2,1)S(1)} %collective-permute-done.after.kv_r, ...), custom_call_target="tpu_custom_call" | custom-call | bytes 2097152 | tf_op jit(solution)/shard_map/own_rest/pallas_call | solution.py:366
  16.9 0.1 far_s.1
  17.0 2.1 %collective-permute-done.1.kv = bf16[4,256,128]{2,1,0:T(8,128)(2,1)S(1)} collective-permute-done((bf16[4,256,128]{2,1,0:T(8,128)(2,1)S(1)}, bf16[4,256,128]{2,1,0:T(8,128)(2,1)S(1)}, u32[]{:S(2)}, u32[]{:S(2)}) %collective-permute-start.1) | collective-permute-done | bytes 262176 | tf_op jit(solution)/shard_map/ppermute | solution.py:309
  19.1 0.4 collective-permute-start.5
  19.5 2.0 %collective-permute-start.6 = (bf16[4,256,128]{2,1,0:T(8,128)(2,1)S(1)}, bf16[4,256,128]{2,1,0:T(8,128)(2,1)S(1)}, u32[]{:S(2)}, u32[]{:S(2)}) collective-permute-start(bf16[4,256,128]{2,1,0:T(8,128)(2,1)S(1)} %get-tuple-element.55), channel_id=1, source_target_pairs={{0,28},{1,29},{2,30},{3,31},{4,0},{5,1},{6,2},{7,3},{8,4},{9,5},{1... | collective-permute-start | bytes 786440 | tf_op jit(solution)/shard_map/ppermute | solution.py:309
  21.5 0.1 far_r.1
  21.7 0.0 collective-permute-done.7.kv
  21.7 1.7 %near_s.1 = (bf16[4,256,128]{2,1,0:T(8,128)(2,1)S(1)}, f32[2,512,128]{2,1,0:T(8,128)S(1)}, f32[2,512,128]{2,1,0:T(8,128)S(1)}) custom-call(bf16[4,256,128]{2,1,0:T(8,128)(2,1)S(1)} %collective-permute-done.7.kv, bf16[1024,128]{1,0:T(8,128)(2,1)S(1)} %get-tuple-element.43.q_s, bf16[1024,128]{1,0:T(8,128)(2,1)S(1)} %get-tuple-element.44.g_s, ...), custom_call_target="tpu_custom_call" | custom-call | bytes 2097152 | tf_op jit(solution)/shard_map/near_s/pallas_call | solution.py:383
  23.4 1.9 %collective-permute-start.9 = (bf16[4,256,128]{2,1,0:T(8,128)(2,1)S(1)}, bf16[4,256,128]{2,1,0:T(8,128)(2,1)S(1)}, u32[]{:S(2)}, u32[]{:S(2)}) collective-permute-start(bf16[4,256,128]{2,1,0:T(8,128)(2,1)S(1)} %get-tuple-element.68), channel_id=1, source_target_pairs={{2,0},{3,1},{4,2},{5,3},{6,4},{7,5},{8,6},{9,7},{10,8},{11,9},{12,... | collective-permute-start | bytes 786440 | tf_op jit(solution)/shard_map/ppermute | solution.py:309
  25.3 5.1 %collective-permute-start.10 = (bf16[4,256,128]{2,1,0:T(8,128)(2,1)S(1)}, bf16[4,256,128]{2,1,0:T(8,128)(2,1)S(1)}, u32[]{:S(2)}, u32[]{:S(2)}) collective-permute-start(bf16[4,256,128]{2,1,0:T(8,128)(2,1)S(1)} %get-tuple-element.70), channel_id=1, source_target_pairs={{0,29},{1,28},{2,31},{3,30},{4,1},{5,0},{6,3},{7,2},{8,5},{9,4},{1... | collective-permute-start | bytes 786440 | tf_op jit(solution)/shard_map/ppermute | solution.py:309
  30.4 0.0 collective-permute-done.5.kv
  30.4 1.7 %near_r.1 = (bf16[4,256,128]{2,1,0:T(8,128)(2,1)S(1)}, f32[2,512,128]{2,1,0:T(8,128)S(1)}, f32[2,512,128]{2,1,0:T(8,128)S(1)}) custom-call(bf16[4,256,128]{2,1,0:T(8,128)(2,1)S(1)} %collective-permute-done.5.kv, bf16[1024,128]{1,0:T(8,128)(2,1)S(1)} %get-tuple-element.43.q_s, bf16[1024,128]{1,0:T(8,128)(2,1)S(1)} %get-tuple-element.44.g_s, ...), custom_call_target="tpu_custom_call" | custom-call | bytes 2097152 | tf_op jit(solution)/shard_map/near_r/pallas_call | solution.py:386
  32.1 0.1 multiply_convert_fusion
  32.3 0.1 collective-permute-start.8
  32.4 1.9 %collective-permute-start.11 = (bf16[4,256,128]{2,1,0:T(8,128)(2,1)S(1)}, bf16[4,256,128]{2,1,0:T(8,128)(2,1)S(1)}, u32[]{:S(2)}, u32[]{:S(2)}) collective-permute-start(bf16[4,256,128]{2,1,0:T(8,128)(2,1)S(1)} %get-tuple-element.71), channel_id=1, source_target_pairs={{2,1},{3,0},{4,3},{5,2},{6,5},{7,4},{8,7},{9,6},{10,9},{11,8},{12,... | collective-permute-start | bytes 786440 | tf_op jit(solution)/shard_map/ppermute | solution.py:309
  34.3 0.1 partial.1.after.part_ref
  34.4 1.1 %final_q.1 = (bf16[256,8,128]{2,1,0:T(8,128)(2,1)}, f32[8,128]{1,0:T(8,128)S(1)}) custom-call(f32[2,512,128]{2,1,0:T(8,128)S(1)} %get-tuple-element.63.own_ref, bf16[8,256,128]{2,1,0:T(8,128)(2,1)S(1)} %collective-permute-done.8.got_ref, f32[4,256,128]{2,1,0:T(8,128)S(1)} %partial.1.after.part_ref), custom_call_target="tpu_custom_call" | custom-call | bytes 2097152 | tf_op jit(solution)/shard_map/final_q/pallas_call | solution.py:392
  35.5 10.2 %collective-permute-done.10.back_r = bf16[4,256,128]{2,1,0:T(8,128)(2,1)S(1)} collective-permute-done((bf16[4,256,128]{2,1,0:T(8,128)(2,1)S(1)}, bf16[4,256,128]{2,1,0:T(8,128)(2,1)S(1)}, u32[]{:S(2)}, u32[]{:S(2)}) %collective-permute-start.10) | collective-permute-done | bytes 262176 | tf_op jit(solution)/shard_map/ppermute | solution.py:309
  45.7 1.2 %final_kv.1 = (bf16[256,4,128]{2,1,0:T(4,128)(2,1)}, bf16[256,4,128]{2,1,0:T(4,128)(2,1)}) custom-call(f32[4,256,128]{2,1,0:T(8,128)S(1)} %partial.1.after.part_ref, bf16[8,256,128]{2,1,0:T(8,128)(2,1)S(1)} %collective-permute-done.8.got_ref, bf16[4,256,128]{2,1,0:T(8,128)(2,1)S(1)} %collective-permute-done.10.back_r, ...), custom_call_target="tpu_custom_call" | custom-call | bytes 2097152 | tf_op jit(solution)/shard_map/final_kv/pallas_call | solution.py:399
  (10 shorter events, 0.2 us)
Async XLA Ops:
  0.6 3.3 %copy-start = (f32[8,256]{1,0:T(8,128)S(1)}, f32[8,256]{1,0:T(8,128)}, u32[]{:S(2)}) copy-start(f32[8,256]{1,0:T(8,128)} %norm_ref.1) | copy-start | bytes 24580
  1.9 2.0 %collective-permute-start = (bf16[4,256,128]{2,1,0:T(8,128)(2,1)S(1)}, bf16[4,256,128]{2,1,0:T(8,128)(2,1)S(1)}, u32[]{:S(2)}, u32[]{:S(2)}) collective-permute-start(bf16[4,256,128]{2,1,0:T(8,128)(2,1)S(1)} %get-tuple-element.39), channel_id=1, source_target_pairs={{0,1},{1,0},{2,3},{3,2},{4,5},{5,4},{6,7},{7,6},{8,9},{9,8},{10,11... | collective-permute-start | bytes 786440 | tf_op jit(solution)/shard_map/ppermute | solution.py:309
  2.7 10.8 %collective-permute-start.2 = (bf16[4,256,128]{2,1,0:T(8,128)(2,1)S(1)}, bf16[4,256,128]{2,1,0:T(8,128)(2,1)S(1)}, u32[]{:S(2)}, u32[]{:S(2)}) collective-permute-start(bf16[4,256,128]{2,1,0:T(8,128)(2,1)S(1)} %get-tuple-element.40.kv_s), channel_id=1, source_target_pairs={{0,4},{1,5},{2,6},{3,7},{4,8},{5,9},{6,10},{7,11},{8,12},{9,13},{1... | collective-permute-start | bytes 786440 | tf_op jit(solution)/shard_map/ppermute | solution.py:309
  6.6 8.3 %collective-permute-start.3 = (bf16[1072,128]{1,0:T(8,128)(2,1)S(1)}, bf16[1072,128]{1,0:T(8,128)(2,1)S(1)}, u32[]{:S(2)}, u32[]{:S(2)}) collective-permute-start(bf16[1072,128]{1,0:T(8,128)(2,1)S(1)} %get-tuple-element.46), channel_id=1, source_target_pairs={{0,1},{1,0},{2,3},{3,2},{4,5},{5,4},{6,7},{7,6},{8,9},{9,8},{10,11... | collective-permute-start | bytes 823304 | tf_op jit(solution)/shard_map/ppermute | solution.py:309
  7.0 7.9 %collective-permute-start.4 = (bf16[1024,128]{1,0:T(8,128)(2,1)S(1)}, bf16[1024,128]{1,0:T(8,128)(2,1)S(1)}, u32[]{:S(2)}, u32[]{:S(2)}) collective-permute-start(bf16[1024,128]{1,0:T(8,128)(2,1)S(1)} %get-tuple-element.47), channel_id=1, source_target_pairs={{0,1},{1,0},{2,3},{3,2},{4,5},{5,4},{6,7},{7,6},{8,9},{9,8},{10,11... | collective-permute-start | bytes 786440 | tf_op jit(solution)/shard_map/ppermute | solution.py:309
  7.2 11.9 %collective-permute-start.1 = (bf16[4,256,128]{2,1,0:T(8,128)(2,1)S(1)}, bf16[4,256,128]{2,1,0:T(8,128)(2,1)S(1)}, u32[]{:S(2)}, u32[]{:S(2)}) collective-permute-start(bf16[4,256,128]{2,1,0:T(8,128)(2,1)S(1)} %collective-permute-done.after.kv_r), channel_id=1, source_target_pairs={{0,4},{1,5},{2,6},{3,7},{4,8},{5,9},{6,10},{7,11},{8,12},{9,13},{1... | collective-permute-start | bytes 786440 | tf_op jit(solution)/shard_map/ppermute | solution.py:309
  13.5 8.2 %collective-permute-start.7 = (bf16[4,256,128]{2,1,0:T(8,128)(2,1)S(1)}, bf16[4,256,128]{2,1,0:T(8,128)(2,1)S(1)}, u32[]{:S(2)}, u32[]{:S(2)}) collective-permute-start(bf16[4,256,128]{2,1,0:T(8,128)(2,1)S(1)} %broadcast_select_fusion), channel_id=1, source_target_pairs={{0,2},{1,3},{2,0},{3,1},{4,6},{5,7},{6,4},{7,5},{8,10},{9,11},{10,... | collective-permute-start | bytes 786440 | tf_op jit(solution)/shard_map/ppermute | solution.py:309
  19.1 11.3 %collective-permute-start.5 = (bf16[4,256,128]{2,1,0:T(8,128)(2,1)S(1)}, bf16[4,256,128]{2,1,0:T(8,128)(2,1)S(1)}, u32[]{:S(2)}, u32[]{:S(2)}) collective-permute-start(bf16[4,256,128]{2,1,0:T(8,128)(2,1)S(1)} %broadcast_select_fusion.1), channel_id=1, source_target_pairs={{0,2},{1,3},{2,0},{3,1},{4,6},{5,7},{6,4},{7,5},{8,10},{9,11},{10,... | collective-permute-start | bytes 786440 | tf_op jit(solution)/shard_map/ppermute | solution.py:309
  19.5 10.9 %collective-permute-start.6 = (bf16[4,256,128]{2,1,0:T(8,128)(2,1)S(1)}, bf16[4,256,128]{2,1,0:T(8,128)(2,1)S(1)}, u32[]{:S(2)}, u32[]{:S(2)}) collective-permute-start(bf16[4,256,128]{2,1,0:T(8,128)(2,1)S(1)} %get-tuple-element.55), channel_id=1, source_target_pairs={{0,28},{1,29},{2,30},{3,31},{4,0},{5,1},{6,2},{7,3},{8,4},{9,5},{1... | collective-permute-start | bytes 786440 | tf_op jit(solution)/shard_map/ppermute | solution.py:309
  23.4 10.9 %collective-permute-start.9 = (bf16[4,256,128]{2,1,0:T(8,128)(2,1)S(1)}, bf16[4,256,128]{2,1,0:T(8,128)(2,1)S(1)}, u32[]{:S(2)}, u32[]{:S(2)}) collective-permute-start(bf16[4,256,128]{2,1,0:T(8,128)(2,1)S(1)} %get-tuple-element.68), channel_id=1, source_target_pairs={{2,0},{3,1},{4,2},{5,3},{6,4},{7,5},{8,6},{9,7},{10,8},{11,9},{12,... | collective-permute-start | bytes 786440 | tf_op jit(solution)/shard_map/ppermute | solution.py:309
  25.3 20.3 %collective-permute-start.10 = (bf16[4,256,128]{2,1,0:T(8,128)(2,1)S(1)}, bf16[4,256,128]{2,1,0:T(8,128)(2,1)S(1)}, u32[]{:S(2)}, u32[]{:S(2)}) collective-permute-start(bf16[4,256,128]{2,1,0:T(8,128)(2,1)S(1)} %get-tuple-element.70), channel_id=1, source_target_pairs={{0,29},{1,28},{2,31},{3,30},{4,1},{5,0},{6,3},{7,2},{8,5},{9,4},{1... | collective-permute-start | bytes 786440 | tf_op jit(solution)/shard_map/ppermute | solution.py:309
  32.3 2.1 %collective-permute-start.8 = (bf16[8,256,128]{2,1,0:T(8,128)(2,1)S(1)}, bf16[8,256,128]{2,1,0:T(8,128)(2,1)S(1)}, u32[]{:S(2)}, u32[]{:S(2)}) collective-permute-start(bf16[8,256,128]{2,1,0:T(8,128)(2,1)S(1)} %pad_maximum_fusion), channel_id=1, source_target_pairs={{0,1},{1,0},{2,3},{3,2},{4,5},{5,4},{6,7},{7,6},{8,9},{9,8},{10,11... | collective-permute-start | bytes 1572872 | tf_op jit(solution)/shard_map/ppermute | solution.py:309
  32.4 13.3 %collective-permute-start.11 = (bf16[4,256,128]{2,1,0:T(8,128)(2,1)S(1)}, bf16[4,256,128]{2,1,0:T(8,128)(2,1)S(1)}, u32[]{:S(2)}, u32[]{:S(2)}) collective-permute-start(bf16[4,256,128]{2,1,0:T(8,128)(2,1)S(1)} %get-tuple-element.71), channel_id=1, source_target_pairs={{2,1},{3,0},{4,3},{5,2},{6,5},{7,4},{8,7},{9,6},{10,9},{11,8},{12,... | collective-permute-start | bytes 786440 | tf_op jit(solution)/shard_map/ppermute | solution.py:309

commit v5 on v4

--- a/solution.py
+++ b/solution.py
@@ -272,11 +272,11 @@
     out_ref[...] = wide[...].astype(out_ref.dtype)
 
 
-def partial_kernel(own_ref, back_ref, side_ref, out_ref):
-    out_ref[...] = own_ref[...] + back_ref[...].astype(jnp.float32) + side_ref[...].astype(jnp.float32)
-
-
-def final_kv_kernel(part_ref, got_ref, back_r, side_r, after, out_k, out_v, wide):
+def partial_kernel(own_ref, back_ref, out_ref):
+    out_ref[...] = own_ref[...] + back_ref[...].astype(jnp.float32)
+
+
+def final_kv_kernel(part_ref, got_ref, back_r, side_s, side_r, after, out_k, out_v, wide):
     rows, heads, size = out_k.shape
     half = heads // 2
     core = lax.axis_index(AXIS) % 2
@@ -284,7 +284,9 @@
     for part in range(2):
         for j in range(half):
             n = part * half + j
-            flat[pl.ds(part * heads + core * half + j, rows, stride=2 * heads), :] = part_ref[n]
+            flat[pl.ds(part * heads + core * half + j, rows, stride=2 * heads), :] = part_ref[n] + side_s[n].astype(
+                jnp.float32
+            )
             flat[pl.ds(part * heads + (1 - core) * half + j, rows, stride=2 * heads), :] = (
                 got_ref[n].astype(jnp.float32)
                 + back_r[n].astype(jnp.float32)
@@ -382,11 +384,10 @@
     near = functools.partial(call, near_kernel, out_shape=[shape(kv_block, low)] + acc, scratch=grad_scratch)
     near_s, gq_s, gq_r = near(name="near_s")(one_s, *sides, gq_s, gq_r)
     side_s = move(near_s, lambda i: i - 2)
-    one_r, back_s = lax.optimization_barrier((one_r, back_s))
     near_r, gq_s, gq_r = near(name="near_r")(one_r, *sides, gq_s, gq_r)
     side_r = move(near_r, lambda i: sibling(i - 2) if i >= 2 else -1)
 
-    part = call(partial_kernel, "partial", shape(kv_block, f32), flops=LONG)(own_s, back_s, side_s)
+    part = call(partial_kernel, "partial", shape(kv_block, f32), flops=LONG)(own_s, back_s)
     give = jnp.concatenate([own_r.astype(low), (gq_r * query_scale).astype(low).reshape(-1, rows, size)])
     got = move(give, sibling)
     grad_q, token = call(
@@ -401,8 +402,8 @@
         "final_kv",
         [shape(key_rows.shape, low), shape(value_rows.shape, low)],
         [pltpu.VMEM((rows, 2 * groups, size), f32)],
-        in_specs=[vmem] * 4 + [anywhere],
-    )(part, got, back_r, side_r, token)
+        in_specs=[vmem] * 5 + [anywhere],
+    )(part, got, back_r, side_s, side_r, token)
     return grad_q, grad_k, grad_v
 
 

time: 47.1 us -> 46 us (0.977)
  starting transfers between devices: 15.6 us -> 14.7 us
    ppermute x12, starting transfers between devices: 15.6 us -> 14.7 us  [move(): return lax.ppermute(x, AXIS, [(i, j) for i, j in pairs if j >= 0])]
  transfers between devices with their start and end apart: 12 -> 12, of which waited for: 3 -> 3; matrix products, arithmetic and copies ran while one was open for 0% -> 0% of each run, Pallas kernels for 22% -> 23%
where the time goes in v5:
time: 46 us; the launch traced here: 45.8 us
  waiting for transfers between devices  16.9 us (37%)
  starting transfers between devices  14.7 us (32%)
  Pallas kernels  13.2 us (29%)
  between operations  0.81 us (2%)
    ppermute x12, waiting for transfers between devices, move(): return lax.ppermute(x, AXIS, [(i, j) for i, j in pairs if j >= 0])  16.9 us
    ppermute x12, starting transfers between devices, move(): return lax.ppermute(x, AXIS, [(i, j) for i, j in pairs if j >= 0])  14.7 us
    pallas_call x1, Pallas kernels, shards(): call(pack_q_kernel, 'pack_q', [shape((half_rows, size), low), shape((half...  2.67 us
    pallas_call x1, Pallas kernels, shards(): call(own_rest_kernel, 'own_rest', [shape(kv_block, f32)] * 2 + acc, flops=0)  2.02 us
    pallas_call x1, Pallas kernels, shards(): near_r, gq_s, gq_r = near(name='near_r')(one_r, *sides, gq_s, gq_r)  1.89 us
    pallas_call x1, Pallas kernels, shards(): near_s, gq_s, gq_r = near(name='near_s')(one_s, *sides, gq_s, gq_r)  1.68 us
    pallas_call x1, Pallas kernels, shards(): call(final_kv_kernel, 'final_kv', [shape(key_rows.shape, low), shape(valu...  1.29 us
    pallas_call x1, Pallas kernels, shards(): call(pack_kv_kernel, 'pack_kv', [shape(kv_block, low)] * 2, [pltpu.VMEM(k...  1.27 us
  transfers between devices with their start and end apart: 12, of which 3 were waited for; matrix products, arithmetic and copies ran while one was open for 0% of the time, Pallas kernels for 23%

profile of v5, /device:TPU:3, one launch (start us, length us, event | category | flops | bytes accessed | tf_op | source)
XLA Modules:
  0.0 45.8 jit_solution(13498764071319708895)
XLA Ops:
  0.6 1.3 %pack_kv.1 = (bf16[4,256,128]{2,1,0:T(8,128)(2,1)S(1)}, bf16[4,256,128]{2,1,0:T(8,128)(2,1)S(1)}) custom-call(bf16[256,4,128]{2,1,0:T(4,128)(2,1)} %k_hbm.1, bf16[256,4,128]{2,1,0:T(4,128)(2,1)} %v_hbm.1), custom_call_target="tpu_custom_call" | custom-call | bytes 2097152 | tf_op jit(solution)/shard_map/pack_kv/pallas_call | solution.py:334
  1.9 0.7 %collective-permute-start = (bf16[4,256,128]{2,1,0:T(8,128)(2,1)S(1)}, bf16[4,256,128]{2,1,0:T(8,128)(2,1)S(1)}, u32[]{:S(2)}, u32[]{:S(2)}) collective-permute-start(bf16[4,256,128]{2,1,0:T(8,128)(2,1)S(1)} %get-tuple-element.37), channel_id=1, source_target_pairs={{0,1},{1,0},{2,3},{3,2},{4,5},{5,4},{6,7},{7,6},{8,9},{9,8},{10,11... | collective-permute-start | bytes 786440 | tf_op jit(solution)/shard_map/ppermute | solution.py:311
  2.7 1.2 %collective-permute-start.2 = (bf16[4,256,128]{2,1,0:T(8,128)(2,1)S(1)}, bf16[4,256,128]{2,1,0:T(8,128)(2,1)S(1)}, u32[]{:S(2)}, u32[]{:S(2)}) collective-permute-start(bf16[4,256,128]{2,1,0:T(8,128)(2,1)S(1)} %get-tuple-element.38.kv_s), channel_id=1, source_target_pairs={{0,4},{1,5},{2,6},{3,7},{4,8},{5,9},{6,10},{7,11},{8,12},{9,13},{1... | collective-permute-start | bytes 786440 | tf_op jit(solution)/shard_map/ppermute | solution.py:311
  3.9 2.7 %pack_q.1 = (bf16[1024,128]{1,0:T(8,128)(2,1)S(1)}, bf16[1024,128]{1,0:T(8,128)(2,1)S(1)}, f32[16,128]{1,0:T(8,128)S(1)}, bf16[1072,128]{1,0:T(8,128)(2,1)S(1)}, bf16[1024,128]{1,0:T(8,128)(2,1)S(1)}) custom-call(bf16[256,8,128]{2,1,0:T(8,128)(2,1)} %q_hbm.1, bf16[256,8,128]{2,1,0:T(8,128)(2,1)} %g_hbm.1, bf16[256,8,128]{2,1,0:T(8,128)(2,1)} %o_hbm.1, ...), custom_call_target="tpu_custom_call" | custom-call | bytes 2097152 | tf_op jit(solution)/shard_map/pack_q/pallas_call | solution.py:345
  6.6 0.4 collective-permute-start.3
  7.0 0.2 collective-permute-start.4
  7.2 1.2 %collective-permute-start.1 = (bf16[4,256,128]{2,1,0:T(8,128)(2,1)S(1)}, bf16[4,256,128]{2,1,0:T(8,128)(2,1)S(1)}, u32[]{:S(2)}, u32[]{:S(2)}) collective-permute-start(bf16[4,256,128]{2,1,0:T(8,128)(2,1)S(1)} %collective-permute-done.after.kv_r), channel_id=1, source_target_pairs={{0,4},{1,5},{2,6},{3,7},{4,8},{5,9},{6,10},{7,11},{8,12},{9,13},{1... | collective-permute-start | bytes 786440 | tf_op jit(solution)/shard_map/ppermute | solution.py:311
  8.4 5.1 %collective-permute-done.2.kv = bf16[4,256,128]{2,1,0:T(8,128)(2,1)S(1)} collective-permute-done((bf16[4,256,128]{2,1,0:T(8,128)(2,1)S(1)}, bf16[4,256,128]{2,1,0:T(8,128)(2,1)S(1)}, u32[]{:S(2)}, u32[]{:S(2)}) %collective-permute-start.2) | collective-permute-done | bytes 262176 | tf_op jit(solution)/shard_map/ppermute | solution.py:311
  13.5 0.4 collective-permute-start.6
  13.9 0.9 %own_side.1 = (f32[4,256,128]{2,1,0:T(8,128)S(1)}, f32[2,512,128]{2,1,0:T(8,128)S(1)}) custom-call(bf16[4,256,128]{2,1,0:T(8,128)(2,1)S(1)} %get-tuple-element.38.kv_s, bf16[1024,128]{1,0:T(8,128)(2,1)S(1)} %get-tuple-element.41.q_s, bf16[1024,128]{1,0:T(8,128)(2,1)S(1)} %get-tuple-element.42.g_s, f32[16,128]{1,0:T(8,128)S(1)} %get-tuple-element.43.rows_s), custom_call_target="tpu_custom_call" | custom-call | bytes 2097152 | tf_op jit(solution)/shard_map/own_side/pallas_call | solution.py:365
  14.9 0.0 collective-permute-done.4.g_r
  14.9 2.0 %own_rest.1 = (f32[4,256,128]{2,1,0:T(8,128)S(1)}, f32[4,256,128]{2,1,0:T(8,128)S(1)}, f32[2,512,128]{2,1,0:T(8,128)S(1)}, f32[2,512,128]{2,1,0:T(8,128)S(1)}) custom-call(bf16[4,256,128]{2,1,0:T(8,128)(2,1)S(1)} %get-tuple-element.38.kv_s, bf16[4,256,128]{2,1,0:T(8,128)(2,1)S(1)} %collective-permute-done.after.kv_r, ...), custom_call_target="tpu_custom_call" | custom-call | bytes 2097152 | tf_op jit(solution)/shard_map/own_rest/pallas_call | solution.py:368
  16.9 0.1 far_s.1
  17.0 2.1 %collective-permute-done.1.kv = bf16[4,256,128]{2,1,0:T(8,128)(2,1)S(1)} collective-permute-done((bf16[4,256,128]{2,1,0:T(8,128)(2,1)S(1)}, bf16[4,256,128]{2,1,0:T(8,128)(2,1)S(1)}, u32[]{:S(2)}, u32[]{:S(2)}) %collective-permute-start.1) | collective-permute-done | bytes 262176 | tf_op jit(solution)/shard_map/ppermute | solution.py:311
  19.1 0.4 collective-permute-start.5
  19.6 2.0 %collective-permute-start.8 = (bf16[4,256,128]{2,1,0:T(8,128)(2,1)S(1)}, bf16[4,256,128]{2,1,0:T(8,128)(2,1)S(1)}, u32[]{:S(2)}, u32[]{:S(2)}) collective-permute-start(bf16[4,256,128]{2,1,0:T(8,128)(2,1)S(1)} %get-tuple-element.63), channel_id=1, source_target_pairs={{0,28},{1,29},{2,30},{3,31},{4,0},{5,1},{6,2},{7,3},{8,4},{9,5},{1... | collective-permute-start | bytes 786440 | tf_op jit(solution)/shard_map/ppermute | solution.py:311
  21.6 0.1 far_r.1
  21.7 4.1 %collective-permute-start.9 = (bf16[4,256,128]{2,1,0:T(8,128)(2,1)S(1)}, bf16[4,256,128]{2,1,0:T(8,128)(2,1)S(1)}, u32[]{:S(2)}, u32[]{:S(2)}) collective-permute-start(bf16[4,256,128]{2,1,0:T(8,128)(2,1)S(1)} %get-tuple-element.65), channel_id=1, source_target_pairs={{0,29},{1,28},{2,31},{3,30},{4,1},{5,0},{6,3},{7,2},{8,5},{9,4},{1... | collective-permute-start | bytes 786440 | tf_op jit(solution)/shard_map/ppermute | solution.py:311
  25.8 0.0 collective-permute-done.6.kv
  25.9 1.7 %near_s.1 = (bf16[4,256,128]{2,1,0:T(8,128)(2,1)S(1)}, f32[2,512,128]{2,1,0:T(8,128)S(1)}, f32[2,512,128]{2,1,0:T(8,128)S(1)}) custom-call(bf16[4,256,128]{2,1,0:T(8,128)(2,1)S(1)} %collective-permute-done.6.kv, bf16[1024,128]{1,0:T(8,128)(2,1)S(1)} %get-tuple-element.41.q_s, bf16[1024,128]{1,0:T(8,128)(2,1)S(1)} %get-tuple-element.42.g_s, ...), custom_call_target="tpu_custom_call" | custom-call | bytes 2097152 | tf_op jit(solution)/shard_map/near_s/pallas_call | solution.py:385
  27.5 1.9 %collective-permute-start.10 = (bf16[4,256,128]{2,1,0:T(8,128)(2,1)S(1)}, bf16[4,256,128]{2,1,0:T(8,128)(2,1)S(1)}, u32[]{:S(2)}, u32[]{:S(2)}) collective-permute-start(bf16[4,256,128]{2,1,0:T(8,128)(2,1)S(1)} %get-tuple-element.66), channel_id=1, source_target_pairs={{2,0},{3,1},{4,2},{5,3},{6,4},{7,5},{8,6},{9,7},{10,8},{11,9},{12,... | collective-permute-start | bytes 786440 | tf_op jit(solution)/shard_map/ppermute | solution.py:311
  29.5 0.0 collective-permute-done.5.kv
  29.5 1.9 %near_r.1 = (bf16[4,256,128]{2,1,0:T(8,128)(2,1)S(1)}, f32[2,512,128]{2,1,0:T(8,128)S(1)}, f32[2,512,128]{2,1,0:T(8,128)S(1)}) custom-call(bf16[4,256,128]{2,1,0:T(8,128)(2,1)S(1)} %collective-permute-done.5.kv, bf16[1024,128]{1,0:T(8,128)(2,1)S(1)} %get-tuple-element.41.q_s, bf16[1024,128]{1,0:T(8,128)(2,1)S(1)} %get-tuple-element.42.g_s, ...), custom_call_target="tpu_custom_call" | custom-call | bytes 2097152 | tf_op jit(solution)/shard_map/near_r/pallas_call | solution.py:387
  31.4 0.1 multiply_convert_fusion
  31.5 0.1 collective-permute-start.7
  31.6 1.9 %collective-permute-start.11 = (bf16[4,256,128]{2,1,0:T(8,128)(2,1)S(1)}, bf16[4,256,128]{2,1,0:T(8,128)(2,1)S(1)}, u32[]{:S(2)}, u32[]{:S(2)}) collective-permute-start(bf16[4,256,128]{2,1,0:T(8,128)(2,1)S(1)} %get-tuple-element.67), channel_id=1, source_target_pairs={{2,1},{3,0},{4,3},{5,2},{6,5},{7,4},{8,7},{9,6},{10,9},{11,8},{12,... | collective-permute-start | bytes 786440 | tf_op jit(solution)/shard_map/ppermute | solution.py:311
  33.6 0.0 collective-permute-done.7.got_ref
  33.6 1.1 %final_q.1 = (bf16[256,8,128]{2,1,0:T(8,128)(2,1)}, f32[8,128]{1,0:T(8,128)S(1)}) custom-call(f32[2,512,128]{2,1,0:T(8,128)S(1)} %get-tuple-element.59.own_ref, bf16[8,256,128]{2,1,0:T(8,128)(2,1)S(1)} %collective-permute-done.7.got_ref, f32[4,256,128]{2,1,0:T(8,128)S(1)} %partial.1.after.part_ref), custom_call_target="tpu_custom_call" | custom-call | bytes 2097152 | tf_op jit(solution)/shard_map/final_q/pallas_call | solution.py:393
  34.7 9.8 %collective-permute-done.9.back_r = bf16[4,256,128]{2,1,0:T(8,128)(2,1)S(1)} collective-permute-done((bf16[4,256,128]{2,1,0:T(8,128)(2,1)S(1)}, bf16[4,256,128]{2,1,0:T(8,128)(2,1)S(1)}, u32[]{:S(2)}, u32[]{:S(2)}) %collective-permute-start.9) | collective-permute-done | bytes 262176 | tf_op jit(solution)/shard_map/ppermute | solution.py:311
  44.5 0.0 collective-permute-done.10.side_s
  44.5 0.0 collective-permute-done.11.side_r
  44.5 1.3 %final_kv.1 = (bf16[256,4,128]{2,1,0:T(4,128)(2,1)}, bf16[256,4,128]{2,1,0:T(4,128)(2,1)}) custom-call(f32[4,256,128]{2,1,0:T(8,128)S(1)} %partial.1.after.part_ref, bf16[8,256,128]{2,1,0:T(8,128)(2,1)S(1)} %collective-permute-done.7.got_ref, bf16[4,256,128]{2,1,0:T(8,128)(2,1)S(1)} %collective-permute-done.9.back_r, ...), custom_call_target="tpu_custom_call" | custom-call | bytes 2097152 | tf_op jit(solution)/shard_map/final_kv/pallas_call | solution.py:400
  (10 shorter events, 0.2 us)
Async XLA Ops:
  0.6 3.3 %copy-start = (f32[8,256]{1,0:T(8,128)S(1)}, f32[8,256]{1,0:T(8,128)}, u32[]{:S(2)}) copy-start(f32[8,256]{1,0:T(8,128)} %norm_ref.1) | copy-start | bytes 24580
  1.9 2.0 %collective-permute-start = (bf16[4,256,128]{2,1,0:T(8,128)(2,1)S(1)}, bf16[4,256,128]{2,1,0:T(8,128)(2,1)S(1)}, u32[]{:S(2)}, u32[]{:S(2)}) collective-permute-start(bf16[4,256,128]{2,1,0:T(8,128)(2,1)S(1)} %get-tuple-element.37), channel_id=1, source_target_pairs={{0,1},{1,0},{2,3},{3,2},{4,5},{5,4},{6,7},{7,6},{8,9},{9,8},{10,11... | collective-permute-start | bytes 786440 | tf_op jit(solution)/shard_map/ppermute | solution.py:311
  2.7 10.8 %collective-permute-start.2 = (bf16[4,256,128]{2,1,0:T(8,128)(2,1)S(1)}, bf16[4,256,128]{2,1,0:T(8,128)(2,1)S(1)}, u32[]{:S(2)}, u32[]{:S(2)}) collective-permute-start(bf16[4,256,128]{2,1,0:T(8,128)(2,1)S(1)} %get-tuple-element.38.kv_s), channel_id=1, source_target_pairs={{0,4},{1,5},{2,6},{3,7},{4,8},{5,9},{6,10},{7,11},{8,12},{9,13},{1... | collective-permute-start | bytes 786440 | tf_op jit(solution)/shard_map/ppermute | solution.py:311
  6.6 8.3 %collective-permute-start.3 = (bf16[1072,128]{1,0:T(8,128)(2,1)S(1)}, bf16[1072,128]{1,0:T(8,128)(2,1)S(1)}, u32[]{:S(2)}, u32[]{:S(2)}) collective-permute-start(bf16[1072,128]{1,0:T(8,128)(2,1)S(1)} %get-tuple-element.44), channel_id=1, source_target_pairs={{0,1},{1,0},{2,3},{3,2},{4,5},{5,4},{6,7},{7,6},{8,9},{9,8},{10,11... | collective-permute-start | bytes 823304 | tf_op jit(solution)/shard_map/ppermute | solution.py:311
  7.0 7.9 %collective-permute-start.4 = (bf16[1024,128]{1,0:T(8,128)(2,1)S(1)}, bf16[1024,128]{1,0:T(8,128)(2,1)S(1)}, u32[]{:S(2)}, u32[]{:S(2)}) collective-permute-start(bf16[1024,128]{1,0:T(8,128)(2,1)S(1)} %get-tuple-element.45), channel_id=1, source_target_pairs={{0,1},{1,0},{2,3},{3,2},{4,5},{5,4},{6,7},{7,6},{8,9},{9,8},{10,11... | collective-permute-start | bytes 786440 | tf_op jit(solution)/shard_map/ppermute | solution.py:311
  7.2 11.9 %collective-permute-start.1 = (bf16[4,256,128]{2,1,0:T(8,128)(2,1)S(1)}, bf16[4,256,128]{2,1,0:T(8,128)(2,1)S(1)}, u32[]{:S(2)}, u32[]{:S(2)}) collective-permute-start(bf16[4,256,128]{2,1,0:T(8,128)(2,1)S(1)} %collective-permute-done.after.kv_r), channel_id=1, source_target_pairs={{0,4},{1,5},{2,6},{3,7},{4,8},{5,9},{6,10},{7,11},{8,12},{9,13},{1... | collective-permute-start | bytes 786440 | tf_op jit(solution)/shard_map/ppermute | solution.py:311
  13.5 12.3 %collective-permute-start.6 = (bf16[4,256,128]{2,1,0:T(8,128)(2,1)S(1)}, bf16[4,256,128]{2,1,0:T(8,128)(2,1)S(1)}, u32[]{:S(2)}, u32[]{:S(2)}) collective-permute-start(bf16[4,256,128]{2,1,0:T(8,128)(2,1)S(1)} %broadcast_select_fusion), channel_id=1, source_target_pairs={{0,2},{1,3},{2,0},{3,1},{4,6},{5,7},{6,4},{7,5},{8,10},{9,11},{10,... | collective-permute-start | bytes 786440 | tf_op jit(solution)/shard_map/ppermute | solution.py:311
  19.1 10.3 %collective-permute-start.5 = (bf16[4,256,128]{2,1,0:T(8,128)(2,1)S(1)}, bf16[4,256,128]{2,1,0:T(8,128)(2,1)S(1)}, u32[]{:S(2)}, u32[]{:S(2)}) collective-permute-start(bf16[4,256,128]{2,1,0:T(8,128)(2,1)S(1)} %broadcast_select_fusion.1), channel_id=1, source_target_pairs={{0,2},{1,3},{2,0},{3,1},{4,6},{5,7},{6,4},{7,5},{8,10},{9,11},{10,... | collective-permute-start | bytes 786440 | tf_op jit(solution)/shard_map/ppermute | solution.py:311
  19.6 13.9 %collective-permute-start.8 = (bf16[4,256,128]{2,1,0:T(8,128)(2,1)S(1)}, bf16[4,256,128]{2,1,0:T(8,128)(2,1)S(1)}, u32[]{:S(2)}, u32[]{:S(2)}) collective-permute-start(bf16[4,256,128]{2,1,0:T(8,128)(2,1)S(1)} %get-tuple-element.63), channel_id=1, source_target_pairs={{0,28},{1,29},{2,30},{3,31},{4,0},{5,1},{6,2},{7,3},{8,4},{9,5},{1... | collective-permute-start | bytes 786440 | tf_op jit(solution)/shard_map/ppermute | solution.py:311
  21.7 22.8 %collective-permute-start.9 = (bf16[4,256,128]{2,1,0:T(8,128)(2,1)S(1)}, bf16[4,256,128]{2,1,0:T(8,128)(2,1)S(1)}, u32[]{:S(2)}, u32[]{:S(2)}) collective-permute-start(bf16[4,256,128]{2,1,0:T(8,128)(2,1)S(1)} %get-tuple-element.65), channel_id=1, source_target_pairs={{0,29},{1,28},{2,31},{3,30},{4,1},{5,0},{6,3},{7,2},{8,5},{9,4},{1... | collective-permute-start | bytes 786440 | tf_op jit(solution)/shard_map/ppermute | solution.py:311
  27.5 17.0 %collective-permute-start.10 = (bf16[4,256,128]{2,1,0:T(8,128)(2,1)S(1)}, bf16[4,256,128]{2,1,0:T(8,128)(2,1)S(1)}, u32[]{:S(2)}, u32[]{:S(2)}) collective-permute-start(bf16[4,256,128]{2,1,0:T(8,128)(2,1)S(1)} %get-tuple-element.66), channel_id=1, source_target_pairs={{2,0},{3,1},{4,2},{5,3},{6,4},{7,5},{8,6},{9,7},{10,8},{11,9},{12,... | collective-permute-start | bytes 786440 | tf_op jit(solution)/shard_map/ppermute | solution.py:311
  31.5 2.1 %collective-permute-start.7 = (bf16[8,256,128]{2,1,0:T(8,128)(2,1)S(1)}, bf16[8,256,128]{2,1,0:T(8,128)(2,1)S(1)}, u32[]{:S(2)}, u32[]{:S(2)}) collective-permute-start(bf16[8,256,128]{2,1,0:T(8,128)(2,1)S(1)} %pad_maximum_fusion), channel_id=1, source_target_pairs={{0,1},{1,0},{2,3},{3,2},{4,5},{5,4},{6,7},{7,6},{8,9},{9,8},{10,11... | collective-permute-start | bytes 1572872 | tf_op jit(solution)/shard_map/ppermute | solution.py:311
  31.6 12.9 %collective-permute-start.11 = (bf16[4,256,128]{2,1,0:T(8,128)(2,1)S(1)}, bf16[4,256,128]{2,1,0:T(8,128)(2,1)S(1)}, u32[]{:S(2)}, u32[]{:S(2)}) collective-permute-start(bf16[4,256,128]{2,1,0:T(8,128)(2,1)S(1)} %get-tuple-element.67), channel_id=1, source_target_pairs={{2,1},{3,0},{4,3},{5,2},{6,5},{7,4},{8,7},{9,6},{10,9},{11,8},{12,... | collective-permute-start | bytes 786440 | tf_op jit(solution)/shard_map/ppermute | solution.py:311

commit v6 on v5

--- a/solution.py
+++ b/solution.py
@@ -384,6 +384,7 @@
     near = functools.partial(call, near_kernel, out_shape=[shape(kv_block, low)] + acc, scratch=grad_scratch)
     near_s, gq_s, gq_r = near(name="near_s")(one_s, *sides, gq_s, gq_r)
     side_s = move(near_s, lambda i: i - 2)
+    back_s, one_r = lax.optimization_barrier((back_s, one_r))
     near_r, gq_s, gq_r = near(name="near_r")(one_r, *sides, gq_s, gq_r)
     side_r = move(near_r, lambda i: sibling(i - 2) if i >= 2 else -1)
 

time: 46 us -> 44.6 us (0.970)
  waiting for transfers between devices: 16.9 us -> 13.2 us
  starting transfers between devices: 14.7 us -> 16.7 us
    ppermute x12, waiting for transfers between devices: 16.9 us -> 13.2 us  [move(): return lax.ppermute(x, AXIS, [(i, j) for i, j in pairs if j >= 0])]
    ppermute x12, starting transfers between devices: 14.7 us -> 16.7 us  [move(): return lax.ppermute(x, AXIS, [(i, j) for i, j in pairs if j >= 0])]
  transfers between devices with their start and end apart: 12 -> 12, of which waited for: 3 -> 3; matrix products, arithmetic and copies ran while one was open for 0% -> 0% of each run, Pallas kernels for 23% -> 24%
where the time goes in v6:
time: 44.6 us; the launch traced here: 44.1 us
  starting transfers between devices  16.7 us (37%)
  Pallas kernels  13.2 us (30%)
  waiting for transfers between devices  13.2 us (30%)
  between operations  0.81 us (2%)
    ppermute x12, starting transfers between devices, move(): return lax.ppermute(x, AXIS, [(i, j) for i, j in pairs if j >= 0])  16.7 us
    ppermute x12, waiting for transfers between devices, move(): return lax.ppermute(x, AXIS, [(i, j) for i, j in pairs if j >= 0])  13.2 us
    pallas_call x1, Pallas kernels, shards(): call(pack_q_kernel, 'pack_q', [shape((half_rows, size), low), shape((half...  2.67 us
    pallas_call x1, Pallas kernels, shards(): call(own_rest_kernel, 'own_rest', [shape(kv_block, f32)] * 2 + acc, flops=0)  2.02 us
    pallas_call x1, Pallas kernels, shards(): near_r, gq_s, gq_r = near(name='near_r')(one_r, *sides, gq_s, gq_r)  1.89 us
    pallas_call x1, Pallas kernels, shards(): near_s, gq_s, gq_r = near(name='near_s')(one_s, *sides, gq_s, gq_r)  1.69 us
    pallas_call x1, Pallas kernels, shards(): call(final_kv_kernel, 'final_kv', [shape(key_rows.shape, low), shape(valu...  1.29 us
    pallas_call x1, Pallas kernels, shards(): call(pack_kv_kernel, 'pack_kv', [shape(kv_block, low)] * 2, [pltpu.VMEM(k...  1.27 us
  transfers between devices with their start and end apart: 12, of which 3 were waited for; matrix products, arithmetic and copies ran while one was open for 0% of the time, Pallas kernels for 24%

profile of v6, /device:TPU:3, one launch (start us, length us, event | category | flops | bytes accessed | tf_op | source)
XLA Modules:
  0.0 44.1 jit_solution(11278022176452518601)
XLA Ops:
  0.6 1.3 %pack_kv.1 = (bf16[4,256,128]{2,1,0:T(8,128)(2,1)S(1)}, bf16[4,256,128]{2,1,0:T(8,128)(2,1)S(1)}) custom-call(bf16[256,4,128]{2,1,0:T(4,128)(2,1)} %k_hbm.1, bf16[256,4,128]{2,1,0:T(4,128)(2,1)} %v_hbm.1), custom_call_target="tpu_custom_call" | custom-call | bytes 2097152 | tf_op jit(solution)/shard_map/pack_kv/pallas_call | solution.py:334
  1.9 0.7 %collective-permute-start.1 = (bf16[4,256,128]{2,1,0:T(8,128)(2,1)S(1)}, bf16[4,256,128]{2,1,0:T(8,128)(2,1)S(1)}, u32[]{:S(2)}, u32[]{:S(2)}) collective-permute-start(bf16[4,256,128]{2,1,0:T(8,128)(2,1)S(1)} %get-tuple-element.40), channel_id=1, source_target_pairs={{0,1},{1,0},{2,3},{3,2},{4,5},{5,4},{6,7},{7,6},{8,9},{9,8},{10,11... | collective-permute-start | bytes 786440 | tf_op jit(solution)/shard_map/ppermute | solution.py:311
  2.7 1.2 %collective-permute-start = (bf16[4,256,128]{2,1,0:T(8,128)(2,1)S(1)}, bf16[4,256,128]{2,1,0:T(8,128)(2,1)S(1)}, u32[]{:S(2)}, u32[]{:S(2)}) collective-permute-start(bf16[4,256,128]{2,1,0:T(8,128)(2,1)S(1)} %get-tuple-element.39.kv_s), channel_id=1, source_target_pairs={{0,4},{1,5},{2,6},{3,7},{4,8},{5,9},{6,10},{7,11},{8,12},{9,13},{1... | collective-permute-start | bytes 786440 | tf_op jit(solution)/shard_map/ppermute | solution.py:311
  3.9 0.0 collective-permute-done.1.after.kv_r
  3.9 2.7 %pack_q.1 = (bf16[1024,128]{1,0:T(8,128)(2,1)S(1)}, bf16[1024,128]{1,0:T(8,128)(2,1)S(1)}, f32[16,128]{1,0:T(8,128)S(1)}, bf16[1072,128]{1,0:T(8,128)(2,1)S(1)}, bf16[1024,128]{1,0:T(8,128)(2,1)S(1)}) custom-call(bf16[256,8,128]{2,1,0:T(8,128)(2,1)} %q_hbm.1, bf16[256,8,128]{2,1,0:T(8,128)(2,1)} %g_hbm.1, bf16[256,8,128]{2,1,0:T(8,128)(2,1)} %o_hbm.1, ...), custom_call_target="tpu_custom_call" | custom-call | bytes 2097152 | tf_op jit(solution)/shard_map/pack_q/pallas_call | solution.py:345
  6.6 0.4 collective-permute-start.2
  7.0 0.2 collective-permute-start.3
  7.2 1.2 %collective-permute-start.5 = (bf16[4,256,128]{2,1,0:T(8,128)(2,1)S(1)}, bf16[4,256,128]{2,1,0:T(8,128)(2,1)S(1)}, u32[]{:S(2)}, u32[]{:S(2)}) collective-permute-start(bf16[4,256,128]{2,1,0:T(8,128)(2,1)S(1)} %collective-permute-done.1.after.kv_r), channel_id=1, source_target_pairs={{0,4},{1,5},{2,6},{3,7},{4,8},{5,9},{6,10},{7,11},{8,12},{9,13},{1... | collective-permute-start | bytes 786440 | tf_op jit(solution)/shard_map/ppermute | solution.py:311
  8.4 5.1 %collective-permute-done.kv = bf16[4,256,128]{2,1,0:T(8,128)(2,1)S(1)} collective-permute-done((bf16[4,256,128]{2,1,0:T(8,128)(2,1)S(1)}, bf16[4,256,128]{2,1,0:T(8,128)(2,1)S(1)}, u32[]{:S(2)}, u32[]{:S(2)}) %collective-permute-start) | collective-permute-done | bytes 262176 | tf_op jit(solution)/shard_map/ppermute | solution.py:311
  13.5 0.4 collective-permute-start.7
  13.9 0.9 %own_side.1 = (f32[4,256,128]{2,1,0:T(8,128)S(1)}, f32[2,512,128]{2,1,0:T(8,128)S(1)}) custom-call(bf16[4,256,128]{2,1,0:T(8,128)(2,1)S(1)} %get-tuple-element.39.kv_s, bf16[1024,128]{1,0:T(8,128)(2,1)S(1)} %get-tuple-element.43.q_s, bf16[1024,128]{1,0:T(8,128)(2,1)S(1)} %get-tuple-element.44.g_s, f32[16,128]{1,0:T(8,128)S(1)} %get-tuple-element.45.rows_s), custom_call_target="tpu_custom_call" | custom-call | bytes 2097152 | tf_op jit(solution)/shard_map/own_side/pallas_call | solution.py:365
  14.9 0.0 collective-permute-done.2.q_r
  14.9 2.0 %own_rest.1 = (f32[4,256,128]{2,1,0:T(8,128)S(1)}, f32[4,256,128]{2,1,0:T(8,128)S(1)}, f32[2,512,128]{2,1,0:T(8,128)S(1)}, f32[2,512,128]{2,1,0:T(8,128)S(1)}) custom-call(bf16[4,256,128]{2,1,0:T(8,128)(2,1)S(1)} %get-tuple-element.39.kv_s, bf16[4,256,128]{2,1,0:T(8,128)(2,1)S(1)} %collective-permute-done.1.after.kv_r, ...), custom_call_target="tpu_custom_call" | custom-call | bytes 2097152 | tf_op jit(solution)/shard_map/own_rest/pallas_call | solution.py:368
  16.9 0.1 far_s.1
  17.0 3.2 %collective-permute-start.4 = (bf16[4,256,128]{2,1,0:T(8,128)(2,1)S(1)}, bf16[4,256,128]{2,1,0:T(8,128)(2,1)S(1)}, u32[]{:S(2)}, u32[]{:S(2)}) collective-permute-start(bf16[4,256,128]{2,1,0:T(8,128)(2,1)S(1)} %get-tuple-element.52), channel_id=1, source_target_pairs={{0,28},{1,29},{2,30},{3,31},{4,0},{5,1},{6,2},{7,3},{8,4},{9,5},{1... | collective-permute-start | bytes 786440 | tf_op jit(solution)/shard_map/ppermute | solution.py:311
  20.2 0.0 collective-permute-done.5.kv
  20.3 1.3 %collective-permute-start.6 = (bf16[4,256,128]{2,1,0:T(8,128)(2,1)S(1)}, bf16[4,256,128]{2,1,0:T(8,128)(2,1)S(1)}, u32[]{:S(2)}, u32[]{:S(2)}) collective-permute-start(bf16[4,256,128]{2,1,0:T(8,128)(2,1)S(1)} %broadcast_select_fusion.1), channel_id=1, source_target_pairs={{0,2},{1,3},{2,0},{3,1},{4,6},{5,7},{6,4},{7,5},{8,10},{9,11},{10,... | collective-permute-start | bytes 786440 | tf_op jit(solution)/shard_map/ppermute | solution.py:311
  21.6 0.1 far_r.1
  21.7 4.1 %collective-permute-start.9 = (bf16[4,256,128]{2,1,0:T(8,128)(2,1)S(1)}, bf16[4,256,128]{2,1,0:T(8,128)(2,1)S(1)}, u32[]{:S(2)}, u32[]{:S(2)}) collective-permute-start(bf16[4,256,128]{2,1,0:T(8,128)(2,1)S(1)} %get-tuple-element.69), channel_id=1, source_target_pairs={{0,29},{1,28},{2,31},{3,30},{4,1},{5,0},{6,3},{7,2},{8,5},{9,4},{1... | collective-permute-start | bytes 786440 | tf_op jit(solution)/shard_map/ppermute | solution.py:311
  25.9 0.0 collective-permute-done.7.kv
  25.9 1.7 %near_s.1 = (bf16[4,256,128]{2,1,0:T(8,128)(2,1)S(1)}, f32[2,512,128]{2,1,0:T(8,128)S(1)}, f32[2,512,128]{2,1,0:T(8,128)S(1)}) custom-call(bf16[4,256,128]{2,1,0:T(8,128)(2,1)S(1)} %collective-permute-done.7.kv, bf16[1024,128]{1,0:T(8,128)(2,1)S(1)} %get-tuple-element.43.q_s, bf16[1024,128]{1,0:T(8,128)(2,1)S(1)} %get-tuple-element.44.g_s, ...), custom_call_target="tpu_custom_call" | custom-call | bytes 2097152 | tf_op jit(solution)/shard_map/near_s/pallas_call | solution.py:385
  27.5 1.9 %collective-permute-start.10 = (bf16[4,256,128]{2,1,0:T(8,128)(2,1)S(1)}, bf16[4,256,128]{2,1,0:T(8,128)(2,1)S(1)}, u32[]{:S(2)}, u32[]{:S(2)}) collective-permute-start(bf16[4,256,128]{2,1,0:T(8,128)(2,1)S(1)} %get-tuple-element.70), channel_id=1, source_target_pairs={{2,0},{3,1},{4,2},{5,3},{6,4},{7,5},{8,6},{9,7},{10,8},{11,9},{12,... | collective-permute-start | bytes 786440 | tf_op jit(solution)/shard_map/ppermute | solution.py:311
  29.5 0.0 collective-permute-done.6.kv
  29.5 1.9 %near_r.1 = (bf16[4,256,128]{2,1,0:T(8,128)(2,1)S(1)}, f32[2,512,128]{2,1,0:T(8,128)S(1)}, f32[2,512,128]{2,1,0:T(8,128)S(1)}) custom-call(bf16[4,256,128]{2,1,0:T(8,128)(2,1)S(1)} %collective-permute-done.6.kv, bf16[1024,128]{1,0:T(8,128)(2,1)S(1)} %get-tuple-element.43.q_s, bf16[1024,128]{1,0:T(8,128)(2,1)S(1)} %get-tuple-element.44.g_s, ...), custom_call_target="tpu_custom_call" | custom-call | bytes 2097152 | tf_op jit(solution)/shard_map/near_r/pallas_call | solution.py:388
  31.4 0.1 multiply_convert_fusion
  31.5 0.1 collective-permute-start.8
  31.6 1.9 %collective-permute-start.11 = (bf16[4,256,128]{2,1,0:T(8,128)(2,1)S(1)}, bf16[4,256,128]{2,1,0:T(8,128)(2,1)S(1)}, u32[]{:S(2)}, u32[]{:S(2)}) collective-permute-start(bf16[4,256,128]{2,1,0:T(8,128)(2,1)S(1)} %get-tuple-element.71), channel_id=1, source_target_pairs={{2,1},{3,0},{4,3},{5,2},{6,5},{7,4},{8,7},{9,6},{10,9},{11,8},{12,... | collective-permute-start | bytes 786440 | tf_op jit(solution)/shard_map/ppermute | solution.py:311
  33.6 0.0 collective-permute-done.8.got_ref
  33.6 1.1 %final_q.1 = (bf16[256,8,128]{2,1,0:T(8,128)(2,1)}, f32[8,128]{1,0:T(8,128)S(1)}) custom-call(f32[2,512,128]{2,1,0:T(8,128)S(1)} %get-tuple-element.63.own_ref, bf16[8,256,128]{2,1,0:T(8,128)(2,1)S(1)} %collective-permute-done.8.got_ref, f32[4,256,128]{2,1,0:T(8,128)S(1)} %partial.1.after.part_ref), custom_call_target="tpu_custom_call" | custom-call | bytes 2097152 | tf_op jit(solution)/shard_map/final_q/pallas_call | solution.py:394
  34.7 2.5 %collective-permute-done.10.side_s = bf16[4,256,128]{2,1,0:T(8,128)(2,1)S(1)} collective-permute-done((bf16[4,256,128]{2,1,0:T(8,128)(2,1)S(1)}, bf16[4,256,128]{2,1,0:T(8,128)(2,1)S(1)}, u32[]{:S(2)}, u32[]{:S(2)}) %collective-permute-start.10) | collective-permute-done | bytes 262176 | tf_op jit(solution)/shard_map/ppermute | solution.py:311
  37.2 5.6 %collective-permute-done.11.side_r = bf16[4,256,128]{2,1,0:T(8,128)(2,1)S(1)} collective-permute-done((bf16[4,256,128]{2,1,0:T(8,128)(2,1)S(1)}, bf16[4,256,128]{2,1,0:T(8,128)(2,1)S(1)}, u32[]{:S(2)}, u32[]{:S(2)}) %collective-permute-start.11) | collective-permute-done | bytes 262176 | tf_op jit(solution)/shard_map/ppermute | solution.py:311
  42.8 1.3 %final_kv.1 = (bf16[256,4,128]{2,1,0:T(4,128)(2,1)}, bf16[256,4,128]{2,1,0:T(4,128)(2,1)}) custom-call(f32[4,256,128]{2,1,0:T(8,128)S(1)} %partial.1.after.part_ref, bf16[8,256,128]{2,1,0:T(8,128)(2,1)S(1)} %collective-permute-done.8.got_ref, bf16[4,256,128]{2,1,0:T(8,128)(2,1)S(1)} %collective-permute-done.9.back_r, ...), custom_call_target="tpu_custom_call" | custom-call | bytes 2097152 | tf_op jit(solution)/shard_map/final_kv/pallas_call | solution.py:401
  (10 shorter events, 0.2 us)
Async XLA Ops:
  0.6 3.3 %copy-start = (f32[8,256]{1,0:T(8,128)S(1)}, f32[8,256]{1,0:T(8,128)}, u32[]{:S(2)}) copy-start(f32[8,256]{1,0:T(8,128)} %norm_ref.1) | copy-start | bytes 24580
  1.9 2.0 %collective-permute-start.1 = (bf16[4,256,128]{2,1,0:T(8,128)(2,1)S(1)}, bf16[4,256,128]{2,1,0:T(8,128)(2,1)S(1)}, u32[]{:S(2)}, u32[]{:S(2)}) collective-permute-start(bf16[4,256,128]{2,1,0:T(8,128)(2,1)S(1)} %get-tuple-element.40), channel_id=1, source_target_pairs={{0,1},{1,0},{2,3},{3,2},{4,5},{5,4},{6,7},{7,6},{8,9},{9,8},{10,11... | collective-permute-start | bytes 786440 | tf_op jit(solution)/shard_map/ppermute | solution.py:311
  2.7 10.8 %collective-permute-start = (bf16[4,256,128]{2,1,0:T(8,128)(2,1)S(1)}, bf16[4,256,128]{2,1,0:T(8,128)(2,1)S(1)}, u32[]{:S(2)}, u32[]{:S(2)}) collective-permute-start(bf16[4,256,128]{2,1,0:T(8,128)(2,1)S(1)} %get-tuple-element.39.kv_s), channel_id=1, source_target_pairs={{0,4},{1,5},{2,6},{3,7},{4,8},{5,9},{6,10},{7,11},{8,12},{9,13},{1... | collective-permute-start | bytes 786440 | tf_op jit(solution)/shard_map/ppermute | solution.py:311
  6.6 8.3 %collective-permute-start.2 = (bf16[1072,128]{1,0:T(8,128)(2,1)S(1)}, bf16[1072,128]{1,0:T(8,128)(2,1)S(1)}, u32[]{:S(2)}, u32[]{:S(2)}) collective-permute-start(bf16[1072,128]{1,0:T(8,128)(2,1)S(1)} %get-tuple-element.46), channel_id=1, source_target_pairs={{0,1},{1,0},{2,3},{3,2},{4,5},{5,4},{6,7},{7,6},{8,9},{9,8},{10,11... | collective-permute-start | bytes 823304 | tf_op jit(solution)/shard_map/ppermute | solution.py:311
  7.0 7.9 %collective-permute-start.3 = (bf16[1024,128]{1,0:T(8,128)(2,1)S(1)}, bf16[1024,128]{1,0:T(8,128)(2,1)S(1)}, u32[]{:S(2)}, u32[]{:S(2)}) collective-permute-start(bf16[1024,128]{1,0:T(8,128)(2,1)S(1)} %get-tuple-element.47), channel_id=1, source_target_pairs={{0,1},{1,0},{2,3},{3,2},{4,5},{5,4},{6,7},{7,6},{8,9},{9,8},{10,11... | collective-permute-start | bytes 786440 | tf_op jit(solution)/shard_map/ppermute | solution.py:311
  7.2 13.1 %collective-permute-start.5 = (bf16[4,256,128]{2,1,0:T(8,128)(2,1)S(1)}, bf16[4,256,128]{2,1,0:T(8,128)(2,1)S(1)}, u32[]{:S(2)}, u32[]{:S(2)}) collective-permute-start(bf16[4,256,128]{2,1,0:T(8,128)(2,1)S(1)} %collective-permute-done.1.after.kv_r), channel_id=1, source_target_pairs={{0,4},{1,5},{2,6},{3,7},{4,8},{5,9},{6,10},{7,11},{8,12},{9,13},{1... | collective-permute-start | bytes 786440 | tf_op jit(solution)/shard_map/ppermute | solution.py:311
  13.5 12.3 %collective-permute-start.7 = (bf16[4,256,128]{2,1,0:T(8,128)(2,1)S(1)}, bf16[4,256,128]{2,1,0:T(8,128)(2,1)S(1)}, u32[]{:S(2)}, u32[]{:S(2)}) collective-permute-start(bf16[4,256,128]{2,1,0:T(8,128)(2,1)S(1)} %broadcast_select_fusion), channel_id=1, source_target_pairs={{0,2},{1,3},{2,0},{3,1},{4,6},{5,7},{6,4},{7,5},{8,10},{9,11},{10,... | collective-permute-start | bytes 786440 | tf_op jit(solution)/shard_map/ppermute | solution.py:311
  17.0 12.4 %collective-permute-start.4 = (bf16[4,256,128]{2,1,0:T(8,128)(2,1)S(1)}, bf16[4,256,128]{2,1,0:T(8,128)(2,1)S(1)}, u32[]{:S(2)}, u32[]{:S(2)}) collective-permute-start(bf16[4,256,128]{2,1,0:T(8,128)(2,1)S(1)} %get-tuple-element.52), channel_id=1, source_target_pairs={{0,28},{1,29},{2,30},{3,31},{4,0},{5,1},{6,2},{7,3},{8,4},{9,5},{1... | collective-permute-start | bytes 786440 | tf_op jit(solution)/shard_map/ppermute | solution.py:311
  20.3 9.2 %collective-permute-start.6 = (bf16[4,256,128]{2,1,0:T(8,128)(2,1)S(1)}, bf16[4,256,128]{2,1,0:T(8,128)(2,1)S(1)}, u32[]{:S(2)}, u32[]{:S(2)}) collective-permute-start(bf16[4,256,128]{2,1,0:T(8,128)(2,1)S(1)} %broadcast_select_fusion.1), channel_id=1, source_target_pairs={{0,2},{1,3},{2,0},{3,1},{4,6},{5,7},{6,4},{7,5},{8,10},{9,11},{10,... | collective-permute-start | bytes 786440 | tf_op jit(solution)/shard_map/ppermute | solution.py:311
  21.7 13.0 %collective-permute-start.9 = (bf16[4,256,128]{2,1,0:T(8,128)(2,1)S(1)}, bf16[4,256,128]{2,1,0:T(8,128)(2,1)S(1)}, u32[]{:S(2)}, u32[]{:S(2)}) collective-permute-start(bf16[4,256,128]{2,1,0:T(8,128)(2,1)S(1)} %get-tuple-element.69), channel_id=1, source_target_pairs={{0,29},{1,28},{2,31},{3,30},{4,1},{5,0},{6,3},{7,2},{8,5},{9,4},{1... | collective-permute-start | bytes 786440 | tf_op jit(solution)/shard_map/ppermute | solution.py:311
  27.5 9.7 %collective-permute-start.10 = (bf16[4,256,128]{2,1,0:T(8,128)(2,1)S(1)}, bf16[4,256,128]{2,1,0:T(8,128)(2,1)S(1)}, u32[]{:S(2)}, u32[]{:S(2)}) collective-permute-start(bf16[4,256,128]{2,1,0:T(8,128)(2,1)S(1)} %get-tuple-element.70), channel_id=1, source_target_pairs={{2,0},{3,1},{4,2},{5,3},{6,4},{7,5},{8,6},{9,7},{10,8},{11,9},{12,... | collective-permute-start | bytes 786440 | tf_op jit(solution)/shard_map/ppermute | solution.py:311
  31.5 2.1 %collective-permute-start.8 = (bf16[8,256,128]{2,1,0:T(8,128)(2,1)S(1)}, bf16[8,256,128]{2,1,0:T(8,128)(2,1)S(1)}, u32[]{:S(2)}, u32[]{:S(2)}) collective-permute-start(bf16[8,256,128]{2,1,0:T(8,128)(2,1)S(1)} %pad_maximum_fusion), channel_id=1, source_target_pairs={{0,1},{1,0},{2,3},{3,2},{4,5},{5,4},{6,7},{7,6},{8,9},{9,8},{10,11... | collective-permute-start | bytes 1572872 | tf_op jit(solution)/shard_map/ppermute | solution.py:311
  31.6 11.2 %collective-permute-start.11 = (bf16[4,256,128]{2,1,0:T(8,128)(2,1)S(1)}, bf16[4,256,128]{2,1,0:T(8,128)(2,1)S(1)}, u32[]{:S(2)}, u32[]{:S(2)}) collective-permute-start(bf16[4,256,128]{2,1,0:T(8,128)(2,1)S(1)} %get-tuple-element.71), channel_id=1, source_target_pairs={{2,1},{3,0},{4,3},{5,2},{6,5},{7,4},{8,7},{9,6},{10,9},{11,8},{12,... | collective-permute-start | bytes 786440 | tf_op jit(solution)/shard_map/ppermute | solution.py:311

commit v7 on v6

--- a/solution.py
+++ b/solution.py
@@ -359,12 +359,12 @@
     q_r, g_r = move(q_give, sibling), move(g_give, sibling)
     acc = [shape(gq_block, f32)] * 2
     grad_scratch = [pltpu.VMEM(kv_block, f32)]
-    two_s, rows_s = lax.optimization_barrier((two_s, rows_s))
-    one_s = move(jnp.where(even, kv_s, two_s), beside)
-    sides = (q_s, g_s, rows_s, q_r, g_r)
     grad_s, gq_s = call(own_side_kernel, "own_side", [shape(kv_block, f32), acc[0]], flops=0)(
         kv_s, q_s, g_s, rows_s
     )
+    two_s, grad_s = lax.optimization_barrier((two_s, grad_s))
+    one_s = move(jnp.where(even, kv_s, two_s), beside)
+    sides = (q_s, g_s, rows_s, q_r, g_r)
     own_s, own_r, gq_s, gq_r = call(own_rest_kernel, "own_rest", [shape(kv_block, f32)] * 2 + acc, flops=0)(
         kv_s, kv_r, *sides, grad_s, gq_s
     )

time: 44.6 us -> 43.6 us (0.978)
  waiting for transfers between devices: 13.2 us -> 12.3 us
    ppermute x12, waiting for transfers between devices: 13.2 us -> 12.3 us  [move(): return lax.ppermute(x, AXIS, [(i, j) for i, j in pairs if j >= 0])]
  transfers between devices with their start and end apart: 12 -> 12, of which waited for: 3 -> 3; matrix products, arithmetic and copies ran while one was open for 0% -> 0% of each run, Pallas kernels for 24% -> 25%
where the time goes in v7:
time: 43.6 us; the launch traced here: 43.1 us
  starting transfers between devices  16.7 us (38%)
  Pallas kernels  13.2 us (30%)
  waiting for transfers between devices  12.3 us (28%)
  between operations  0.8 us (2%)
    ppermute x12, starting transfers between devices, move(): return lax.ppermute(x, AXIS, [(i, j) for i, j in pairs if j >= 0])  16.7 us
    ppermute x12, waiting for transfers between devices, move(): return lax.ppermute(x, AXIS, [(i, j) for i, j in pairs if j >= 0])  12.3 us
    pallas_call x1, Pallas kernels, shards(): call(pack_q_kernel, 'pack_q', [shape((half_rows, size), low), shape((half...  2.67 us
    pallas_call x1, Pallas kernels, shards(): call(own_rest_kernel, 'own_rest', [shape(kv_block, f32)] * 2 + acc, flops=0)  2.01 us
    pallas_call x1, Pallas kernels, shards(): near_r, gq_s, gq_r = near(name='near_r')(one_r, *sides, gq_s, gq_r)  1.89 us
    pallas_call x1, Pallas kernels, shards(): near_s, gq_s, gq_r = near(name='near_s')(one_s, *sides, gq_s, gq_r)  1.69 us
    pallas_call x1, Pallas kernels, shards(): call(final_kv_kernel, 'final_kv', [shape(key_rows.shape, low), shape(valu...  1.29 us
    pallas_call x1, Pallas kernels, shards(): call(pack_kv_kernel, 'pack_kv', [shape(kv_block, low)] * 2, [pltpu.VMEM(k...  1.27 us
  transfers between devices with their start and end apart: 12, of which 3 were waited for; matrix products, arithmetic and copies ran while one was open for 0% of the time, Pallas kernels for 25%

profile of v7, /device:TPU:3, one launch (start us, length us, event | category | flops | bytes accessed | tf_op | source)
XLA Modules:
  0.0 43.1 jit_solution(10280300071689211499)
XLA Ops:
  0.6 1.3 %pack_kv.1 = (bf16[4,256,128]{2,1,0:T(8,128)(2,1)S(1)}, bf16[4,256,128]{2,1,0:T(8,128)(2,1)S(1)}) custom-call(bf16[256,4,128]{2,1,0:T(4,128)(2,1)} %k_hbm.1, bf16[256,4,128]{2,1,0:T(4,128)(2,1)} %v_hbm.1), custom_call_target="tpu_custom_call" | custom-call | bytes 2097152 | tf_op jit(solution)/shard_map/pack_kv/pallas_call | solution.py:334
  1.9 0.7 %collective-permute-start.1 = (bf16[4,256,128]{2,1,0:T(8,128)(2,1)S(1)}, bf16[4,256,128]{2,1,0:T(8,128)(2,1)S(1)}, u32[]{:S(2)}, u32[]{:S(2)}) collective-permute-start(bf16[4,256,128]{2,1,0:T(8,128)(2,1)S(1)} %get-tuple-element.40), channel_id=1, source_target_pairs={{0,1},{1,0},{2,3},{3,2},{4,5},{5,4},{6,7},{7,6},{8,9},{9,8},{10,11... | collective-permute-start | bytes 786440 | tf_op jit(solution)/shard_map/ppermute | solution.py:311
  2.7 1.2 %collective-permute-start = (bf16[4,256,128]{2,1,0:T(8,128)(2,1)S(1)}, bf16[4,256,128]{2,1,0:T(8,128)(2,1)S(1)}, u32[]{:S(2)}, u32[]{:S(2)}) collective-permute-start(bf16[4,256,128]{2,1,0:T(8,128)(2,1)S(1)} %get-tuple-element.39.kv_s), channel_id=1, source_target_pairs={{0,4},{1,5},{2,6},{3,7},{4,8},{5,9},{6,10},{7,11},{8,12},{9,13},{1... | collective-permute-start | bytes 786440 | tf_op jit(solution)/shard_map/ppermute | solution.py:311
  3.9 0.0 collective-permute-done.1.after.kv_r
  3.9 2.7 %pack_q.1 = (bf16[1024,128]{1,0:T(8,128)(2,1)S(1)}, bf16[1024,128]{1,0:T(8,128)(2,1)S(1)}, f32[16,128]{1,0:T(8,128)S(1)}, bf16[1072,128]{1,0:T(8,128)(2,1)S(1)}, bf16[1024,128]{1,0:T(8,128)(2,1)S(1)}) custom-call(bf16[256,8,128]{2,1,0:T(8,128)(2,1)} %q_hbm.1, bf16[256,8,128]{2,1,0:T(8,128)(2,1)} %g_hbm.1, bf16[256,8,128]{2,1,0:T(8,128)(2,1)} %o_hbm.1, ...), custom_call_target="tpu_custom_call" | custom-call | bytes 2097152 | tf_op jit(solution)/shard_map/pack_q/pallas_call | solution.py:345
  6.6 0.4 collective-permute-start.2
  7.0 0.2 collective-permute-start.3
  7.2 1.2 %collective-permute-start.5 = (bf16[4,256,128]{2,1,0:T(8,128)(2,1)S(1)}, bf16[4,256,128]{2,1,0:T(8,128)(2,1)S(1)}, u32[]{:S(2)}, u32[]{:S(2)}) collective-permute-start(bf16[4,256,128]{2,1,0:T(8,128)(2,1)S(1)} %collective-permute-done.1.after.kv_r), channel_id=1, source_target_pairs={{0,4},{1,5},{2,6},{3,7},{4,8},{5,9},{6,10},{7,11},{8,12},{9,13},{1... | collective-permute-start | bytes 786440 | tf_op jit(solution)/shard_map/ppermute | solution.py:311
  8.4 0.9 %own_side.1 = (f32[4,256,128]{2,1,0:T(8,128)S(1)}, f32[2,512,128]{2,1,0:T(8,128)S(1)}) custom-call(bf16[4,256,128]{2,1,0:T(8,128)(2,1)S(1)} %get-tuple-element.39.kv_s, bf16[1024,128]{1,0:T(8,128)(2,1)S(1)} %get-tuple-element.41.q_s, bf16[1024,128]{1,0:T(8,128)(2,1)S(1)} %get-tuple-element.42.g_s, f32[16,128]{1,0:T(8,128)S(1)} %get-tuple-element.43.rows_s), custom_call_target="tpu_custom_call" | custom-call | bytes 2097152 | tf_op jit(solution)/shard_map/own_side/pallas_call | solution.py:362
  9.4 4.1 %collective-permute-done.kv = bf16[4,256,128]{2,1,0:T(8,128)(2,1)S(1)} collective-permute-done((bf16[4,256,128]{2,1,0:T(8,128)(2,1)S(1)}, bf16[4,256,128]{2,1,0:T(8,128)(2,1)S(1)}, u32[]{:S(2)}, u32[]{:S(2)}) %collective-permute-start) | collective-permute-done | bytes 262176 | tf_op jit(solution)/shard_map/ppermute | solution.py:311
  13.5 0.4 collective-permute-start.7
  13.9 0.0 collective-permute-done.3.g_r
  13.9 0.0 collective-permute-done.2.q_r
  13.9 2.0 %own_rest.1 = (f32[4,256,128]{2,1,0:T(8,128)S(1)}, f32[4,256,128]{2,1,0:T(8,128)S(1)}, f32[2,512,128]{2,1,0:T(8,128)S(1)}, f32[2,512,128]{2,1,0:T(8,128)S(1)}) custom-call(bf16[4,256,128]{2,1,0:T(8,128)(2,1)S(1)} %get-tuple-element.39.kv_s, bf16[4,256,128]{2,1,0:T(8,128)(2,1)S(1)} %collective-permute-done.1.after.kv_r, ...), custom_call_target="tpu_custom_call" | custom-call | bytes 2097152 | tf_op jit(solution)/shard_map/own_rest/pallas_call | solution.py:368
  15.9 0.1 far_s.1
  16.1 3.2 %collective-permute-start.4 = (bf16[4,256,128]{2,1,0:T(8,128)(2,1)S(1)}, bf16[4,256,128]{2,1,0:T(8,128)(2,1)S(1)}, u32[]{:S(2)}, u32[]{:S(2)}) collective-permute-start(bf16[4,256,128]{2,1,0:T(8,128)(2,1)S(1)} %get-tuple-element.52), channel_id=1, source_target_pairs={{0,28},{1,29},{2,30},{3,31},{4,0},{5,1},{6,2},{7,3},{8,4},{9,5},{1... | collective-permute-start | bytes 786440 | tf_op jit(solution)/shard_map/ppermute | solution.py:311
  19.3 1.3 %collective-permute-start.6 = (bf16[4,256,128]{2,1,0:T(8,128)(2,1)S(1)}, bf16[4,256,128]{2,1,0:T(8,128)(2,1)S(1)}, u32[]{:S(2)}, u32[]{:S(2)}) collective-permute-start(bf16[4,256,128]{2,1,0:T(8,128)(2,1)S(1)} %broadcast_select_fusion.1), channel_id=1, source_target_pairs={{0,2},{1,3},{2,0},{3,1},{4,6},{5,7},{6,4},{7,5},{8,10},{9,11},{10,... | collective-permute-start | bytes 786440 | tf_op jit(solution)/shard_map/ppermute | solution.py:311
  20.6 0.1 far_r.1
  20.7 4.1 %collective-permute-start.9 = (bf16[4,256,128]{2,1,0:T(8,128)(2,1)S(1)}, bf16[4,256,128]{2,1,0:T(8,128)(2,1)S(1)}, u32[]{:S(2)}, u32[]{:S(2)}) collective-permute-start(bf16[4,256,128]{2,1,0:T(8,128)(2,1)S(1)} %get-tuple-element.69), channel_id=1, source_target_pairs={{0,29},{1,28},{2,31},{3,30},{4,1},{5,0},{6,3},{7,2},{8,5},{9,4},{1... | collective-permute-start | bytes 786440 | tf_op jit(solution)/shard_map/ppermute | solution.py:311
  24.9 0.0 collective-permute-done.7.kv
  24.9 1.7 %near_s.1 = (bf16[4,256,128]{2,1,0:T(8,128)(2,1)S(1)}, f32[2,512,128]{2,1,0:T(8,128)S(1)}, f32[2,512,128]{2,1,0:T(8,128)S(1)}) custom-call(bf16[4,256,128]{2,1,0:T(8,128)(2,1)S(1)} %collective-permute-done.7.kv, bf16[1024,128]{1,0:T(8,128)(2,1)S(1)} %get-tuple-element.41.q_s, bf16[1024,128]{1,0:T(8,128)(2,1)S(1)} %get-tuple-element.42.g_s, ...), custom_call_target="tpu_custom_call" | custom-call | bytes 2097152 | tf_op jit(solution)/shard_map/near_s/pallas_call | solution.py:385
  26.6 1.9 %collective-permute-start.10 = (bf16[4,256,128]{2,1,0:T(8,128)(2,1)S(1)}, bf16[4,256,128]{2,1,0:T(8,128)(2,1)S(1)}, u32[]{:S(2)}, u32[]{:S(2)}) collective-permute-start(bf16[4,256,128]{2,1,0:T(8,128)(2,1)S(1)} %get-tuple-element.70), channel_id=1, source_target_pairs={{2,0},{3,1},{4,2},{5,3},{6,4},{7,5},{8,6},{9,7},{10,8},{11,9},{12,... | collective-permute-start | bytes 786440 | tf_op jit(solution)/shard_map/ppermute | solution.py:311
  28.5 0.0 collective-permute-done.4.back_ref
  28.5 1.9 %near_r.1 = (bf16[4,256,128]{2,1,0:T(8,128)(2,1)S(1)}, f32[2,512,128]{2,1,0:T(8,128)S(1)}, f32[2,512,128]{2,1,0:T(8,128)S(1)}) custom-call(bf16[4,256,128]{2,1,0:T(8,128)(2,1)S(1)} %collective-permute-done.6.kv, bf16[1024,128]{1,0:T(8,128)(2,1)S(1)} %get-tuple-element.41.q_s, bf16[1024,128]{1,0:T(8,128)(2,1)S(1)} %get-tuple-element.42.g_s, ...), custom_call_target="tpu_custom_call" | custom-call | bytes 2097152 | tf_op jit(solution)/shard_map/near_r/pallas_call | solution.py:388
  30.4 0.1 multiply_convert_fusion
  30.5 0.1 collective-permute-start.8
  30.6 1.9 %collective-permute-start.11 = (bf16[4,256,128]{2,1,0:T(8,128)(2,1)S(1)}, bf16[4,256,128]{2,1,0:T(8,128)(2,1)S(1)}, u32[]{:S(2)}, u32[]{:S(2)}) collective-permute-start(bf16[4,256,128]{2,1,0:T(8,128)(2,1)S(1)} %get-tuple-element.71), channel_id=1, source_target_pairs={{2,1},{3,0},{4,3},{5,2},{6,5},{7,4},{8,7},{9,6},{10,9},{11,8},{12,... | collective-permute-start | bytes 786440 | tf_op jit(solution)/shard_map/ppermute | solution.py:311
  32.6 0.0 collective-permute-done.8.got_ref
  32.6 1.1 %final_q.1 = (bf16[256,8,128]{2,1,0:T(8,128)(2,1)}, f32[8,128]{1,0:T(8,128)S(1)}) custom-call(f32[2,512,128]{2,1,0:T(8,128)S(1)} %get-tuple-element.63.own_ref, bf16[8,256,128]{2,1,0:T(8,128)(2,1)S(1)} %collective-permute-done.8.got_ref, f32[4,256,128]{2,1,0:T(8,128)S(1)} %partial.1.after.part_ref), custom_call_target="tpu_custom_call" | custom-call | bytes 2097152 | tf_op jit(solution)/shard_map/final_q/pallas_call | solution.py:394
  33.7 2.5 %collective-permute-done.10.side_s = bf16[4,256,128]{2,1,0:T(8,128)(2,1)S(1)} collective-permute-done((bf16[4,256,128]{2,1,0:T(8,128)(2,1)S(1)}, bf16[4,256,128]{2,1,0:T(8,128)(2,1)S(1)}, u32[]{:S(2)}, u32[]{:S(2)}) %collective-permute-start.10) | collective-permute-done | bytes 262176 | tf_op jit(solution)/shard_map/ppermute | solution.py:311
  36.2 5.6 %collective-permute-done.11.side_r = bf16[4,256,128]{2,1,0:T(8,128)(2,1)S(1)} collective-permute-done((bf16[4,256,128]{2,1,0:T(8,128)(2,1)S(1)}, bf16[4,256,128]{2,1,0:T(8,128)(2,1)S(1)}, u32[]{:S(2)}, u32[]{:S(2)}) %collective-permute-start.11) | collective-permute-done | bytes 262176 | tf_op jit(solution)/shard_map/ppermute | solution.py:311
  41.9 1.3 %final_kv.1 = (bf16[256,4,128]{2,1,0:T(4,128)(2,1)}, bf16[256,4,128]{2,1,0:T(4,128)(2,1)}) custom-call(f32[4,256,128]{2,1,0:T(8,128)S(1)} %partial.1.after.part_ref, bf16[8,256,128]{2,1,0:T(8,128)(2,1)S(1)} %collective-permute-done.8.got_ref, bf16[4,256,128]{2,1,0:T(8,128)(2,1)S(1)} %collective-permute-done.9.back_r, ...), custom_call_target="tpu_custom_call" | custom-call | bytes 2097152 | tf_op jit(solution)/shard_map/final_kv/pallas_call | solution.py:401
  (10 shorter events, 0.2 us)
Async XLA Ops:
  0.6 3.3 %copy-start = (f32[8,256]{1,0:T(8,128)S(1)}, f32[8,256]{1,0:T(8,128)}, u32[]{:S(2)}) copy-start(f32[8,256]{1,0:T(8,128)} %norm_ref.1) | copy-start | bytes 24580
  1.9 2.0 %collective-permute-start.1 = (bf16[4,256,128]{2,1,0:T(8,128)(2,1)S(1)}, bf16[4,256,128]{2,1,0:T(8,128)(2,1)S(1)}, u32[]{:S(2)}, u32[]{:S(2)}) collective-permute-start(bf16[4,256,128]{2,1,0:T(8,128)(2,1)S(1)} %get-tuple-element.40), channel_id=1, source_target_pairs={{0,1},{1,0},{2,3},{3,2},{4,5},{5,4},{6,7},{7,6},{8,9},{9,8},{10,11... | collective-permute-start | bytes 786440 | tf_op jit(solution)/shard_map/ppermute | solution.py:311
  2.7 10.8 %collective-permute-start = (bf16[4,256,128]{2,1,0:T(8,128)(2,1)S(1)}, bf16[4,256,128]{2,1,0:T(8,128)(2,1)S(1)}, u32[]{:S(2)}, u32[]{:S(2)}) collective-permute-start(bf16[4,256,128]{2,1,0:T(8,128)(2,1)S(1)} %get-tuple-element.39.kv_s), channel_id=1, source_target_pairs={{0,4},{1,5},{2,6},{3,7},{4,8},{5,9},{6,10},{7,11},{8,12},{9,13},{1... | collective-permute-start | bytes 786440 | tf_op jit(solution)/shard_map/ppermute | solution.py:311
  6.6 7.3 %collective-permute-start.2 = (bf16[1072,128]{1,0:T(8,128)(2,1)S(1)}, bf16[1072,128]{1,0:T(8,128)(2,1)S(1)}, u32[]{:S(2)}, u32[]{:S(2)}) collective-permute-start(bf16[1072,128]{1,0:T(8,128)(2,1)S(1)} %get-tuple-element.46), channel_id=1, source_target_pairs={{0,1},{1,0},{2,3},{3,2},{4,5},{5,4},{6,7},{7,6},{8,9},{9,8},{10,11... | collective-permute-start | bytes 823304 | tf_op jit(solution)/shard_map/ppermute | solution.py:311
  7.0 6.9 %collective-permute-start.3 = (bf16[1024,128]{1,0:T(8,128)(2,1)S(1)}, bf16[1024,128]{1,0:T(8,128)(2,1)S(1)}, u32[]{:S(2)}, u32[]{:S(2)}) collective-permute-start(bf16[1024,128]{1,0:T(8,128)(2,1)S(1)} %get-tuple-element.47), channel_id=1, source_target_pairs={{0,1},{1,0},{2,3},{3,2},{4,5},{5,4},{6,7},{7,6},{8,9},{9,8},{10,11... | collective-permute-start | bytes 786440 | tf_op jit(solution)/shard_map/ppermute | solution.py:311
  7.2 12.1 %collective-permute-start.5 = (bf16[4,256,128]{2,1,0:T(8,128)(2,1)S(1)}, bf16[4,256,128]{2,1,0:T(8,128)(2,1)S(1)}, u32[]{:S(2)}, u32[]{:S(2)}) collective-permute-start(bf16[4,256,128]{2,1,0:T(8,128)(2,1)S(1)} %collective-permute-done.1.after.kv_r), channel_id=1, source_target_pairs={{0,4},{1,5},{2,6},{3,7},{4,8},{5,9},{6,10},{7,11},{8,12},{9,13},{1... | collective-permute-start | bytes 786440 | tf_op jit(solution)/shard_map/ppermute | solution.py:311
  13.5 11.4 %collective-permute-start.7 = (bf16[4,256,128]{2,1,0:T(8,128)(2,1)S(1)}, bf16[4,256,128]{2,1,0:T(8,128)(2,1)S(1)}, u32[]{:S(2)}, u32[]{:S(2)}) collective-permute-start(bf16[4,256,128]{2,1,0:T(8,128)(2,1)S(1)} %broadcast_select_fusion), channel_id=1, source_target_pairs={{0,2},{1,3},{2,0},{3,1},{4,6},{5,7},{6,4},{7,5},{8,10},{9,11},{10,... | collective-permute-start | bytes 786440 | tf_op jit(solution)/shard_map/ppermute | solution.py:311
  16.1 12.4 %collective-permute-start.4 = (bf16[4,256,128]{2,1,0:T(8,128)(2,1)S(1)}, bf16[4,256,128]{2,1,0:T(8,128)(2,1)S(1)}, u32[]{:S(2)}, u32[]{:S(2)}) collective-permute-start(bf16[4,256,128]{2,1,0:T(8,128)(2,1)S(1)} %get-tuple-element.52), channel_id=1, source_target_pairs={{0,28},{1,29},{2,30},{3,31},{4,0},{5,1},{6,2},{7,3},{8,4},{9,5},{1... | collective-permute-start | bytes 786440 | tf_op jit(solution)/shard_map/ppermute | solution.py:311
  19.3 9.2 %collective-permute-start.6 = (bf16[4,256,128]{2,1,0:T(8,128)(2,1)S(1)}, bf16[4,256,128]{2,1,0:T(8,128)(2,1)S(1)}, u32[]{:S(2)}, u32[]{:S(2)}) collective-permute-start(bf16[4,256,128]{2,1,0:T(8,128)(2,1)S(1)} %broadcast_select_fusion.1), channel_id=1, source_target_pairs={{0,2},{1,3},{2,0},{3,1},{4,6},{5,7},{6,4},{7,5},{8,10},{9,11},{10,... | collective-permute-start | bytes 786440 | tf_op jit(solution)/shard_map/ppermute | solution.py:311
  20.7 13.0 %collective-permute-start.9 = (bf16[4,256,128]{2,1,0:T(8,128)(2,1)S(1)}, bf16[4,256,128]{2,1,0:T(8,128)(2,1)S(1)}, u32[]{:S(2)}, u32[]{:S(2)}) collective-permute-start(bf16[4,256,128]{2,1,0:T(8,128)(2,1)S(1)} %get-tuple-element.69), channel_id=1, source_target_pairs={{0,29},{1,28},{2,31},{3,30},{4,1},{5,0},{6,3},{7,2},{8,5},{9,4},{1... | collective-permute-start | bytes 786440 | tf_op jit(solution)/shard_map/ppermute | solution.py:311
  26.6 9.7 %collective-permute-start.10 = (bf16[4,256,128]{2,1,0:T(8,128)(2,1)S(1)}, bf16[4,256,128]{2,1,0:T(8,128)(2,1)S(1)}, u32[]{:S(2)}, u32[]{:S(2)}) collective-permute-start(bf16[4,256,128]{2,1,0:T(8,128)(2,1)S(1)} %get-tuple-element.70), channel_id=1, source_target_pairs={{2,0},{3,1},{4,2},{5,3},{6,4},{7,5},{8,6},{9,7},{10,8},{11,9},{12,... | collective-permute-start | bytes 786440 | tf_op jit(solution)/shard_map/ppermute | solution.py:311
  30.5 2.1 %collective-permute-start.8 = (bf16[8,256,128]{2,1,0:T(8,128)(2,1)S(1)}, bf16[8,256,128]{2,1,0:T(8,128)(2,1)S(1)}, u32[]{:S(2)}, u32[]{:S(2)}) collective-permute-start(bf16[8,256,128]{2,1,0:T(8,128)(2,1)S(1)} %pad_maximum_fusion), channel_id=1, source_target_pairs={{0,1},{1,0},{2,3},{3,2},{4,5},{5,4},{6,7},{7,6},{8,9},{9,8},{10,11... | collective-permute-start | bytes 1572872 | tf_op jit(solution)/shard_map/ppermute | solution.py:311
  30.6 11.2 %collective-permute-start.11 = (bf16[4,256,128]{2,1,0:T(8,128)(2,1)S(1)}, bf16[4,256,128]{2,1,0:T(8,128)(2,1)S(1)}, u32[]{:S(2)}, u32[]{:S(2)}) collective-permute-start(bf16[4,256,128]{2,1,0:T(8,128)(2,1)S(1)} %get-tuple-element.71), channel_id=1, source_target_pairs={{2,1},{3,0},{4,3},{5,2},{6,5},{7,4},{8,7},{9,6},{10,9},{11,8},{12,... | collective-permute-start | bytes 786440 | tf_op jit(solution)/shard_map/ppermute | solution.py:311

commit v8 on v7

--- a/solution.py
+++ b/solution.py
@@ -85,8 +85,10 @@
     keep_q,
     keep_g,
     keep_rows,
-    give_q,
-    give_g,
+    give_q0,
+    give_q1,
+    give_g0,
+    give_g1,
     q_ref,
     g_ref,
     o_ref,
@@ -99,29 +101,32 @@
     half = heads // 2
     pieces = rows // size
     core = lax.axis_index(AXIS) % 2
-    ones = jnp.ones((8, size), jnp.float32)
+    ones = jnp.ones((16, size), jnp.bfloat16)
     flat = wide.reshape(rows * heads, size)
 
     def spread(outs):
-        for out, side in zip(outs, (core, 1 - core), strict=True):
-            for j in range(half):
-                block = flat[pl.ds(side * half + j, rows, stride=heads), :]
-                out[j * rows : (j + 1) * rows] = block.astype(out.dtype)
+        keep, low, high = outs
+        for j in range(half):
+            block = flat[pl.ds(core * half + j, rows, stride=heads), :]
+            keep[j * rows : (j + 1) * rows] = block.astype(keep.dtype)
+            block = flat[pl.ds((1 - core) * half + j, rows, stride=heads), :]
+            out, at = (low, j) if j < half // 2 else (high, j - half // 2)
+            out[at * rows : (at + 1) * rows] = block.astype(out.dtype)
 
     copy_q.wait()
     wide[...] = q_ref[...].astype(jnp.float32)
-    spread((keep_q, give_q))
+    spread((keep_q, give_q0, give_q1))
     copy_g.wait()
     wide[...] = g_ref[...].astype(jnp.float32)
-    spread((keep_g, give_g))
+    spread((keep_g, give_g0, give_g1))
     copy_o.wait()
     wide[...] = g_ref[...].astype(jnp.float32) * o_ref[...].astype(jnp.float32)
     for out, side in ((keep_rows, core), (give_rows, 1 - core)):
         for j in range(half):
             product = flat[pl.ds(side * half + j, rows, stride=heads), :]
-            delta = lax.dot_general(
-                ones, product, NT, precision=lax.Precision.HIGHEST, preferred_element_type=jnp.float32
-            )
+            high = product.astype(jnp.bfloat16)
+            rest = (product - high.astype(jnp.float32)).astype(jnp.bfloat16)
+            delta = dot(ones, high, NT) + dot(ones, rest, NT)
             norm = norm_ref[pl.ds(side * half + j, 1), :] * LOG2E
             for n in range(pieces):
                 out[j * pieces + n : j * pieces + n + 1] = norm[:, n * size : (n + 1) * size]
@@ -129,7 +134,8 @@
                 out[at : at + 1] = delta[:1, n * size : (n + 1) * size]
     count = heads * pieces
     for n, part in enumerate(split_three(give_rows[...])):
-        give_q[half * rows + n * count : half * rows + (n + 1) * count] = part
+        start = half // 2 * rows + n * count
+        give_q0[start : start + count] = part
 
 
 def tile(kv_ref, side, grad_ref, gq_in, gq_ref, offset, first):
@@ -140,7 +146,7 @@
     share = span // rows
     pieces = span // size
     if row_ref is None:
-        vectors = join_three(q_ref, g_ref.shape[0], 2 * groups * pieces)
+        vectors = join_three(q_ref[0], g_ref[0].shape[0], 2 * groups * pieces)
     else:
         vectors = row_ref[...]
 
@@ -150,8 +156,11 @@
     for g in range(groups):
         k = kv_ref[g]
         v = kv_ref[groups + g]
-        q = q_ref[g * span : (g + 1) * span]
-        d = g_ref[g * span : (g + 1) * span]
+        if row_ref is None:
+            q, d = q_ref[g][:span], g_ref[g][...]
+        else:
+            q = q_ref[g * span : (g + 1) * span]
+            d = g_ref[g * span : (g + 1) * span]
         norm = vector(g * pieces)
         delta = vector((groups + g) * pieces)
         x = dot(k, q, NT) * (query_scale * LOG2E) - norm
@@ -186,8 +195,8 @@
     tile(kv_s, (q_s, g_s, rows_s), grad_s, None, gq_s, 0, True)
 
 
-def own_rest_kernel(kv_s, kv_r, q_s, g_s, rows_s, q_r, g_r, grad_s_in, gq_s_in, grad_s, grad_r, gq_s, gq_r):
-    side_s, side_r = (q_s, g_s, rows_s), (q_r, g_r, None)
+def own_rest_kernel(kv_s, kv_r, q_s, g_s, rows_s, q_r0, q_r1, g_r0, g_r1, grad_s_in, gq_s_in, grad_s, grad_r, gq_s, gq_r):
+    side_s, side_r = (q_s, g_s, rows_s), ((q_r0, q_r1), (g_r0, g_r1), None)
     core = lax.axis_index(AXIS) % 2
     grad_s[...] = grad_s_in[...]
     tile(kv_r, side_r, grad_r, None, gq_r, 0, True)
@@ -205,13 +214,13 @@
     scale_keys(grad_r)
 
 
-def far_kernel(first, kv, q_s, g_s, rows_s, q_r, g_r, *refs):
+def far_kernel(first, kv, q_s, g_s, rows_s, q_r0, q_r1, g_r0, g_r1, *refs):
     if first:
         gq_s_in, gq_r_in, out, gq_s, gq_r, grad = refs
-        side_s, side_r, seen_by = (q_s, g_s, rows_s), (q_r, g_r, None), 1
+        side_s, side_r, seen_by = (q_s, g_s, rows_s), ((q_r0, q_r1), (g_r0, g_r1), None), 1
     else:
         gq_r_in, gq_s_in, out, gq_r, gq_s, grad = refs
-        side_s, side_r, seen_by = (q_r, g_r, None), (q_s, g_s, rows_s), 0
+        side_s, side_r, seen_by = ((q_r0, q_r1), (g_r0, g_r1), None), (q_s, g_s, rows_s), 0
     device = lax.axis_index(AXIS)
     core = device % 2
     valid = device // 2 >= 2
@@ -239,8 +248,8 @@
         gq_r[...] = gq_r_in[...]
 
 
-def near_kernel(kv, q_s, g_s, rows_s, q_r, g_r, gq_s_in, gq_r_in, out, gq_s, gq_r, grad):
-    side_s, side_r = (q_s, g_s, rows_s), (q_r, g_r, None)
+def near_kernel(kv, q_s, g_s, rows_s, q_r0, q_r1, g_r0, g_r1, gq_s_in, gq_r_in, out, gq_s, gq_r, grad):
+    side_s, side_r = (q_s, g_s, rows_s), ((q_r0, q_r1), (g_r0, g_r1), None)
     valid = lax.axis_index(AXIS) // 2 >= 1
 
     @pl.when(valid)
@@ -342,32 +351,36 @@
     kv_r = move(kv_give, sibling)
     two_s = move(kv_s, ahead)
     two_r = move(kv_r, ahead)
-    q_s, g_s, rows_s, q_give, g_give = call(
+    q_s, g_s, rows_s, *gives = call(
         pack_q_kernel,
         "pack_q",
         [
             shape((half_rows, size), low),
             shape((half_rows, size), low),
             shape(row_block, f32),
-            shape((half_rows + 3 * row_block[0], size), low),
-            shape((half_rows, size), low),
+            shape((half_rows // 2 + 3 * row_block[0], size), low),
+            shape((half_rows // 2, size), low),
+            shape((half_rows // 2, size), low),
+            shape((half_rows // 2, size), low),
         ],
         [pltpu.VMEM(queries.shape, low)] * 3
         + [pltpu.VMEM((rows, heads, size), f32), pltpu.VMEM(row_block, f32), pltpu.SemaphoreType.DMA((3,))],
         in_specs=[hbm, hbm, hbm, vmem, anywhere],
     )(pin(queries), pin(grad_output), pin(attn_output), log_norm, kv_r)
-    q_r, g_r = move(q_give, sibling), move(g_give, sibling)
+    received = [move(x, sibling) for x in gives]
     acc = [shape(gq_block, f32)] * 2
     grad_scratch = [pltpu.VMEM(kv_block, f32)]
     grad_s, gq_s = call(own_side_kernel, "own_side", [shape(kv_block, f32), acc[0]], flops=0)(
         kv_s, q_s, g_s, rows_s
     )
-    two_s, grad_s = lax.optimization_barrier((two_s, grad_s))
-    one_s = move(jnp.where(even, kv_s, two_s), beside)
-    sides = (q_s, g_s, rows_s, q_r, g_r)
+    sides = (q_s, g_s, rows_s, *received)
     own_s, own_r, gq_s, gq_r = call(own_rest_kernel, "own_rest", [shape(kv_block, f32)] * 2 + acc, flops=0)(
         kv_s, kv_r, *sides, grad_s, gq_s
     )
+    two_s, gq_s, gq_r = lax.optimization_barrier((two_s, gq_s, gq_r))
+    send_s = jnp.where(even, kv_s, two_s)
+    one_s = move(send_s, beside)
+    gq_s, gq_r, send_s = lax.optimization_barrier((gq_s, gq_r, send_s))
     far_s, gq_s, gq_r = call(
         functools.partial(far_kernel, True), "far_s", [shape(kv_block, low)] + acc, grad_scratch
     )(two_s, *sides, gq_s, gq_r)

time: 43.6 us -> 43.3 us (level)
  Pallas kernels: 13.2 us -> 12.7 us
  waiting for transfers between devices: 12.3 us -> 12.8 us
    ppermute x12 -> x14, waiting for transfers between devices: 12.3 us -> 12.8 us  [move(): return lax.ppermute(x, AXIS, [(i, j) for i, j in pairs if j >= 0])]
    pallas_call x1, Pallas kernels: 2.67 us -> 2.22 us  [shards(): call(pack_q_kernel, 'pack_q', [shape((half_rows, size), low), shape((half...]
    ppermute x12 -> x14, starting transfers between devices: 16.7 us -> 16.6 us  [move(): return lax.ppermute(x, AXIS, [(i, j) for i, j in pairs if j >= 0])]
  transfers between devices with their start and end apart: 12 -> 14, of which waited for: 3 -> 4; matrix products, arithmetic and copies ran while one was open for 0% -> 0% of each run, Pallas kernels for 25% -> 24%
where the time goes in v8:
time: 43.3 us; the launch traced here: 43.1 us
  starting transfers between devices  16.6 us (38%)
  waiting for transfers between devices  12.8 us (30%)
  Pallas kernels  12.7 us (29%)
  between operations  0.8 us (2%)
    ppermute x14, starting transfers between devices, move(): return lax.ppermute(x, AXIS, [(i, j) for i, j in pairs if j >= 0])  16.6 us
    ppermute x14, waiting for transfers between devices, move(): return lax.ppermute(x, AXIS, [(i, j) for i, j in pairs if j >= 0])  12.8 us
    pallas_call x1, Pallas kernels, shards(): call(pack_q_kernel, 'pack_q', [shape((half_rows, size), low), shape((half...  2.22 us
    pallas_call x1, Pallas kernels, shards(): call(own_rest_kernel, 'own_rest', [shape(kv_block, f32)] * 2 + acc, flops=0)  2.01 us
    pallas_call x1, Pallas kernels, shards(): near_r, gq_s, gq_r = near(name='near_r')(one_r, *sides, gq_s, gq_r)  1.88 us
    pallas_call x1, Pallas kernels, shards(): near_s, gq_s, gq_r = near(name='near_s')(one_s, *sides, gq_s, gq_r)  1.69 us
    pallas_call x1, Pallas kernels, shards(): call(final_kv_kernel, 'final_kv', [shape(key_rows.shape, low), shape(valu...  1.29 us
    pallas_call x1, Pallas kernels, shards(): call(pack_kv_kernel, 'pack_kv', [shape(kv_block, low)] * 2, [pltpu.VMEM(k...  1.27 us
  transfers between devices with their start and end apart: 14, of which 4 were waited for; matrix products, arithmetic and copies ran while one was open for 0% of the time, Pallas kernels for 24%

profile of v8, /device:TPU:3, one launch (start us, length us, event | category | flops | bytes accessed | tf_op | source)
XLA Modules:
  0.0 43.1 jit_solution(16105624922010186332)
XLA Ops:
  0.6 1.3 %pack_kv.1 = (bf16[4,256,128]{2,1,0:T(8,128)(2,1)S(1)}, bf16[4,256,128]{2,1,0:T(8,128)(2,1)S(1)}) custom-call(bf16[256,4,128]{2,1,0:T(4,128)(2,1)} %k_hbm.1, bf16[256,4,128]{2,1,0:T(4,128)(2,1)} %v_hbm.1), custom_call_target="tpu_custom_call" | custom-call | bytes 2097152 | tf_op jit(solution)/shard_map/pack_kv/pallas_call | solution.py:343
  1.9 0.7 %collective-permute-start.1 = (bf16[4,256,128]{2,1,0:T(8,128)(2,1)S(1)}, bf16[4,256,128]{2,1,0:T(8,128)(2,1)S(1)}, u32[]{:S(2)}, u32[]{:S(2)}) collective-permute-start(bf16[4,256,128]{2,1,0:T(8,128)(2,1)S(1)} %get-tuple-element.45), channel_id=1, source_target_pairs={{0,1},{1,0},{2,3},{3,2},{4,5},{5,4},{6,7},{7,6},{8,9},{9,8},{10,11... | collective-permute-start | bytes 786440 | tf_op jit(solution)/shard_map/ppermute | solution.py:320
  2.7 1.2 %collective-permute-start = (bf16[4,256,128]{2,1,0:T(8,128)(2,1)S(1)}, bf16[4,256,128]{2,1,0:T(8,128)(2,1)S(1)}, u32[]{:S(2)}, u32[]{:S(2)}) collective-permute-start(bf16[4,256,128]{2,1,0:T(8,128)(2,1)S(1)} %get-tuple-element.44.kv_s), channel_id=1, source_target_pairs={{0,4},{1,5},{2,6},{3,7},{4,8},{5,9},{6,10},{7,11},{8,12},{9,13},{1... | collective-permute-start | bytes 786440 | tf_op jit(solution)/shard_map/ppermute | solution.py:320
  3.9 0.0 collective-permute-done.1.after.kv_r
  3.9 2.2 %pack_q.1 = (bf16[1024,128]{1,0:T(8,128)(2,1)S(1)}, bf16[1024,128]{1,0:T(8,128)(2,1)S(1)}, f32[16,128]{1,0:T(8,128)S(1)}, bf16[560,128]{1,0:T(8,128)(2,1)S(1)}, ...) custom-call(bf16[256,8,128]{2,1,0:T(8,128)(2,1)} %q_hbm.1, ...), custom_call_target="tpu_custom_call" | custom-call | bytes 2097152 | tf_op jit(solution)/shard_map/pack_q/pallas_call | solution.py:354
  6.1 0.4 collective-permute-start.3
  6.5 0.2 collective-permute-start.2
  6.7 0.3 collective-permute-start.4
  7.1 0.2 collective-permute-start.5
  7.2 0.3 collective-permute-done.3.q_r1
  7.5 1.2 %collective-permute-start.7 = (bf16[4,256,128]{2,1,0:T(8,128)(2,1)S(1)}, bf16[4,256,128]{2,1,0:T(8,128)(2,1)S(1)}, u32[]{:S(2)}, u32[]{:S(2)}) collective-permute-start(bf16[4,256,128]{2,1,0:T(8,128)(2,1)S(1)} %collective-permute-done.1.after.kv_r), channel_id=1, source_target_pairs={{0,4},{1,5},{2,6},{3,7},{4,8},{5,9},{6,10},{7,11},{8,12},{9,13},{1... | collective-permute-start | bytes 786440 | tf_op jit(solution)/shard_map/ppermute | solution.py:320
  8.8 0.9 %own_side.1 = (f32[4,256,128]{2,1,0:T(8,128)S(1)}, f32[2,512,128]{2,1,0:T(8,128)S(1)}) custom-call(bf16[4,256,128]{2,1,0:T(8,128)(2,1)S(1)} %get-tuple-element.44.kv_s, bf16[1024,128]{1,0:T(8,128)(2,1)S(1)} %get-tuple-element.46.q_s, bf16[1024,128]{1,0:T(8,128)(2,1)S(1)} %get-tuple-element.47.g_s, f32[16,128]{1,0:T(8,128)S(1)} %get-tuple-element.48.rows_s), custom_call_target="tpu_custom_call" | custom-call | bytes 2097152 | tf_op jit(solution)/shard_map/own_side/pallas_call | solution.py:373
  9.8 0.0 collective-permute-done.2.q_r0
  9.8 2.0 %own_rest.1 = (f32[4,256,128]{2,1,0:T(8,128)S(1)}, f32[4,256,128]{2,1,0:T(8,128)S(1)}, f32[2,512,128]{2,1,0:T(8,128)S(1)}, f32[2,512,128]{2,1,0:T(8,128)S(1)}) custom-call(bf16[4,256,128]{2,1,0:T(8,128)(2,1)S(1)} %get-tuple-element.44.kv_s, bf16[4,256,128]{2,1,0:T(8,128)(2,1)S(1)} %collective-permute-done.1.after.kv_r, ...), custom_call_target="tpu_custom_call" | custom-call | bytes 2097152 | tf_op jit(solution)/shard_map/own_rest/pallas_call | solution.py:377
  11.8 1.7 %collective-permute-done.kv = bf16[4,256,128]{2,1,0:T(8,128)(2,1)S(1)} collective-permute-done((bf16[4,256,128]{2,1,0:T(8,128)(2,1)S(1)}, bf16[4,256,128]{2,1,0:T(8,128)(2,1)S(1)}, u32[]{:S(2)}, u32[]{:S(2)}) %collective-permute-start) | collective-permute-done | bytes 262176 | tf_op jit(solution)/shard_map/ppermute | solution.py:320
  13.5 0.4 collective-permute-start.9
  13.9 0.1 far_s.1
  14.0 3.2 %collective-permute-start.6 = (bf16[4,256,128]{2,1,0:T(8,128)(2,1)S(1)}, bf16[4,256,128]{2,1,0:T(8,128)(2,1)S(1)}, u32[]{:S(2)}, u32[]{:S(2)}) collective-permute-start(bf16[4,256,128]{2,1,0:T(8,128)(2,1)S(1)} %get-tuple-element.62), channel_id=1, source_target_pairs={{0,28},{1,29},{2,30},{3,31},{4,0},{5,1},{6,2},{7,3},{8,4},{9,5},{1... | collective-permute-start | bytes 786440 | tf_op jit(solution)/shard_map/ppermute | solution.py:320
  17.2 1.9 %collective-permute-done.7.kv = bf16[4,256,128]{2,1,0:T(8,128)(2,1)S(1)} collective-permute-done((bf16[4,256,128]{2,1,0:T(8,128)(2,1)S(1)}, bf16[4,256,128]{2,1,0:T(8,128)(2,1)S(1)}, u32[]{:S(2)}, u32[]{:S(2)}) %collective-permute-start.7) | collective-permute-done | bytes 262176 | tf_op jit(solution)/shard_map/ppermute | solution.py:320
  19.1 0.4 collective-permute-start.8
  19.6 0.1 far_r.1
  19.7 4.2 %collective-permute-start.11 = (bf16[4,256,128]{2,1,0:T(8,128)(2,1)S(1)}, bf16[4,256,128]{2,1,0:T(8,128)(2,1)S(1)}, u32[]{:S(2)}, u32[]{:S(2)}) collective-permute-start(bf16[4,256,128]{2,1,0:T(8,128)(2,1)S(1)} %get-tuple-element.79), channel_id=1, source_target_pairs={{0,29},{1,28},{2,31},{3,30},{4,1},{5,0},{6,3},{7,2},{8,5},{9,4},{1... | collective-permute-start | bytes 786440 | tf_op jit(solution)/shard_map/ppermute | solution.py:320
  23.9 1.7 %near_s.1 = (bf16[4,256,128]{2,1,0:T(8,128)(2,1)S(1)}, f32[2,512,128]{2,1,0:T(8,128)S(1)}, f32[2,512,128]{2,1,0:T(8,128)S(1)}) custom-call(bf16[4,256,128]{2,1,0:T(8,128)(2,1)S(1)} %collective-permute-done.9.kv, bf16[1024,128]{1,0:T(8,128)(2,1)S(1)} %get-tuple-element.46.q_s, bf16[1024,128]{1,0:T(8,128)(2,1)S(1)} %get-tuple-element.47.g_s, ...), custom_call_target="tpu_custom_call" | custom-call | bytes 2097152 | tf_op jit(solution)/shard_map/near_s/pallas_call | solution.py:398
  25.6 1.9 %collective-permute-start.12 = (bf16[4,256,128]{2,1,0:T(8,128)(2,1)S(1)}, bf16[4,256,128]{2,1,0:T(8,128)(2,1)S(1)}, u32[]{:S(2)}, u32[]{:S(2)}) collective-permute-start(bf16[4,256,128]{2,1,0:T(8,128)(2,1)S(1)} %get-tuple-element.80), channel_id=1, source_target_pairs={{2,0},{3,1},{4,2},{5,3},{6,4},{7,5},{8,6},{9,7},{10,8},{11,9},{12,... | collective-permute-start | bytes 786440 | tf_op jit(solution)/shard_map/ppermute | solution.py:320
  27.5 1.9 %near_r.1 = (bf16[4,256,128]{2,1,0:T(8,128)(2,1)S(1)}, f32[2,512,128]{2,1,0:T(8,128)S(1)}, f32[2,512,128]{2,1,0:T(8,128)S(1)}) custom-call(bf16[4,256,128]{2,1,0:T(8,128)(2,1)S(1)} %collective-permute-done.8.kv, bf16[1024,128]{1,0:T(8,128)(2,1)S(1)} %get-tuple-element.46.q_s, bf16[1024,128]{1,0:T(8,128)(2,1)S(1)} %get-tuple-element.47.g_s, ...), custom_call_target="tpu_custom_call" | custom-call | bytes 2097152 | tf_op jit(solution)/shard_map/near_r/pallas_call | solution.py:401
  29.4 0.1 multiply_convert_fusion
  29.6 0.2 collective-permute-start.10
  29.8 1.9 %collective-permute-start.13 = (bf16[4,256,128]{2,1,0:T(8,128)(2,1)S(1)}, bf16[4,256,128]{2,1,0:T(8,128)(2,1)S(1)}, u32[]{:S(2)}, u32[]{:S(2)}) collective-permute-start(bf16[4,256,128]{2,1,0:T(8,128)(2,1)S(1)} %get-tuple-element.81), channel_id=1, source_target_pairs={{2,1},{3,0},{4,3},{5,2},{6,5},{7,4},{8,7},{9,6},{10,9},{11,8},{12,... | collective-permute-start | bytes 786440 | tf_op jit(solution)/shard_map/ppermute | solution.py:320
  31.7 0.1 partial.1.after.part_ref
  31.8 1.1 %final_q.1 = (bf16[256,8,128]{2,1,0:T(8,128)(2,1)}, f32[8,128]{1,0:T(8,128)S(1)}) custom-call(f32[2,512,128]{2,1,0:T(8,128)S(1)} %get-tuple-element.73.own_ref, bf16[8,256,128]{2,1,0:T(8,128)(2,1)S(1)} %collective-permute-done.10.got_ref, f32[4,256,128]{2,1,0:T(8,128)S(1)} %partial.1.after.part_ref), custom_call_target="tpu_custom_call" | custom-call | bytes 2097152 | tf_op jit(solution)/shard_map/final_q/pallas_call | solution.py:407
  32.9 8.9 %collective-permute-done.11.back_r = bf16[4,256,128]{2,1,0:T(8,128)(2,1)S(1)} collective-permute-done((bf16[4,256,128]{2,1,0:T(8,128)(2,1)S(1)}, bf16[4,256,128]{2,1,0:T(8,128)(2,1)S(1)}, u32[]{:S(2)}, u32[]{:S(2)}) %collective-permute-start.11) | collective-permute-done | bytes 262176 | tf_op jit(solution)/shard_map/ppermute | solution.py:320
  41.8 1.3 %final_kv.1 = (bf16[256,4,128]{2,1,0:T(4,128)(2,1)}, bf16[256,4,128]{2,1,0:T(4,128)(2,1)}) custom-call(f32[4,256,128]{2,1,0:T(8,128)S(1)} %partial.1.after.part_ref, bf16[8,256,128]{2,1,0:T(8,128)(2,1)S(1)} %collective-permute-done.10.got_ref, bf16[4,256,128]{2,1,0:T(8,128)(2,1)S(1)} %collective-permute-done.11.back_r, ...), custom_call_target="tpu_custom_call" | custom-call | bytes 2097152 | tf_op jit(solution)/shard_map/final_kv/pallas_call | solution.py:414
  (14 shorter events, 0.2 us)
Async XLA Ops:
  0.6 3.3 %copy-start = (f32[8,256]{1,0:T(8,128)S(1)}, f32[8,256]{1,0:T(8,128)}, u32[]{:S(2)}) copy-start(f32[8,256]{1,0:T(8,128)} %norm_ref.1) | copy-start | bytes 24580
  1.9 2.0 %collective-permute-start.1 = (bf16[4,256,128]{2,1,0:T(8,128)(2,1)S(1)}, bf16[4,256,128]{2,1,0:T(8,128)(2,1)S(1)}, u32[]{:S(2)}, u32[]{:S(2)}) collective-permute-start(bf16[4,256,128]{2,1,0:T(8,128)(2,1)S(1)} %get-tuple-element.45), channel_id=1, source_target_pairs={{0,1},{1,0},{2,3},{3,2},{4,5},{5,4},{6,7},{7,6},{8,9},{9,8},{10,11... | collective-permute-start | bytes 786440 | tf_op jit(solution)/shard_map/ppermute | solution.py:320
  2.7 10.8 %collective-permute-start = (bf16[4,256,128]{2,1,0:T(8,128)(2,1)S(1)}, bf16[4,256,128]{2,1,0:T(8,128)(2,1)S(1)}, u32[]{:S(2)}, u32[]{:S(2)}) collective-permute-start(bf16[4,256,128]{2,1,0:T(8,128)(2,1)S(1)} %get-tuple-element.44.kv_s), channel_id=1, source_target_pairs={{0,4},{1,5},{2,6},{3,7},{4,8},{5,9},{6,10},{7,11},{8,12},{9,13},{1... | collective-permute-start | bytes 786440 | tf_op jit(solution)/shard_map/ppermute | solution.py:320
  6.1 1.4 %collective-permute-start.3 = (bf16[512,128]{1,0:T(8,128)(2,1)S(1)}, bf16[512,128]{1,0:T(8,128)(2,1)S(1)}, u32[]{:S(2)}, u32[]{:S(2)}) collective-permute-start(bf16[512,128]{1,0:T(8,128)(2,1)S(1)} %get-tuple-element.50), channel_id=1, source_target_pairs={{0,1},{1,0},{2,3},{3,2},{4,5},{5,4},{6,7},{7,6},{8,9},{9,8},{10,11... | collective-permute-start | bytes 393224 | tf_op jit(solution)/shard_map/ppermute | solution.py:320
  6.5 3.2 %collective-permute-start.2 = (bf16[560,128]{1,0:T(8,128)(2,1)S(1)}, bf16[560,128]{1,0:T(8,128)(2,1)S(1)}, u32[]{:S(2)}, u32[]{:S(2)}) collective-permute-start(bf16[560,128]{1,0:T(8,128)(2,1)S(1)} %get-tuple-element.49), channel_id=1, source_target_pairs={{0,1},{1,0},{2,3},{3,2},{4,5},{5,4},{6,7},{7,6},{8,9},{9,8},{10,11... | collective-permute-start | bytes 430088 | tf_op jit(solution)/shard_map/ppermute | solution.py:320
  6.7 3.0 %collective-permute-start.4 = (bf16[512,128]{1,0:T(8,128)(2,1)S(1)}, bf16[512,128]{1,0:T(8,128)(2,1)S(1)}, u32[]{:S(2)}, u32[]{:S(2)}) collective-permute-start(bf16[512,128]{1,0:T(8,128)(2,1)S(1)} %get-tuple-element.51), channel_id=1, source_target_pairs={{0,1},{1,0},{2,3},{3,2},{4,5},{5,4},{6,7},{7,6},{8,9},{9,8},{10,11... | collective-permute-start | bytes 393224 | tf_op jit(solution)/shard_map/ppermute | solution.py:320
  7.1 2.7 %collective-permute-start.5 = (bf16[512,128]{1,0:T(8,128)(2,1)S(1)}, bf16[512,128]{1,0:T(8,128)(2,1)S(1)}, u32[]{:S(2)}, u32[]{:S(2)}) collective-permute-start(bf16[512,128]{1,0:T(8,128)(2,1)S(1)} %get-tuple-element.52), channel_id=1, source_target_pairs={{0,1},{1,0},{2,3},{3,2},{4,5},{5,4},{6,7},{7,6},{8,9},{9,8},{10,11... | collective-permute-start | bytes 393224 | tf_op jit(solution)/shard_map/ppermute | solution.py:320
  7.5 11.5 %collective-permute-start.7 = (bf16[4,256,128]{2,1,0:T(8,128)(2,1)S(1)}, bf16[4,256,128]{2,1,0:T(8,128)(2,1)S(1)}, u32[]{:S(2)}, u32[]{:S(2)}) collective-permute-start(bf16[4,256,128]{2,1,0:T(8,128)(2,1)S(1)} %collective-permute-done.1.after.kv_r), channel_id=1, source_target_pairs={{0,4},{1,5},{2,6},{3,7},{4,8},{5,9},{6,10},{7,11},{8,12},{9,13},{1... | collective-permute-start | bytes 786440 | tf_op jit(solution)/shard_map/ppermute | solution.py:320
  13.5 10.4 %collective-permute-start.9 = (bf16[4,256,128]{2,1,0:T(8,128)(2,1)S(1)}, bf16[4,256,128]{2,1,0:T(8,128)(2,1)S(1)}, u32[]{:S(2)}, u32[]{:S(2)}) collective-permute-start(bf16[4,256,128]{2,1,0:T(8,128)(2,1)S(1)} %broadcast_select_fusion.1), channel_id=1, source_target_pairs={{0,2},{1,3},{2,0},{3,1},{4,6},{5,7},{6,4},{7,5},{8,10},{9,11},{10,... | collective-permute-start | bytes 786440 | tf_op jit(solution)/shard_map/ppermute | solution.py:320
  14.0 13.5 %collective-permute-start.6 = (bf16[4,256,128]{2,1,0:T(8,128)(2,1)S(1)}, bf16[4,256,128]{2,1,0:T(8,128)(2,1)S(1)}, u32[]{:S(2)}, u32[]{:S(2)}) collective-permute-start(bf16[4,256,128]{2,1,0:T(8,128)(2,1)S(1)} %get-tuple-element.62), channel_id=1, source_target_pairs={{0,28},{1,29},{2,30},{3,31},{4,0},{5,1},{6,2},{7,3},{8,4},{9,5},{1... | collective-permute-start | bytes 786440 | tf_op jit(solution)/shard_map/ppermute | solution.py:320
  19.1 8.4 %collective-permute-start.8 = (bf16[4,256,128]{2,1,0:T(8,128)(2,1)S(1)}, bf16[4,256,128]{2,1,0:T(8,128)(2,1)S(1)}, u32[]{:S(2)}, u32[]{:S(2)}) collective-permute-start(bf16[4,256,128]{2,1,0:T(8,128)(2,1)S(1)} %broadcast_select_fusion), channel_id=1, source_target_pairs={{0,2},{1,3},{2,0},{3,1},{4,6},{5,7},{6,4},{7,5},{8,10},{9,11},{10,... | collective-permute-start | bytes 786440 | tf_op jit(solution)/shard_map/ppermute | solution.py:320
  19.7 22.1 %collective-permute-start.11 = (bf16[4,256,128]{2,1,0:T(8,128)(2,1)S(1)}, bf16[4,256,128]{2,1,0:T(8,128)(2,1)S(1)}, u32[]{:S(2)}, u32[]{:S(2)}) collective-permute-start(bf16[4,256,128]{2,1,0:T(8,128)(2,1)S(1)} %get-tuple-element.79), channel_id=1, source_target_pairs={{0,29},{1,28},{2,31},{3,30},{4,1},{5,0},{6,3},{7,2},{8,5},{9,4},{1... | collective-permute-start | bytes 786440 | tf_op jit(solution)/shard_map/ppermute | solution.py:320
  25.6 16.2 %collective-permute-start.12 = (bf16[4,256,128]{2,1,0:T(8,128)(2,1)S(1)}, bf16[4,256,128]{2,1,0:T(8,128)(2,1)S(1)}, u32[]{:S(2)}, u32[]{:S(2)}) collective-permute-start(bf16[4,256,128]{2,1,0:T(8,128)(2,1)S(1)} %get-tuple-element.80), channel_id=1, source_target_pairs={{2,0},{3,1},{4,2},{5,3},{6,4},{7,5},{8,6},{9,7},{10,8},{11,9},{12,... | collective-permute-start | bytes 786440 | tf_op jit(solution)/shard_map/ppermute | solution.py:320
  29.6 2.2 %collective-permute-start.10 = (bf16[8,256,128]{2,1,0:T(8,128)(2,1)S(1)}, bf16[8,256,128]{2,1,0:T(8,128)(2,1)S(1)}, u32[]{:S(2)}, u32[]{:S(2)}) collective-permute-start(bf16[8,256,128]{2,1,0:T(8,128)(2,1)S(1)} %pad_maximum_fusion), channel_id=1, source_target_pairs={{0,1},{1,0},{2,3},{3,2},{4,5},{5,4},{6,7},{7,6},{8,9},{9,8},{10,11... | collective-permute-start | bytes 1572872 | tf_op jit(solution)/shard_map/ppermute | solution.py:320
  29.8 12.0 %collective-permute-start.13 = (bf16[4,256,128]{2,1,0:T(8,128)(2,1)S(1)}, bf16[4,256,128]{2,1,0:T(8,128)(2,1)S(1)}, u32[]{:S(2)}, u32[]{:S(2)}) collective-permute-start(bf16[4,256,128]{2,1,0:T(8,128)(2,1)S(1)} %get-tuple-element.81), channel_id=1, source_target_pairs={{2,1},{3,0},{4,3},{5,2},{6,5},{7,4},{8,7},{9,6},{10,9},{11,8},{12,... | collective-permute-start | bytes 786440 | tf_op jit(solution)/shard_map/ppermute | solution.py:320

commit v9 on v8

--- a/solution.py
+++ b/solution.py
@@ -399,7 +399,7 @@
     side_s = move(near_s, lambda i: i - 2)
     back_s, one_r = lax.optimization_barrier((back_s, one_r))
     near_r, gq_s, gq_r = near(name="near_r")(one_r, *sides, gq_s, gq_r)
-    side_r = move(near_r, lambda i: sibling(i - 2) if i >= 2 else -1)
+    side_r = move(near_r, lambda i: sibling((i - 2) % devices))
 
     part = call(partial_kernel, "partial", shape(kv_block, f32), flops=LONG)(own_s, back_s)
     give = jnp.concatenate([own_r.astype(low), (gq_r * query_scale).astype(low).reshape(-1, rows, size)])

time: 43.3 us -> 43.3 us (level)
  starting transfers between devices: 16.6 us -> 14.6 us
  waiting for transfers between devices: 12.8 us -> 14.7 us
    ppermute x14, waiting for transfers between devices: 12.8 us -> 14.7 us  [move(): return lax.ppermute(x, AXIS, [(i, j) for i, j in pairs if j >= 0])]
    ppermute x14, starting transfers between devices: 16.6 us -> 14.6 us  [move(): return lax.ppermute(x, AXIS, [(i, j) for i, j in pairs if j >= 0])]
  transfers between devices with their start and end apart: 14 -> 14, of which waited for: 4 -> 5; matrix products, arithmetic and copies ran while one was open for 0% -> 0% of each run, Pallas kernels for 24% -> 24%
where the time goes in v9:
time: 43.3 us; the launch traced here: 43.1 us
  waiting for transfers between devices  14.7 us (34%)
  starting transfers between devices  14.6 us (34%)
  Pallas kernels  12.7 us (29%)
  between operations  0.79 us (2%)
    ppermute x14, waiting for transfers between devices, move(): return lax.ppermute(x, AXIS, [(i, j) for i, j in pairs if j >= 0])  14.7 us
    ppermute x14, starting transfers between devices, move(): return lax.ppermute(x, AXIS, [(i, j) for i, j in pairs if j >= 0])  14.6 us
    pallas_call x1, Pallas kernels, shards(): call(pack_q_kernel, 'pack_q', [shape((half_rows, size), low), shape((half...  2.22 us
    pallas_call x1, Pallas kernels, shards(): call(own_rest_kernel, 'own_rest', [shape(kv_block, f32)] * 2 + acc, flops=0)  2.01 us
    pallas_call x1, Pallas kernels, shards(): near_r, gq_s, gq_r = near(name='near_r')(one_r, *sides, gq_s, gq_r)  1.88 us
    pallas_call x1, Pallas kernels, shards(): near_s, gq_s, gq_r = near(name='near_s')(one_s, *sides, gq_s, gq_r)  1.69 us
    pallas_call x1, Pallas kernels, shards(): call(final_kv_kernel, 'final_kv', [shape(key_rows.shape, low), shape(valu...  1.29 us
    pallas_call x1, Pallas kernels, shards(): call(pack_kv_kernel, 'pack_kv', [shape(kv_block, low)] * 2, [pltpu.VMEM(k...  1.27 us
  transfers between devices with their start and end apart: 14, of which 5 were waited for; matrix products, arithmetic and copies ran while one was open for 0% of the time, Pallas kernels for 24%

profile of v9, /device:TPU:3, one launch (start us, length us, event | category | flops | bytes accessed | tf_op | source)
XLA Modules:
  0.0 43.1 jit_solution(18419588658119909200)
XLA Ops:
  0.6 1.3 %pack_kv.1 = (bf16[4,256,128]{2,1,0:T(8,128)(2,1)S(1)}, bf16[4,256,128]{2,1,0:T(8,128)(2,1)S(1)}) custom-call(bf16[256,4,128]{2,1,0:T(4,128)(2,1)} %k_hbm.1, bf16[256,4,128]{2,1,0:T(4,128)(2,1)} %v_hbm.1), custom_call_target="tpu_custom_call" | custom-call | bytes 2097152 | tf_op jit(solution)/shard_map/pack_kv/pallas_call | solution.py:343
  1.9 0.7 %collective-permute-start.1 = (bf16[4,256,128]{2,1,0:T(8,128)(2,1)S(1)}, bf16[4,256,128]{2,1,0:T(8,128)(2,1)S(1)}, u32[]{:S(2)}, u32[]{:S(2)}) collective-permute-start(bf16[4,256,128]{2,1,0:T(8,128)(2,1)S(1)} %get-tuple-element.45), channel_id=1, source_target_pairs={{0,1},{1,0},{2,3},{3,2},{4,5},{5,4},{6,7},{7,6},{8,9},{9,8},{10,11... | collective-permute-start | bytes 786440 | tf_op jit(solution)/shard_map/ppermute | solution.py:320
  2.7 1.2 %collective-permute-start = (bf16[4,256,128]{2,1,0:T(8,128)(2,1)S(1)}, bf16[4,256,128]{2,1,0:T(8,128)(2,1)S(1)}, u32[]{:S(2)}, u32[]{:S(2)}) collective-permute-start(bf16[4,256,128]{2,1,0:T(8,128)(2,1)S(1)} %get-tuple-element.44.kv_s), channel_id=1, source_target_pairs={{0,4},{1,5},{2,6},{3,7},{4,8},{5,9},{6,10},{7,11},{8,12},{9,13},{1... | collective-permute-start | bytes 786440 | tf_op jit(solution)/shard_map/ppermute | solution.py:320
  3.9 0.0 collective-permute-done.1.after.kv_r
  3.9 2.2 %pack_q.1 = (bf16[1024,128]{1,0:T(8,128)(2,1)S(1)}, bf16[1024,128]{1,0:T(8,128)(2,1)S(1)}, f32[16,128]{1,0:T(8,128)S(1)}, bf16[560,128]{1,0:T(8,128)(2,1)S(1)}, ...) custom-call(bf16[256,8,128]{2,1,0:T(8,128)(2,1)} %q_hbm.1, ...), custom_call_target="tpu_custom_call" | custom-call | bytes 2097152 | tf_op jit(solution)/shard_map/pack_q/pallas_call | solution.py:354
  6.1 0.4 collective-permute-start.3
  6.5 0.2 collective-permute-start.2
  6.7 0.3 collective-permute-start.4
  7.1 0.2 collective-permute-start.5
  7.2 0.3 collective-permute-done.3.q_r1
  7.5 1.2 %collective-permute-start.7 = (bf16[4,256,128]{2,1,0:T(8,128)(2,1)S(1)}, bf16[4,256,128]{2,1,0:T(8,128)(2,1)S(1)}, u32[]{:S(2)}, u32[]{:S(2)}) collective-permute-start(bf16[4,256,128]{2,1,0:T(8,128)(2,1)S(1)} %collective-permute-done.1.after.kv_r), channel_id=1, source_target_pairs={{0,4},{1,5},{2,6},{3,7},{4,8},{5,9},{6,10},{7,11},{8,12},{9,13},{1... | collective-permute-start | bytes 786440 | tf_op jit(solution)/shard_map/ppermute | solution.py:320
  8.8 0.9 %own_side.1 = (f32[4,256,128]{2,1,0:T(8,128)S(1)}, f32[2,512,128]{2,1,0:T(8,128)S(1)}) custom-call(bf16[4,256,128]{2,1,0:T(8,128)(2,1)S(1)} %get-tuple-element.44.kv_s, bf16[1024,128]{1,0:T(8,128)(2,1)S(1)} %get-tuple-element.46.q_s, bf16[1024,128]{1,0:T(8,128)(2,1)S(1)} %get-tuple-element.47.g_s, f32[16,128]{1,0:T(8,128)S(1)} %get-tuple-element.48.rows_s), custom_call_target="tpu_custom_call" | custom-call | bytes 2097152 | tf_op jit(solution)/shard_map/own_side/pallas_call | solution.py:373
  9.8 0.0 collective-permute-done.2.q_r0
  9.8 2.0 %own_rest.1 = (f32[4,256,128]{2,1,0:T(8,128)S(1)}, f32[4,256,128]{2,1,0:T(8,128)S(1)}, f32[2,512,128]{2,1,0:T(8,128)S(1)}, f32[2,512,128]{2,1,0:T(8,128)S(1)}) custom-call(bf16[4,256,128]{2,1,0:T(8,128)(2,1)S(1)} %get-tuple-element.44.kv_s, bf16[4,256,128]{2,1,0:T(8,128)(2,1)S(1)} %collective-permute-done.1.after.kv_r, ...), custom_call_target="tpu_custom_call" | custom-call | bytes 2097152 | tf_op jit(solution)/shard_map/own_rest/pallas_call | solution.py:377
  11.8 1.7 %collective-permute-done.kv = bf16[4,256,128]{2,1,0:T(8,128)(2,1)S(1)} collective-permute-done((bf16[4,256,128]{2,1,0:T(8,128)(2,1)S(1)}, bf16[4,256,128]{2,1,0:T(8,128)(2,1)S(1)}, u32[]{:S(2)}, u32[]{:S(2)}) %collective-permute-start) | collective-permute-done | bytes 262176 | tf_op jit(solution)/shard_map/ppermute | solution.py:320
  13.5 0.4 collective-permute-start.9
  13.9 0.1 far_s.1
  14.0 3.2 %collective-permute-start.6 = (bf16[4,256,128]{2,1,0:T(8,128)(2,1)S(1)}, bf16[4,256,128]{2,1,0:T(8,128)(2,1)S(1)}, u32[]{:S(2)}, u32[]{:S(2)}) collective-permute-start(bf16[4,256,128]{2,1,0:T(8,128)(2,1)S(1)} %get-tuple-element.62), channel_id=1, source_target_pairs={{0,28},{1,29},{2,30},{3,31},{4,0},{5,1},{6,2},{7,3},{8,4},{9,5},{1... | collective-permute-start | bytes 786440 | tf_op jit(solution)/shard_map/ppermute | solution.py:320
  17.2 1.9 %collective-permute-done.7.kv = bf16[4,256,128]{2,1,0:T(8,128)(2,1)S(1)} collective-permute-done((bf16[4,256,128]{2,1,0:T(8,128)(2,1)S(1)}, bf16[4,256,128]{2,1,0:T(8,128)(2,1)S(1)}, u32[]{:S(2)}, u32[]{:S(2)}) %collective-permute-start.7) | collective-permute-done | bytes 262176 | tf_op jit(solution)/shard_map/ppermute | solution.py:320
  19.1 0.4 collective-permute-start.8
  19.6 0.1 far_r.1
  19.7 4.2 %collective-permute-start.11 = (bf16[4,256,128]{2,1,0:T(8,128)(2,1)S(1)}, bf16[4,256,128]{2,1,0:T(8,128)(2,1)S(1)}, u32[]{:S(2)}, u32[]{:S(2)}) collective-permute-start(bf16[4,256,128]{2,1,0:T(8,128)(2,1)S(1)} %get-tuple-element.79), channel_id=1, source_target_pairs={{0,29},{1,28},{2,31},{3,30},{4,1},{5,0},{6,3},{7,2},{8,5},{9,4},{1... | collective-permute-start | bytes 786440 | tf_op jit(solution)/shard_map/ppermute | solution.py:320
  23.9 1.7 %near_s.1 = (bf16[4,256,128]{2,1,0:T(8,128)(2,1)S(1)}, f32[2,512,128]{2,1,0:T(8,128)S(1)}, f32[2,512,128]{2,1,0:T(8,128)S(1)}) custom-call(bf16[4,256,128]{2,1,0:T(8,128)(2,1)S(1)} %collective-permute-done.9.kv, bf16[1024,128]{1,0:T(8,128)(2,1)S(1)} %get-tuple-element.46.q_s, bf16[1024,128]{1,0:T(8,128)(2,1)S(1)} %get-tuple-element.47.g_s, ...), custom_call_target="tpu_custom_call" | custom-call | bytes 2097152 | tf_op jit(solution)/shard_map/near_s/pallas_call | solution.py:398
  25.6 1.9 %collective-permute-start.12 = (bf16[4,256,128]{2,1,0:T(8,128)(2,1)S(1)}, bf16[4,256,128]{2,1,0:T(8,128)(2,1)S(1)}, u32[]{:S(2)}, u32[]{:S(2)}) collective-permute-start(bf16[4,256,128]{2,1,0:T(8,128)(2,1)S(1)} %get-tuple-element.80), channel_id=1, source_target_pairs={{2,0},{3,1},{4,2},{5,3},{6,4},{7,5},{8,6},{9,7},{10,8},{11,9},{12,... | collective-permute-start | bytes 786440 | tf_op jit(solution)/shard_map/ppermute | solution.py:320
  27.5 1.9 %near_r.1 = (bf16[4,256,128]{2,1,0:T(8,128)(2,1)S(1)}, f32[2,512,128]{2,1,0:T(8,128)S(1)}, f32[2,512,128]{2,1,0:T(8,128)S(1)}) custom-call(bf16[4,256,128]{2,1,0:T(8,128)(2,1)S(1)} %collective-permute-done.8.kv, bf16[1024,128]{1,0:T(8,128)(2,1)S(1)} %get-tuple-element.46.q_s, bf16[1024,128]{1,0:T(8,128)(2,1)S(1)} %get-tuple-element.47.g_s, ...), custom_call_target="tpu_custom_call" | custom-call | bytes 2097152 | tf_op jit(solution)/shard_map/near_r/pallas_call | solution.py:401
  29.4 0.1 multiply_convert_fusion
  29.6 0.2 collective-permute-start.10
  29.8 0.1 partial.1.after.part_ref
  29.9 1.7 %collective-permute-done.10.got_ref = bf16[8,256,128]{2,1,0:T(8,128)(2,1)S(1)} collective-permute-done((bf16[8,256,128]{2,1,0:T(8,128)(2,1)S(1)}, bf16[8,256,128]{2,1,0:T(8,128)(2,1)S(1)}, u32[]{:S(2)}, u32[]{:S(2)}) %collective-permute-start.10) | collective-permute-done | bytes 524320 | tf_op jit(solution)/shard_map/ppermute | solution.py:320
  31.5 1.1 %final_q.1 = (bf16[256,8,128]{2,1,0:T(8,128)(2,1)}, f32[8,128]{1,0:T(8,128)S(1)}) custom-call(f32[2,512,128]{2,1,0:T(8,128)S(1)} %get-tuple-element.73.own_ref, bf16[8,256,128]{2,1,0:T(8,128)(2,1)S(1)} %collective-permute-done.10.got_ref, f32[4,256,128]{2,1,0:T(8,128)S(1)} %partial.1.after.part_ref), custom_call_target="tpu_custom_call" | custom-call | bytes 2097152 | tf_op jit(solution)/shard_map/final_q/pallas_call | solution.py:407
  32.7 9.1 %collective-permute-done.11.back_r = bf16[4,256,128]{2,1,0:T(8,128)(2,1)S(1)} collective-permute-done((bf16[4,256,128]{2,1,0:T(8,128)(2,1)S(1)}, bf16[4,256,128]{2,1,0:T(8,128)(2,1)S(1)}, u32[]{:S(2)}, u32[]{:S(2)}) %collective-permute-start.11) | collective-permute-done | bytes 262176 | tf_op jit(solution)/shard_map/ppermute | solution.py:320
  41.8 1.3 %final_kv.1 = (bf16[256,4,128]{2,1,0:T(4,128)(2,1)}, bf16[256,4,128]{2,1,0:T(4,128)(2,1)}) custom-call(f32[4,256,128]{2,1,0:T(8,128)S(1)} %partial.1.after.part_ref, bf16[8,256,128]{2,1,0:T(8,128)(2,1)S(1)} %collective-permute-done.10.got_ref, bf16[4,256,128]{2,1,0:T(8,128)(2,1)S(1)} %collective-permute-done.11.back_r, ...), custom_call_target="tpu_custom_call" | custom-call | bytes 2097152 | tf_op jit(solution)/shard_map/final_kv/pallas_call | solution.py:414
  (14 shorter events, 0.2 us)
Async XLA Ops:
  0.6 3.3 %copy-start = (f32[8,256]{1,0:T(8,128)S(1)}, f32[8,256]{1,0:T(8,128)}, u32[]{:S(2)}) copy-start(f32[8,256]{1,0:T(8,128)} %norm_ref.1) | copy-start | bytes 24580
  1.9 2.0 %collective-permute-start.1 = (bf16[4,256,128]{2,1,0:T(8,128)(2,1)S(1)}, bf16[4,256,128]{2,1,0:T(8,128)(2,1)S(1)}, u32[]{:S(2)}, u32[]{:S(2)}) collective-permute-start(bf16[4,256,128]{2,1,0:T(8,128)(2,1)S(1)} %get-tuple-element.45), channel_id=1, source_target_pairs={{0,1},{1,0},{2,3},{3,2},{4,5},{5,4},{6,7},{7,6},{8,9},{9,8},{10,11... | collective-permute-start | bytes 786440 | tf_op jit(solution)/shard_map/ppermute | solution.py:320
  2.7 10.8 %collective-permute-start = (bf16[4,256,128]{2,1,0:T(8,128)(2,1)S(1)}, bf16[4,256,128]{2,1,0:T(8,128)(2,1)S(1)}, u32[]{:S(2)}, u32[]{:S(2)}) collective-permute-start(bf16[4,256,128]{2,1,0:T(8,128)(2,1)S(1)} %get-tuple-element.44.kv_s), channel_id=1, source_target_pairs={{0,4},{1,5},{2,6},{3,7},{4,8},{5,9},{6,10},{7,11},{8,12},{9,13},{1... | collective-permute-start | bytes 786440 | tf_op jit(solution)/shard_map/ppermute | solution.py:320
  6.1 1.4 %collective-permute-start.3 = (bf16[512,128]{1,0:T(8,128)(2,1)S(1)}, bf16[512,128]{1,0:T(8,128)(2,1)S(1)}, u32[]{:S(2)}, u32[]{:S(2)}) collective-permute-start(bf16[512,128]{1,0:T(8,128)(2,1)S(1)} %get-tuple-element.50), channel_id=1, source_target_pairs={{0,1},{1,0},{2,3},{3,2},{4,5},{5,4},{6,7},{7,6},{8,9},{9,8},{10,11... | collective-permute-start | bytes 393224 | tf_op jit(solution)/shard_map/ppermute | solution.py:320
  6.5 3.2 %collective-permute-start.2 = (bf16[560,128]{1,0:T(8,128)(2,1)S(1)}, bf16[560,128]{1,0:T(8,128)(2,1)S(1)}, u32[]{:S(2)}, u32[]{:S(2)}) collective-permute-start(bf16[560,128]{1,0:T(8,128)(2,1)S(1)} %get-tuple-element.49), channel_id=1, source_target_pairs={{0,1},{1,0},{2,3},{3,2},{4,5},{5,4},{6,7},{7,6},{8,9},{9,8},{10,11... | collective-permute-start | bytes 430088 | tf_op jit(solution)/shard_map/ppermute | solution.py:320
  6.7 3.0 %collective-permute-start.4 = (bf16[512,128]{1,0:T(8,128)(2,1)S(1)}, bf16[512,128]{1,0:T(8,128)(2,1)S(1)}, u32[]{:S(2)}, u32[]{:S(2)}) collective-permute-start(bf16[512,128]{1,0:T(8,128)(2,1)S(1)} %get-tuple-element.51), channel_id=1, source_target_pairs={{0,1},{1,0},{2,3},{3,2},{4,5},{5,4},{6,7},{7,6},{8,9},{9,8},{10,11... | collective-permute-start | bytes 393224 | tf_op jit(solution)/shard_map/ppermute | solution.py:320
  7.1 2.7 %collective-permute-start.5 = (bf16[512,128]{1,0:T(8,128)(2,1)S(1)}, bf16[512,128]{1,0:T(8,128)(2,1)S(1)}, u32[]{:S(2)}, u32[]{:S(2)}) collective-permute-start(bf16[512,128]{1,0:T(8,128)(2,1)S(1)} %get-tuple-element.52), channel_id=1, source_target_pairs={{0,1},{1,0},{2,3},{3,2},{4,5},{5,4},{6,7},{7,6},{8,9},{9,8},{10,11... | collective-permute-start | bytes 393224 | tf_op jit(solution)/shard_map/ppermute | solution.py:320
  7.5 11.5 %collective-permute-start.7 = (bf16[4,256,128]{2,1,0:T(8,128)(2,1)S(1)}, bf16[4,256,128]{2,1,0:T(8,128)(2,1)S(1)}, u32[]{:S(2)}, u32[]{:S(2)}) collective-permute-start(bf16[4,256,128]{2,1,0:T(8,128)(2,1)S(1)} %collective-permute-done.1.after.kv_r), channel_id=1, source_target_pairs={{0,4},{1,5},{2,6},{3,7},{4,8},{5,9},{6,10},{7,11},{8,12},{9,13},{1... | collective-permute-start | bytes 786440 | tf_op jit(solution)/shard_map/ppermute | solution.py:320
  13.5 10.4 %collective-permute-start.9 = (bf16[4,256,128]{2,1,0:T(8,128)(2,1)S(1)}, bf16[4,256,128]{2,1,0:T(8,128)(2,1)S(1)}, u32[]{:S(2)}, u32[]{:S(2)}) collective-permute-start(bf16[4,256,128]{2,1,0:T(8,128)(2,1)S(1)} %broadcast_select_fusion.1), channel_id=1, source_target_pairs={{0,2},{1,3},{2,0},{3,1},{4,6},{5,7},{6,4},{7,5},{8,10},{9,11},{10,... | collective-permute-start | bytes 786440 | tf_op jit(solution)/shard_map/ppermute | solution.py:320
  14.0 13.5 %collective-permute-start.6 = (bf16[4,256,128]{2,1,0:T(8,128)(2,1)S(1)}, bf16[4,256,128]{2,1,0:T(8,128)(2,1)S(1)}, u32[]{:S(2)}, u32[]{:S(2)}) collective-permute-start(bf16[4,256,128]{2,1,0:T(8,128)(2,1)S(1)} %get-tuple-element.62), channel_id=1, source_target_pairs={{0,28},{1,29},{2,30},{3,31},{4,0},{5,1},{6,2},{7,3},{8,4},{9,5},{1... | collective-permute-start | bytes 786440 | tf_op jit(solution)/shard_map/ppermute | solution.py:320
  19.1 8.4 %collective-permute-start.8 = (bf16[4,256,128]{2,1,0:T(8,128)(2,1)S(1)}, bf16[4,256,128]{2,1,0:T(8,128)(2,1)S(1)}, u32[]{:S(2)}, u32[]{:S(2)}) collective-permute-start(bf16[4,256,128]{2,1,0:T(8,128)(2,1)S(1)} %broadcast_select_fusion), channel_id=1, source_target_pairs={{0,2},{1,3},{2,0},{3,1},{4,6},{5,7},{6,4},{7,5},{8,10},{9,11},{10,... | collective-permute-start | bytes 786440 | tf_op jit(solution)/shard_map/ppermute | solution.py:320
  19.7 22.1 %collective-permute-start.11 = (bf16[4,256,128]{2,1,0:T(8,128)(2,1)S(1)}, bf16[4,256,128]{2,1,0:T(8,128)(2,1)S(1)}, u32[]{:S(2)}, u32[]{:S(2)}) collective-permute-start(bf16[4,256,128]{2,1,0:T(8,128)(2,1)S(1)} %get-tuple-element.79), channel_id=1, source_target_pairs={{0,29},{1,28},{2,31},{3,30},{4,1},{5,0},{6,3},{7,2},{8,5},{9,4},{1... | collective-permute-start | bytes 786440 | tf_op jit(solution)/shard_map/ppermute | solution.py:320
  25.6 16.2 %collective-permute-start.12 = (bf16[4,256,128]{2,1,0:T(8,128)(2,1)S(1)}, bf16[4,256,128]{2,1,0:T(8,128)(2,1)S(1)}, u32[]{:S(2)}, u32[]{:S(2)}) collective-permute-start(bf16[4,256,128]{2,1,0:T(8,128)(2,1)S(1)} %get-tuple-element.80), channel_id=1, source_target_pairs={{2,0},{3,1},{4,2},{5,3},{6,4},{7,5},{8,6},{9,7},{10,8},{11,9},{12,... | collective-permute-start | bytes 786440 | tf_op jit(solution)/shard_map/ppermute | solution.py:320
  29.6 2.0 %collective-permute-start.10 = (bf16[8,256,128]{2,1,0:T(8,128)(2,1)S(1)}, bf16[8,256,128]{2,1,0:T(8,128)(2,1)S(1)}, u32[]{:S(2)}, u32[]{:S(2)}) collective-permute-start(bf16[8,256,128]{2,1,0:T(8,128)(2,1)S(1)} %pad_maximum_fusion), channel_id=1, source_target_pairs={{0,1},{1,0},{2,3},{3,2},{4,5},{5,4},{6,7},{7,6},{8,9},{9,8},{10,11... | collective-permute-start | bytes 1572872 | tf_op jit(solution)/shard_map/ppermute | solution.py:320
  29.8 12.0 %collective-permute-start.13 = (bf16[4,256,128]{2,1,0:T(8,128)(2,1)S(1)}, bf16[4,256,128]{2,1,0:T(8,128)(2,1)S(1)}, u32[]{:S(2)}, u32[]{:S(2)}) collective-permute-start(bf16[4,256,128]{2,1,0:T(8,128)(2,1)S(1)} %get-tuple-element.81), channel_id=1, source_target_pairs={{0,31},{1,30},{2,1},{3,0},{4,3},{5,2},{6,5},{7,4},{8,7},{9,6},{10,... | collective-permute-start | bytes 786440 | tf_op jit(solution)/shard_map/ppermute | solution.py:320

commit v10 on v9

--- a/solution.py
+++ b/solution.py
@@ -15,6 +15,7 @@
 AXIS = "seq"
 VMEM_LIMIT = 16 * 1024 * 1024
 LONG = 10**10
+CHUNKS = 2
 
 NT = (((1,), (1,)), ((), ()))
 NN = (((1,), (0,)), ((), ()))
@@ -25,8 +26,7 @@
     return lax.dot_general(a, b, dims, preferred_element_type=jnp.float32)
 
 
-def call(kernel, name, out_shape, scratch=(), flops=0, in_specs=None):
-    specs = {} if in_specs is None else {"in_specs": in_specs}
+def call(kernel, name, out_shape, scratch=(), flops=0, **specs):
     return pl.pallas_call(
         kernel,
         out_shape=out_shape,
@@ -285,24 +285,33 @@
     out_ref[...] = own_ref[...] + back_ref[...].astype(jnp.float32)
 
 
-def final_kv_kernel(part_ref, got_ref, back_r, side_s, side_r, after, out_k, out_v, wide):
+def final_kv_kernel(part_ref, got_ref, back_r, side_s, side_r, after, hbm_k, hbm_v, out_k, out_v, wide, sems):
     rows, heads, size = out_k.shape
     half = heads // 2
     core = lax.axis_index(AXIS) % 2
     flat = wide.reshape(rows * 2 * heads, size)
-    for part in range(2):
-        for j in range(half):
-            n = part * half + j
-            flat[pl.ds(part * heads + core * half + j, rows, stride=2 * heads), :] = part_ref[n] + side_s[n].astype(
-                jnp.float32
-            )
-            flat[pl.ds(part * heads + (1 - core) * half + j, rows, stride=2 * heads), :] = (
-                got_ref[n].astype(jnp.float32)
-                + back_r[n].astype(jnp.float32)
-                + side_r[n].astype(jnp.float32)
-            )
-    out_k[...] = wide[:, :heads, :].astype(out_k.dtype)
-    out_v[...] = wide[:, heads:, :].astype(out_v.dtype)
+    chunk = rows // CHUNKS
+    copies = []
+    for c in range(CHUNKS):
+        span = slice(c * chunk, (c + 1) * chunk)
+        first = c * chunk * 2 * heads
+        for part in range(2):
+            for j in range(half):
+                n = part * half + j
+                own = part_ref[n, span] + side_s[n, span].astype(jnp.float32)
+                flat[pl.ds(first + part * heads + core * half + j, chunk, stride=2 * heads), :] = own
+                other = (
+                    got_ref[n, span].astype(jnp.float32)
+                    + back_r[n, span].astype(jnp.float32)
+                    + side_r[n, span].astype(jnp.float32)
+                )
+                flat[pl.ds(first + part * heads + (1 - core) * half + j, chunk, stride=2 * heads), :] = other
+        out_k[span] = wide[span, :heads, :].astype(out_k.dtype)
+        out_v[span] = wide[span, heads:, :].astype(out_v.dtype)
+        pairs = ((out_k.at[span], hbm_k.at[span]), (out_v.at[span], hbm_v.at[span]))
+        copies += fetch(pairs, sems.at[c])
+    for copy in copies:
+        copy.wait()
 
 
 def shards(queries, key_rows, value_rows, attn_output, grad_output, log_norm):
@@ -415,8 +424,10 @@
         final_kv_kernel,
         "final_kv",
         [shape(key_rows.shape, low), shape(value_rows.shape, low)],
-        [pltpu.VMEM((rows, 2 * groups, size), f32)],
+        [pltpu.VMEM(key_rows.shape, low)] * 2
+        + [pltpu.VMEM((rows, 2 * groups, size), f32), pltpu.SemaphoreType.DMA((CHUNKS, 2))],
         in_specs=[vmem] * 5 + [anywhere],
+        out_specs=[hbm, hbm],
     )(part, got, back_r, side_s, side_r, token)
     return grad_q, grad_k, grad_v
 

time: 43.3 us -> 43.4 us (level)
  no operation moved by 1% of the time
where the time goes in v10:
time: 43.4 us; the launch traced here: 43.2 us
  waiting for transfers between devices  14.7 us (34%)
  starting transfers between devices  14.6 us (34%)
  Pallas kernels  12.7 us (29%)
  between operations  0.95 us (2%)
    ppermute x14, waiting for transfers between devices, move(): return lax.ppermute(x, AXIS, [(i, j) for i, j in pairs if j >= 0])  14.7 us
    ppermute x14, starting transfers between devices, move(): return lax.ppermute(x, AXIS, [(i, j) for i, j in pairs if j >= 0])  14.6 us
    pallas_call x1, Pallas kernels, shards(): call(pack_q_kernel, 'pack_q', [shape((half_rows, size), low), shape((half...  2.22 us
    pallas_call x1, Pallas kernels, shards(): call(own_rest_kernel, 'own_rest', [shape(kv_block, f32)] * 2 + acc, flops=0)  2.01 us
    pallas_call x1, Pallas kernels, shards(): near_r, gq_s, gq_r = near(name='near_r')(one_r, *sides, gq_s, gq_r)  1.88 us
    pallas_call x1, Pallas kernels, shards(): near_s, gq_s, gq_r = near(name='near_s')(one_s, *sides, gq_s, gq_r)  1.69 us
    pallas_call x1, Pallas kernels, shards(): call(pack_kv_kernel, 'pack_kv', [shape(kv_block, low)] * 2, [pltpu.VMEM(k...  1.27 us
    pallas_call x1, Pallas kernels, shards(): call(final_kv_kernel, 'final_kv', [shape(key_rows.shape, low), shape(valu...  1.22 us
  transfers between devices with their start and end apart: 14, of which 5 were waited for; matrix products, arithmetic and copies ran while one was open for 0% of the time, Pallas kernels for 24%

profile of v10, /device:TPU:3, one launch (start us, length us, event | category | flops | bytes accessed | tf_op | source)
XLA Modules:
  0.0 43.2 jit_solution(13091926426494949536)
XLA Ops:
  0.6 1.3 %pack_kv.1 = (bf16[4,256,128]{2,1,0:T(8,128)(2,1)S(1)}, bf16[4,256,128]{2,1,0:T(8,128)(2,1)S(1)}) custom-call(bf16[256,4,128]{2,1,0:T(4,128)(2,1)} %k_hbm.1, bf16[256,4,128]{2,1,0:T(4,128)(2,1)} %v_hbm.1), custom_call_target="tpu_custom_call" | custom-call | bytes 2097152 | tf_op jit(solution)/shard_map/pack_kv/pallas_call | solution.py:352
  1.9 0.7 %collective-permute-start.1 = (bf16[4,256,128]{2,1,0:T(8,128)(2,1)S(1)}, bf16[4,256,128]{2,1,0:T(8,128)(2,1)S(1)}, u32[]{:S(2)}, u32[]{:S(2)}) collective-permute-start(bf16[4,256,128]{2,1,0:T(8,128)(2,1)S(1)} %get-tuple-element.45), channel_id=1, source_target_pairs={{0,1},{1,0},{2,3},{3,2},{4,5},{5,4},{6,7},{7,6},{8,9},{9,8},{10,11... | collective-permute-start | bytes 786440 | tf_op jit(solution)/shard_map/ppermute | solution.py:329
  2.7 1.2 %collective-permute-start = (bf16[4,256,128]{2,1,0:T(8,128)(2,1)S(1)}, bf16[4,256,128]{2,1,0:T(8,128)(2,1)S(1)}, u32[]{:S(2)}, u32[]{:S(2)}) collective-permute-start(bf16[4,256,128]{2,1,0:T(8,128)(2,1)S(1)} %get-tuple-element.44.kv_s), channel_id=1, source_target_pairs={{0,4},{1,5},{2,6},{3,7},{4,8},{5,9},{6,10},{7,11},{8,12},{9,13},{1... | collective-permute-start | bytes 786440 | tf_op jit(solution)/shard_map/ppermute | solution.py:329
  3.9 2.2 %pack_q.1 = (bf16[1024,128]{1,0:T(8,128)(2,1)S(1)}, bf16[1024,128]{1,0:T(8,128)(2,1)S(1)}, f32[16,128]{1,0:T(8,128)S(1)}, bf16[560,128]{1,0:T(8,128)(2,1)S(1)}, ...) custom-call(bf16[256,8,128]{2,1,0:T(8,128)(2,1)} %q_hbm.1, ...), custom_call_target="tpu_custom_call" | custom-call | bytes 2097152 | tf_op jit(solution)/shard_map/pack_q/pallas_call | solution.py:363
  6.1 0.4 collective-permute-start.3
  6.5 0.2 collective-permute-start.2
  6.7 0.3 collective-permute-start.4
  7.1 0.2 collective-permute-start.5
  7.2 0.3 collective-permute-done.3.q_r1
  7.5 1.2 %collective-permute-start.7 = (bf16[4,256,128]{2,1,0:T(8,128)(2,1)S(1)}, bf16[4,256,128]{2,1,0:T(8,128)(2,1)S(1)}, u32[]{:S(2)}, u32[]{:S(2)}) collective-permute-start(bf16[4,256,128]{2,1,0:T(8,128)(2,1)S(1)} %collective-permute-done.1.after.kv_r), channel_id=1, source_target_pairs={{0,4},{1,5},{2,6},{3,7},{4,8},{5,9},{6,10},{7,11},{8,12},{9,13},{1... | collective-permute-start | bytes 786440 | tf_op jit(solution)/shard_map/ppermute | solution.py:329
  8.8 0.9 %own_side.1 = (f32[4,256,128]{2,1,0:T(8,128)S(1)}, f32[2,512,128]{2,1,0:T(8,128)S(1)}) custom-call(bf16[4,256,128]{2,1,0:T(8,128)(2,1)S(1)} %get-tuple-element.44.kv_s, bf16[1024,128]{1,0:T(8,128)(2,1)S(1)} %get-tuple-element.46.q_s, bf16[1024,128]{1,0:T(8,128)(2,1)S(1)} %get-tuple-element.47.g_s, f32[16,128]{1,0:T(8,128)S(1)} %get-tuple-element.48.rows_s), custom_call_target="tpu_custom_call" | custom-call | bytes 2097152 | tf_op jit(solution)/shard_map/own_side/pallas_call | solution.py:382
  9.7 0.0 collective-permute-done.4.g_r0
  9.8 2.0 %own_rest.1 = (f32[4,256,128]{2,1,0:T(8,128)S(1)}, f32[4,256,128]{2,1,0:T(8,128)S(1)}, f32[2,512,128]{2,1,0:T(8,128)S(1)}, f32[2,512,128]{2,1,0:T(8,128)S(1)}) custom-call(bf16[4,256,128]{2,1,0:T(8,128)(2,1)S(1)} %get-tuple-element.44.kv_s, bf16[4,256,128]{2,1,0:T(8,128)(2,1)S(1)} %collective-permute-done.1.after.kv_r, ...), custom_call_target="tpu_custom_call" | custom-call | bytes 2097152 | tf_op jit(solution)/shard_map/own_rest/pallas_call | solution.py:386
  11.8 1.7 %collective-permute-done.kv = bf16[4,256,128]{2,1,0:T(8,128)(2,1)S(1)} collective-permute-done((bf16[4,256,128]{2,1,0:T(8,128)(2,1)S(1)}, bf16[4,256,128]{2,1,0:T(8,128)(2,1)S(1)}, u32[]{:S(2)}, u32[]{:S(2)}) %collective-permute-start) | collective-permute-done | bytes 262176 | tf_op jit(solution)/shard_map/ppermute | solution.py:329
  13.5 0.4 collective-permute-start.9
  13.9 0.1 far_s.1
  14.0 3.2 %collective-permute-start.6 = (bf16[4,256,128]{2,1,0:T(8,128)(2,1)S(1)}, bf16[4,256,128]{2,1,0:T(8,128)(2,1)S(1)}, u32[]{:S(2)}, u32[]{:S(2)}) collective-permute-start(bf16[4,256,128]{2,1,0:T(8,128)(2,1)S(1)} %get-tuple-element.62), channel_id=1, source_target_pairs={{0,28},{1,29},{2,30},{3,31},{4,0},{5,1},{6,2},{7,3},{8,4},{9,5},{1... | collective-permute-start | bytes 786440 | tf_op jit(solution)/shard_map/ppermute | solution.py:329
  17.2 1.9 %collective-permute-done.7.kv = bf16[4,256,128]{2,1,0:T(8,128)(2,1)S(1)} collective-permute-done((bf16[4,256,128]{2,1,0:T(8,128)(2,1)S(1)}, bf16[4,256,128]{2,1,0:T(8,128)(2,1)S(1)}, u32[]{:S(2)}, u32[]{:S(2)}) %collective-permute-start.7) | collective-permute-done | bytes 262176 | tf_op jit(solution)/shard_map/ppermute | solution.py:329
  19.1 0.4 collective-permute-start.8
  19.6 0.1 far_r.1
  19.7 4.2 %collective-permute-start.11 = (bf16[4,256,128]{2,1,0:T(8,128)(2,1)S(1)}, bf16[4,256,128]{2,1,0:T(8,128)(2,1)S(1)}, u32[]{:S(2)}, u32[]{:S(2)}) collective-permute-start(bf16[4,256,128]{2,1,0:T(8,128)(2,1)S(1)} %get-tuple-element.79), channel_id=1, source_target_pairs={{0,29},{1,28},{2,31},{3,30},{4,1},{5,0},{6,3},{7,2},{8,5},{9,4},{1... | collective-permute-start | bytes 786440 | tf_op jit(solution)/shard_map/ppermute | solution.py:329
  23.9 1.7 %near_s.1 = (bf16[4,256,128]{2,1,0:T(8,128)(2,1)S(1)}, f32[2,512,128]{2,1,0:T(8,128)S(1)}, f32[2,512,128]{2,1,0:T(8,128)S(1)}) custom-call(bf16[4,256,128]{2,1,0:T(8,128)(2,1)S(1)} %collective-permute-done.9.kv, bf16[1024,128]{1,0:T(8,128)(2,1)S(1)} %get-tuple-element.46.q_s, bf16[1024,128]{1,0:T(8,128)(2,1)S(1)} %get-tuple-element.47.g_s, ...), custom_call_target="tpu_custom_call" | custom-call | bytes 2097152 | tf_op jit(solution)/shard_map/near_s/pallas_call | solution.py:407
  25.6 1.9 %collective-permute-start.12 = (bf16[4,256,128]{2,1,0:T(8,128)(2,1)S(1)}, bf16[4,256,128]{2,1,0:T(8,128)(2,1)S(1)}, u32[]{:S(2)}, u32[]{:S(2)}) collective-permute-start(bf16[4,256,128]{2,1,0:T(8,128)(2,1)S(1)} %get-tuple-element.80), channel_id=1, source_target_pairs={{2,0},{3,1},{4,2},{5,3},{6,4},{7,5},{8,6},{9,7},{10,8},{11,9},{12,... | collective-permute-start | bytes 786440 | tf_op jit(solution)/shard_map/ppermute | solution.py:329
  27.5 0.0 collective-permute-done.6.back_ref
  27.5 1.9 %near_r.1 = (bf16[4,256,128]{2,1,0:T(8,128)(2,1)S(1)}, f32[2,512,128]{2,1,0:T(8,128)S(1)}, f32[2,512,128]{2,1,0:T(8,128)S(1)}) custom-call(bf16[4,256,128]{2,1,0:T(8,128)(2,1)S(1)} %collective-permute-done.8.kv, bf16[1024,128]{1,0:T(8,128)(2,1)S(1)} %get-tuple-element.46.q_s, bf16[1024,128]{1,0:T(8,128)(2,1)S(1)} %get-tuple-element.47.g_s, ...), custom_call_target="tpu_custom_call" | custom-call | bytes 2097152 | tf_op jit(solution)/shard_map/near_r/pallas_call | solution.py:410
  29.4 0.1 multiply_convert_fusion
  29.6 0.2 collective-permute-start.10
  29.8 0.1 partial.1.after.part_ref
  29.9 1.7 %collective-permute-done.10.got_ref = bf16[8,256,128]{2,1,0:T(8,128)(2,1)S(1)} collective-permute-done((bf16[8,256,128]{2,1,0:T(8,128)(2,1)S(1)}, bf16[8,256,128]{2,1,0:T(8,128)(2,1)S(1)}, u32[]{:S(2)}, u32[]{:S(2)}) %collective-permute-start.10) | collective-permute-done | bytes 524320 | tf_op jit(solution)/shard_map/ppermute | solution.py:329
  31.5 1.1 %final_q.1 = (bf16[256,8,128]{2,1,0:T(8,128)(2,1)}, f32[8,128]{1,0:T(8,128)S(1)}) custom-call(f32[2,512,128]{2,1,0:T(8,128)S(1)} %get-tuple-element.73.own_ref, bf16[8,256,128]{2,1,0:T(8,128)(2,1)S(1)} %collective-permute-done.10.got_ref, f32[4,256,128]{2,1,0:T(8,128)S(1)} %partial.1.after.part_ref), custom_call_target="tpu_custom_call" | custom-call | bytes 2097152 | tf_op jit(solution)/shard_map/final_q/pallas_call | solution.py:416
  32.7 9.1 %collective-permute-done.11.back_r = bf16[4,256,128]{2,1,0:T(8,128)(2,1)S(1)} collective-permute-done((bf16[4,256,128]{2,1,0:T(8,128)(2,1)S(1)}, bf16[4,256,128]{2,1,0:T(8,128)(2,1)S(1)}, u32[]{:S(2)}, u32[]{:S(2)}) %collective-permute-start.11) | collective-permute-done | bytes 262176 | tf_op jit(solution)/shard_map/ppermute | solution.py:329
  41.8 1.2 %final_kv.1 = (bf16[256,4,128]{2,1,0:T(4,128)(2,1)}, bf16[256,4,128]{2,1,0:T(4,128)(2,1)}) custom-call(f32[4,256,128]{2,1,0:T(8,128)S(1)} %partial.1.after.part_ref, bf16[8,256,128]{2,1,0:T(8,128)(2,1)S(1)} %collective-permute-done.10.got_ref, bf16[4,256,128]{2,1,0:T(8,128)(2,1)S(1)} %collective-permute-done.11.back_r, ...), custom_call_target="tpu_custom_call" | custom-call | bytes 2097152 | tf_op jit(solution)/shard_map/final_kv/pallas_call | solution.py:423
  (14 shorter events, 0.2 us)
Async XLA Ops:
  0.6 3.3 %copy-start = (f32[8,256]{1,0:T(8,128)S(1)}, f32[8,256]{1,0:T(8,128)}, u32[]{:S(2)}) copy-start(f32[8,256]{1,0:T(8,128)} %norm_ref.1) | copy-start | bytes 24580
  1.9 2.0 %collective-permute-start.1 = (bf16[4,256,128]{2,1,0:T(8,128)(2,1)S(1)}, bf16[4,256,128]{2,1,0:T(8,128)(2,1)S(1)}, u32[]{:S(2)}, u32[]{:S(2)}) collective-permute-start(bf16[4,256,128]{2,1,0:T(8,128)(2,1)S(1)} %get-tuple-element.45), channel_id=1, source_target_pairs={{0,1},{1,0},{2,3},{3,2},{4,5},{5,4},{6,7},{7,6},{8,9},{9,8},{10,11... | collective-permute-start | bytes 786440 | tf_op jit(solution)/shard_map/ppermute | solution.py:329
  2.7 10.8 %collective-permute-start = (bf16[4,256,128]{2,1,0:T(8,128)(2,1)S(1)}, bf16[4,256,128]{2,1,0:T(8,128)(2,1)S(1)}, u32[]{:S(2)}, u32[]{:S(2)}) collective-permute-start(bf16[4,256,128]{2,1,0:T(8,128)(2,1)S(1)} %get-tuple-element.44.kv_s), channel_id=1, source_target_pairs={{0,4},{1,5},{2,6},{3,7},{4,8},{5,9},{6,10},{7,11},{8,12},{9,13},{1... | collective-permute-start | bytes 786440 | tf_op jit(solution)/shard_map/ppermute | solution.py:329
  6.1 1.4 %collective-permute-start.3 = (bf16[512,128]{1,0:T(8,128)(2,1)S(1)}, bf16[512,128]{1,0:T(8,128)(2,1)S(1)}, u32[]{:S(2)}, u32[]{:S(2)}) collective-permute-start(bf16[512,128]{1,0:T(8,128)(2,1)S(1)} %get-tuple-element.50), channel_id=1, source_target_pairs={{0,1},{1,0},{2,3},{3,2},{4,5},{5,4},{6,7},{7,6},{8,9},{9,8},{10,11... | collective-permute-start | bytes 393224 | tf_op jit(solution)/shard_map/ppermute | solution.py:329
  6.5 3.2 %collective-permute-start.2 = (bf16[560,128]{1,0:T(8,128)(2,1)S(1)}, bf16[560,128]{1,0:T(8,128)(2,1)S(1)}, u32[]{:S(2)}, u32[]{:S(2)}) collective-permute-start(bf16[560,128]{1,0:T(8,128)(2,1)S(1)} %get-tuple-element.49), channel_id=1, source_target_pairs={{0,1},{1,0},{2,3},{3,2},{4,5},{5,4},{6,7},{7,6},{8,9},{9,8},{10,11... | collective-permute-start | bytes 430088 | tf_op jit(solution)/shard_map/ppermute | solution.py:329
  6.7 3.0 %collective-permute-start.4 = (bf16[512,128]{1,0:T(8,128)(2,1)S(1)}, bf16[512,128]{1,0:T(8,128)(2,1)S(1)}, u32[]{:S(2)}, u32[]{:S(2)}) collective-permute-start(bf16[512,128]{1,0:T(8,128)(2,1)S(1)} %get-tuple-element.51), channel_id=1, source_target_pairs={{0,1},{1,0},{2,3},{3,2},{4,5},{5,4},{6,7},{7,6},{8,9},{9,8},{10,11... | collective-permute-start | bytes 393224 | tf_op jit(solution)/shard_map/ppermute | solution.py:329
  7.1 2.7 %collective-permute-start.5 = (bf16[512,128]{1,0:T(8,128)(2,1)S(1)}, bf16[512,128]{1,0:T(8,128)(2,1)S(1)}, u32[]{:S(2)}, u32[]{:S(2)}) collective-permute-start(bf16[512,128]{1,0:T(8,128)(2,1)S(1)} %get-tuple-element.52), channel_id=1, source_target_pairs={{0,1},{1,0},{2,3},{3,2},{4,5},{5,4},{6,7},{7,6},{8,9},{9,8},{10,11... | collective-permute-start | bytes 393224 | tf_op jit(solution)/shard_map/ppermute | solution.py:329
  7.5 11.5 %collective-permute-start.7 = (bf16[4,256,128]{2,1,0:T(8,128)(2,1)S(1)}, bf16[4,256,128]{2,1,0:T(8,128)(2,1)S(1)}, u32[]{:S(2)}, u32[]{:S(2)}) collective-permute-start(bf16[4,256,128]{2,1,0:T(8,128)(2,1)S(1)} %collective-permute-done.1.after.kv_r), channel_id=1, source_target_pairs={{0,4},{1,5},{2,6},{3,7},{4,8},{5,9},{6,10},{7,11},{8,12},{9,13},{1... | collective-permute-start | bytes 786440 | tf_op jit(solution)/shard_map/ppermute | solution.py:329
  13.5 10.4 %collective-permute-start.9 = (bf16[4,256,128]{2,1,0:T(8,128)(2,1)S(1)}, bf16[4,256,128]{2,1,0:T(8,128)(2,1)S(1)}, u32[]{:S(2)}, u32[]{:S(2)}) collective-permute-start(bf16[4,256,128]{2,1,0:T(8,128)(2,1)S(1)} %broadcast_select_fusion.1), channel_id=1, source_target_pairs={{0,2},{1,3},{2,0},{3,1},{4,6},{5,7},{6,4},{7,5},{8,10},{9,11},{10,... | collective-permute-start | bytes 786440 | tf_op jit(solution)/shard_map/ppermute | solution.py:329
  14.0 13.5 %collective-permute-start.6 = (bf16[4,256,128]{2,1,0:T(8,128)(2,1)S(1)}, bf16[4,256,128]{2,1,0:T(8,128)(2,1)S(1)}, u32[]{:S(2)}, u32[]{:S(2)}) collective-permute-start(bf16[4,256,128]{2,1,0:T(8,128)(2,1)S(1)} %get-tuple-element.62), channel_id=1, source_target_pairs={{0,28},{1,29},{2,30},{3,31},{4,0},{5,1},{6,2},{7,3},{8,4},{9,5},{1... | collective-permute-start | bytes 786440 | tf_op jit(solution)/shard_map/ppermute | solution.py:329
  19.1 8.4 %collective-permute-start.8 = (bf16[4,256,128]{2,1,0:T(8,128)(2,1)S(1)}, bf16[4,256,128]{2,1,0:T(8,128)(2,1)S(1)}, u32[]{:S(2)}, u32[]{:S(2)}) collective-permute-start(bf16[4,256,128]{2,1,0:T(8,128)(2,1)S(1)} %broadcast_select_fusion), channel_id=1, source_target_pairs={{0,2},{1,3},{2,0},{3,1},{4,6},{5,7},{6,4},{7,5},{8,10},{9,11},{10,... | collective-permute-start | bytes 786440 | tf_op jit(solution)/shard_map/ppermute | solution.py:329
  19.7 22.1 %collective-permute-start.11 = (bf16[4,256,128]{2,1,0:T(8,128)(2,1)S(1)}, bf16[4,256,128]{2,1,0:T(8,128)(2,1)S(1)}, u32[]{:S(2)}, u32[]{:S(2)}) collective-permute-start(bf16[4,256,128]{2,1,0:T(8,128)(2,1)S(1)} %get-tuple-element.79), channel_id=1, source_target_pairs={{0,29},{1,28},{2,31},{3,30},{4,1},{5,0},{6,3},{7,2},{8,5},{9,4},{1... | collective-permute-start | bytes 786440 | tf_op jit(solution)/shard_map/ppermute | solution.py:329
  25.6 16.2 %collective-permute-start.12 = (bf16[4,256,128]{2,1,0:T(8,128)(2,1)S(1)}, bf16[4,256,128]{2,1,0:T(8,128)(2,1)S(1)}, u32[]{:S(2)}, u32[]{:S(2)}) collective-permute-start(bf16[4,256,128]{2,1,0:T(8,128)(2,1)S(1)} %get-tuple-element.80), channel_id=1, source_target_pairs={{2,0},{3,1},{4,2},{5,3},{6,4},{7,5},{8,6},{9,7},{10,8},{11,9},{12,... | collective-permute-start | bytes 786440 | tf_op jit(solution)/shard_map/ppermute | solution.py:329
  29.6 2.0 %collective-permute-start.10 = (bf16[8,256,128]{2,1,0:T(8,128)(2,1)S(1)}, bf16[8,256,128]{2,1,0:T(8,128)(2,1)S(1)}, u32[]{:S(2)}, u32[]{:S(2)}) collective-permute-start(bf16[8,256,128]{2,1,0:T(8,128)(2,1)S(1)} %pad_maximum_fusion), channel_id=1, source_target_pairs={{0,1},{1,0},{2,3},{3,2},{4,5},{5,4},{6,7},{7,6},{8,9},{9,8},{10,11... | collective-permute-start | bytes 1572872 | tf_op jit(solution)/shard_map/ppermute | solution.py:329
  29.8 12.0 %collective-permute-start.13 = (bf16[4,256,128]{2,1,0:T(8,128)(2,1)S(1)}, bf16[4,256,128]{2,1,0:T(8,128)(2,1)S(1)}, u32[]{:S(2)}, u32[]{:S(2)}) collective-permute-start(bf16[4,256,128]{2,1,0:T(8,128)(2,1)S(1)} %get-tuple-element.81), channel_id=1, source_target_pairs={{0,31},{1,30},{2,1},{3,0},{4,3},{5,2},{6,5},{7,4},{8,7},{9,6},{10,... | collective-permute-start | bytes 786440 | tf_op jit(solution)/shard_map/ppermute | solution.py:329
